TPU v7x, 128 devices: a whole 4x4x4 slice. The times are simulated.
128 devices in a mesh: pipe: 4 (over y), dp: 32 (over x, z, core).
Axes of the slice: x: 4, y: 4, z: 4, core: 2. Of those that a mesh axis runs over, the one named last changes fastest.
Arguments:
- acts: bfloat16 [4, 16384, 8192], P('pipe', 'dp'), may hold values from -6 to 6
- output_gradient: bfloat16 [4, 16384, 1024], P('pipe', 'dp'), may hold values from -6 to 6
- frozen_value_weight: bfloat16 [4, 8192, 1024], P('pipe'), may hold values from -0.1875 to 0.1875
- adapter_down_weight: bfloat16 [4, 128, 16, 8192], P('pipe', 'dp'), may hold values from -0.0625 to 0.0625
- adapter_up_weight: bfloat16 [4, 128, 16, 1024], P('pipe', 'dp'), may hold values from -0.1875 to 0.1875
- block_adapter_index: int32 [4, 128], P('pipe', 'dp'), may hold values from 0 to 63
- token_row_count: int32 [4, 128], P('pipe', 'dp'), may hold values from 32 to 128
- adapter_slot_table: int32 [64], replicated, may hold values from 0 to 63, as said below
Outputs:
- received: bfloat16 [4, 16384, 8192], P('pipe', 'dp')
- grad_a: bfloat16 [4, 64, 16, 8192], P('pipe', None, None, 'dp')
- grad_b: bfloat16 [4, 64, 16, 1024], P('pipe', None, None, 'dp')
Inputs may be any that keep to these rules, and one draw needn't show every extreme that they name: adapter_slot_table is a permutation of 0 to 63.
All inputs are finite; a program needn't handle non-finite values.
Results may differ from a plain program's by a relative error of at most 0.0057.
Values may be sent and summed in bfloat16 or wider, within the bound.
No kernel may reach another device: no remote copies, remote signals or barrier semaphores. Data moves between devices by JAX's collectives and lax.ppermute only.
A program may use at most 128 MiB of HBM per device.

v0:
```python
import jax
import jax.numpy as jnp
from jax import lax
from jax.sharding import PartitionSpec as P

BLOCK_ROWS = 128


adapter_scale = 2.0


def passed_along(block, axis, distance):
    devices = range(lax.axis_size(axis))
    route = [(i - distance, i) for i in devices if i - distance in devices]
    return lax.ppermute(block, axis, route)


def lookup_slots(adapter_ids, slot_map):
    match = adapter_ids[:, None] == jnp.arange(slot_map.shape[0], dtype=jnp.int32)[None, :]
    return jnp.sum(jnp.where(match, slot_map[None, :], 0), axis=1)


def body(
    acts,
    output_gradient,
    frozen_value_weight,
    adapter_down_weight,
    adapter_up_weight,
    block_adapter_index,
    token_row_count,
    adapter_slot_table,
):
    inputs = acts[0]
    upstream = output_gradient[0]
    weight = frozen_value_weight[0]
    down_matrix = adapter_down_weight[0]
    up_matrix = adapter_up_weight[0]
    live_count = token_row_count.shape[1]
    width = inputs.shape[1]
    out_width = upstream.shape[1]
    adapters = adapter_slot_table.shape[0]
    groups = lax.axis_size("dp")
    activation_rows = inputs.reshape(live_count, BLOCK_ROWS, width)
    grad_rows = upstream.reshape(live_count, BLOCK_ROWS, out_width)
    keep = jnp.arange(BLOCK_ROWS, dtype=jnp.int32)[None, :] < token_row_count[0][:, None]
    grad_rows = jnp.where(keep[:, :, None], grad_rows, jnp.zeros_like(grad_rows))
    rank_activation = jnp.einsum(
        "jug,jpg->jup", activation_rows, down_matrix, preferred_element_type=jnp.float32
    ).astype(jnp.bfloat16)
    rank_gradient = (
        adapter_scale
        * jnp.einsum("mig,mjg->mij", grad_rows, up_matrix, preferred_element_type=jnp.float32)
    ).astype(jnp.bfloat16)
    down_gradient_part = jnp.einsum(
        "sze,szv->sev", rank_gradient, activation_rows, preferred_element_type=jnp.float32
    ).astype(jnp.bfloat16)
    up_gradient_part = (
        adapter_scale
        * jnp.einsum("upg,upf->ugf", rank_activation, grad_rows, preferred_element_type=jnp.float32)
    ).astype(jnp.bfloat16)
    base_term = lax.dot_general(
        grad_rows.reshape(live_count * BLOCK_ROWS, out_width),
        weight,
        (((1,), (1,)), ((), ())),
        preferred_element_type=jnp.float32,
    )
    adapter_term = jnp.einsum(
        "cyl,clp->cyp", rank_gradient, down_matrix, preferred_element_type=jnp.float32
    ).reshape(live_count * BLOCK_ROWS, width)
    passed = (base_term + adapter_term).astype(jnp.bfloat16)
    received = passed_along(passed[None], "pipe", -1)
    every_ids = lax.all_gather(block_adapter_index, "dp", axis=1, tiled=True)[0]
    every_slot = lookup_slots(every_ids, adapter_slot_table)
    pick = (every_slot[None, :] == jnp.arange(adapters, dtype=jnp.int32)[:, None]).astype(
        jnp.bfloat16
    )
    rank = down_gradient_part.shape[1]
    send_a = down_gradient_part.reshape(live_count, rank, groups, width // groups)
    send_b = up_gradient_part.reshape(live_count, rank, groups, out_width // groups)
    recv_a, recv_b = (
        lax.all_to_all(send_a, "dp", split_axis=2, concat_axis=0, tiled=True),
        lax.all_to_all(send_b, "dp", split_axis=2, concat_axis=0, tiled=True),
    )
    total_a = jnp.einsum("js,srxd->jrd", pick, recv_a, preferred_element_type=jnp.float32)
    total_b = jnp.einsum("js,srxd->jrd", pick, recv_b, preferred_element_type=jnp.float32)
    return (received, total_a.astype(jnp.bfloat16)[None], total_b.astype(jnp.bfloat16)[None])


def solution(mesh):
    in_specs = (
        P("pipe", "dp", None),
        P("pipe", "dp", None),
        P("pipe", None, None),
        P("pipe", "dp", None, None),
        P("pipe", "dp", None, None),
        P("pipe", "dp"),
        P("pipe", "dp"),
        P(),
    )
    out_specs = (P("pipe", "dp", None), P("pipe", None, None, "dp"), P("pipe", None, None, "dp"))
    return jax.shard_map(body, mesh=mesh, in_specs=in_specs, out_specs=out_specs, check_vma=False)
```

profile of v0, /device:TPU:1, one launch (start us, length us, event | category | flops | bytes accessed | tf_op | source)
XLA Modules:
  0.0 222.5 jit_solution(13455108209149115371)
XLA Ops:
  0.6 0.8 fusion.31
  1.5 1.7 fusion.10
  3.2 8.1 %fusion.14 = f32[4,128,8192]{2,1,0:T(8,128)} fusion(bf16[4,128,16]{1,2,0:T(8,128)(2,1)S(1)} %fusion.10, bf16[1,4,16,8192]{3,2,1,0:T(8,128)(2,1)S(1)} %copy-done), kind=kOutput, calls=%fused_computation.16 | convolution fusion | flops 134217728 | bytes 17842176 | tf_op jit(solution)/shard_map/cyl,clp->cyp/dot_general | solution.py:67
  11.2 19.4 %fusion.5 = bf16[1,512,8192]{2,1,0:T(8,128)(2,1)} fusion(f32[4,128,8192]{2,1,0:T(8,128)} %fusion.14, bf16[1,8192,1024]{2,1,0:T(8,128)(2,1)} %param.10, bf16[1,512,1024]{2,1,0:T(8,128)(2,1)S(1)} %copy-done.1, pred[512]{0:T(512)(128)(4,1)S(1)} %get-tuple-element.15), kind=kOutput, calls=%fused_computation.4 | convolution fusion | flops 8598847488 | bytes 42992128 | tf_op jit(solution)/shard_map/dot_general | solution.py:61
  30.6 1.3 collective-permute-start
  31.9 5.8 %fusion.9 = bf16[4,16,1024]{2,1,0:T(8,128)(2,1)S(1)} fusion(bf16[4,128,8192]{2,1,0:T(8,128)(2,1)} %bitcast.67, bf16[1,4,16,8192]{3,2,1,0:T(8,128)(2,1)S(1)} %copy-done, bf16[4,128,1024]{2,1,0:T(8,128)(2,1)S(1)} %bitcast.75, pred[4,128]{1,0:T(4,128)(4,1)S(1)} %get-tuple-element.16), kind=kOutput, calls=%fused_computation.9 | convolution fusion | flops 151658496 | bytes 10617344 | tf_op jit(solution)/shard_map/upg,upf->ugf/dot_general | solution.py:59
  37.7 0.4 reshape.63
  38.1 0.2 copy.35
  38.3 1.2 reshape.73
  39.5 9.4 %all-to-all-start.1 = ((bf16[32,2,1024]{2,1,0:T(2,128)(2,1)}), bf16[32,2,1024]{2,1,0:T(2,128)(2,1)S(1)}, u32[]{:S(2)}, u32[]{:S(2)}) async-start(bf16[32,2,1024]{2,1,0:T(2,128)(2,1)} %reshape.73), calls=%async_computation.1 | async-start | bytes 262144 | tf_op jit(solution)/shard_map/all_to_all | solution.py:82
  48.9 4.6 %convolution_convert_fusion = bf16[4,16,8192]{2,1,0:T(8,128)(2,1)S(1)} fusion(bf16[4,128,16]{1,2,0:T(8,128)(2,1)S(1)} %fusion.10, bf16[4,128,8192]{2,1,0:T(8,128)(2,1)} %bitcast.68), kind=kOutput, calls=%fused_computation.5 | convolution fusion | flops 134742016 | bytes 9453568 | tf_op jit(solution)/shard_map/sze,szv->sev/dot_general | solution.py:54
  53.5 1.2 copy.34
  54.7 1.9 all-to-all-done.1
  56.6 5.4 %all-to-all-start = ((bf16[4,16,32,256]{3,1,0,2:T(8,128)(2,1)}), bf16[4,16,32,256]{3,1,0,2:T(8,128)(2,1)S(1)}, u32[]{:S(2)}, u32[]{:S(2)}) async-start(bf16[4,16,32,256]{3,1,0,2:T(8,128)(2,1)} %bitcast.65), calls=%async_computation | async-start | bytes 2097152 | tf_op jit(solution)/shard_map/all_to_all | solution.py:81
  62.1 0.6 dynamic-slice
  63.5 21.8 %all-reduce = s32[128]{0:T(128)S(1)} all-reduce(s32[128]{0:T(128)S(1)} %bitcast_dynamic-update-slice_fusion), channel_id=1, replica_groups=mesh['pipe'=4,'dp'=32] {'dp'}, use_global_device_ids=true, to_apply=%add | all-reduce | flops 128 | bytes 1024
  85.4 0.3 reshape.74
  85.7 0.4 copy.26
  86.1 0.2 fusion.23
  86.3 0.7 convert_bitcast_fusion
  87.0 0.5 fusion.8
  87.5 1.1 copy.27
  88.5 126.2 %collective-permute-done = bf16[1,512,8192]{2,1,0:T(8,128)(2,1)} collective-permute-done((bf16[1,512,8192]{2,1,0:T(8,128)(2,1)}, bf16[1,512,8192]{2,1,0:T(8,128)(2,1)}, u32[]{:S(2)}, u32[]{:S(2)}) %collective-permute-start) | collective-permute-done | bytes 8388640 | tf_op jit(solution)/shard_map/ppermute | solution.py:15
  214.7 7.8 %copy.38 = bf16[1,512,8192]{2,1,0:T(8,128)(2,1)} copy(bf16[1,512,8192]{2,1,0:T(8,128)(2,1)} %collective-permute-done) | data formatting | bytes 16777216
  (14 shorter events, 0.2 us)
Async XLA Ops:
  0.6 2.5 %copy-start = (bf16[1,4,16,8192]{3,2,1,0:T(8,128)(2,1)S(1)}, bf16[1,4,16,8192]{3,2,1,0:T(8,128)(2,1)}, u32[]{:S(2)}) copy-start(bf16[1,4,16,8192]{3,2,1,0:T(8,128)(2,1)} %param.11) | copy-start | bytes 3145732
  3.1 8.1 %copy-start.1 = (bf16[1,512,1024]{2,1,0:T(8,128)(2,1)S(1)}, bf16[1,512,1024]{2,1,0:T(8,128)(2,1)}, u32[]{:S(2)}) copy-start(bf16[1,512,1024]{2,1,0:T(8,128)(2,1)} %param.9) | copy-start | bytes 3145732
  30.6 184.1 %collective-permute-start = (bf16[1,512,8192]{2,1,0:T(8,128)(2,1)}, bf16[1,512,8192]{2,1,0:T(8,128)(2,1)}, u32[]{:S(2)}, u32[]{:S(2)}) collective-permute-start(bf16[1,512,8192]{2,1,0:T(8,128)(2,1)} %fusion.5), channel_id=1, source_target_pairs={{32,0},{64,32},{96,64},{33,1},{65,33},{97,65},{34,2},{66,34},{98,6... | collective-permute-start | bytes 25165832 | tf_op jit(solution)/shard_map/ppermute | solution.py:15
  37.7 24.4 %copy-start.4 = (u32[128]{0:T(128)S(1)}, u32[128]{0:T(128)}, u32[]{:S(2)}) copy-start(u32[128]{0:T(128)} %constant.17) | copy-start | bytes 1540
  37.7 25.6 %copy-start.2 = (s32[1,4]{1,0:T(1,128)S(1)}, s32[1,4]{1,0:T(1,128)}, u32[]{:S(2)}) copy-start(s32[1,4]{1,0:T(1,128)} %param.13) | copy-start | bytes 52
  37.7 47.6 %copy-start.3 = (s32[64]{0:T(128)S(1)}, s32[64]{0:T(128)}, u32[]{:S(2)}) copy-start(s32[64]{0:T(128)} %param.15) | copy-start | bytes 772
  39.5 17.1 %all-to-all-start.1 = ((bf16[32,2,1024]{2,1,0:T(2,128)(2,1)}), bf16[32,2,1024]{2,1,0:T(2,128)(2,1)S(1)}, u32[]{:S(2)}, u32[]{:S(2)}) async-start(bf16[32,2,1024]{2,1,0:T(2,128)(2,1)} %reshape.73), calls=%async_computation.1 | async-start | bytes 262144 | tf_op jit(solution)/shard_map/all_to_all | solution.py:82
  56.6 30.3 %all-to-all-start = ((bf16[4,16,32,256]{3,1,0,2:T(8,128)(2,1)}), bf16[4,16,32,256]{3,1,0,2:T(8,128)(2,1)S(1)}, u32[]{:S(2)}, u32[]{:S(2)}) async-start(bf16[4,16,32,256]{3,1,0,2:T(8,128)(2,1)} %bitcast.65), calls=%async_computation | async-start | bytes 2097152 | tf_op jit(solution)/shard_map/all_to_all | solution.py:81
where the time goes:
time: 223 us; the launch traced here: 222 us
  waiting for transfers between devices  128 us (57%)
  matrix products  40.2 us (18%)
  blocking collectives  21.8 us (10%)
  starting transfers between devices  16.2 us (7%)
  local copies, waits for them, and re-layouts  13.2 us (6%)
    ppermute x1, waiting for transfers between devices, passed_along(): return lax.ppermute(block, axis, route)  126 us
    unnamed x1, blocking collectives  21.8 us
    dot_general x1, matrix products, body(): lax.dot_general(grad_rows.reshape(live_count * BLOCK_ROWS, out_width), we...  19.4 us
    unnamed x17, local copies, waits for them, and re-layouts  11 us
    all_to_all x1, starting transfers between devices, body(): lax.all_to_all(send_b, 'dp', split_axis=2, concat_axis=0, tiled=True)  9.44 us
    dot_general x1, matrix products, body(): jnp.einsum('cyl,clp->cyp', rank_gradient, down_matrix, preferred_element_...  8.08 us
    dot_general x1, matrix products, body(): jnp.einsum('upg,upf->ugf', rank_activation, grad_rows, preferred_element_...  5.82 us
    all_to_all x1, starting transfers between devices, body(): lax.all_to_all(send_a, 'dp', split_axis=2, concat_axis=0, tiled=True)  5.44 us
  transfers between devices with their start and end apart: 3, of which 2 were waited for; matrix products, arithmetic and copies ran while one was open for 8% of the time, Pallas kernels for 0%

commit v1 on v0

v1 whole, which is shorter than its diff:
```python
import functools

import jax
import jax.numpy as jnp
from jax import lax
from jax.experimental import pallas as pl
from jax.experimental.pallas import tpu as pltpu
from jax.sharding import PartitionSpec as P

BLOCK_ROWS = 128
RANK = 16
BF16 = jnp.bfloat16
F32 = jnp.float32

adapter_scale = 2.0

LAST = (((1,), (1,)), ((), ()))
FIRST = (((0,), (0,)), ((), ()))


def dot(a, b, dims=(((1,), (0,)), ((), ()))):
    return lax.dot_general(a, b, dims, preferred_element_type=F32)


def vmem(mib):
    return pltpu.CompilerParams(vmem_limit_bytes=mib << 20)


def prepare_kernel(count_ref, grad_ref, up_ref, message_ref):
    blocks = count_ref.shape[0]
    rows, width = grad_ref.shape
    message_ref[rows:, :] = jnp.zeros((RANK, width), BF16)
    for b in range(blocks):
        span = slice(b * BLOCK_ROWS, (b + 1) * BLOCK_ROWS)
        at = lax.broadcasted_iota(jnp.int32, (BLOCK_ROWS, width), 0)
        masked = jnp.where(at < count_ref[b], grad_ref[span, :].astype(F32), 0.0).astype(BF16)
        message_ref[span, :] = masked
        low = dot(up_ref[b * RANK : (b + 1) * RANK, :], masked, LAST)
        message_ref[rows:, span] = (adapter_scale * low).astype(BF16)


def prepare(count, grad, up):
    rows, width = grad.shape
    return pl.pallas_call(
        prepare_kernel,
        out_shape=jax.ShapeDtypeStruct((rows + RANK, width), BF16),
        in_specs=[
            pl.BlockSpec(memory_space=pltpu.SMEM),
            pl.BlockSpec(memory_space=pltpu.VMEM),
            pl.BlockSpec(memory_space=pltpu.VMEM),
        ],
        out_specs=pl.BlockSpec(memory_space=pltpu.VMEM),
        compiler_params=vmem(24),
        name="prepare",
    )(count, grad, up)


def grads_kernel(groups, ids_ref, table_ref, message_ref, acts_ref, down_ref, out_ref, low_ref):
    step = pl.program_id(0)
    blocks = ids_ref.shape[0]
    rows, chunk = acts_ref.shape
    take = out_ref.shape[2]

    @pl.when(step == 0)
    def _():
        low_ref[...] = jnp.zeros_like(low_ref)

    for b in range(blocks):
        span = slice(b * BLOCK_ROWS, (b + 1) * BLOCK_ROWS)
        ranks = slice(b * RANK, (b + 1) * RANK)
        acts = acts_ref[span, :]
        low_ref[ranks, :] += dot(down_ref[ranks, :], acts, LAST)
        part = dot(message_ref[rows:, span], acts).astype(BF16)
        for k in range(chunk // take):
            out_ref[step * (chunk // take) + k, ranks, :] = part[:, k * take : (k + 1) * take]

    @pl.when(step == pl.num_programs(0) - 1)
    def _():
        parts = []
        for b in range(blocks):
            span = slice(b * BLOCK_ROWS, (b + 1) * BLOCK_ROWS)
            low = low_ref[b * RANK : (b + 1) * RANK, :].astype(BF16)
            parts.append(adapter_scale * dot(low, message_ref[span, :]))
        part = jnp.concatenate(parts, axis=0)
        width = part.shape[1] // groups
        lane = lax.broadcasted_iota(jnp.int32, (8, 128), 1) // width
        row = lax.broadcasted_iota(jnp.int32, (8, take), 0)
        slots = jnp.zeros((8, take), F32)
        for b in range(blocks):
            slots = jnp.where(row == b, table_ref[ids_ref[b]].astype(F32), slots)
        fit = 128 // width
        for d in range(groups):
            column, mine = d // fit, d % fit
            halves = []
            for h in range(take // 128):
                total = jnp.zeros((8, 128), F32)
                for g in range(fit):
                    k = h * fit + g
                    tile = part[8 * k : 8 * k + 8, 128 * column : 128 * column + 128]
                    tile = pltpu.roll(tile, ((g - mine) * width) % 128, 1)
                    total = jnp.where(lane == g, tile, total)
                halves.append(total)
            packed = jnp.concatenate([jnp.concatenate(halves, axis=1), slots], axis=0)
            out_ref[d, blocks * RANK :, :] = packed.astype(BF16)


def grads(ids, table, message, acts, down, groups):
    blocks = ids.shape[0]
    rows, width = acts.shape
    chunk = 1024
    shape = (groups, blocks * RANK + 16, width // groups)
    return pl.pallas_call(
        functools.partial(grads_kernel, groups),
        out_shape=jax.ShapeDtypeStruct(shape, BF16),
        grid=(width // chunk,),
        in_specs=[
            pl.BlockSpec(memory_space=pltpu.SMEM),
            pl.BlockSpec(memory_space=pltpu.SMEM),
            pl.BlockSpec(message.shape, lambda i: (0, 0)),
            pl.BlockSpec((rows, chunk), lambda i: (0, i)),
            pl.BlockSpec((blocks * RANK, chunk), lambda i: (0, i)),
        ],
        out_specs=pl.BlockSpec(shape, lambda i: (0, 0, 0)),
        scratch_shapes=[pltpu.VMEM((blocks * RANK, BLOCK_ROWS), F32)],
        compiler_params=vmem(32),
        name="grads",
    )(ids, table, message, acts, down)


def product_kernel(message_ref, weight_ref, down_ref, out_ref):
    rows = out_ref.shape[0]
    ranks = down_ref.shape[0]
    low = jnp.concatenate([message_ref[rows:, :rows].astype(F32)] * (ranks // RANK), axis=0)
    own = lax.broadcasted_iota(jnp.int32, low.shape, 0) // RANK
    of = lax.broadcasted_iota(jnp.int32, low.shape, 1) // BLOCK_ROWS
    low = jnp.where(own == of, low, 0.0).astype(BF16)
    total = dot(message_ref[:rows, :], weight_ref[...], LAST) + dot(low, down_ref[...], FIRST)
    out_ref[...] = total.astype(BF16)


def product(message, weight, down):
    width, depth = weight.shape
    rows = message.shape[0] - RANK
    chunk = 1024
    return pl.pallas_call(
        product_kernel,
        out_shape=jax.ShapeDtypeStruct((rows, width), BF16),
        grid=(width // chunk,),
        in_specs=[
            pl.BlockSpec(message.shape, lambda i: (0, 0)),
            pl.BlockSpec((chunk, depth), lambda i: (i, 0)),
            pl.BlockSpec((down.shape[0], chunk), lambda i: (0, i)),
        ],
        out_specs=pl.BlockSpec((rows, chunk), lambda i: (0, i)),
        compiler_params=vmem(40),
        name="product",
    )(message, weight, down)


def body(
    acts,
    output_gradient,
    frozen_value_weight,
    adapter_down_weight,
    adapter_up_weight,
    block_adapter_index,
    token_row_count,
    adapter_slot_table,
):
    blocks = token_row_count.shape[1]
    rows, width = acts.shape[1:]
    depth = output_gradient.shape[2]
    adapters = adapter_slot_table.shape[0]
    groups = lax.axis_size("dp")
    down = adapter_down_weight.reshape(blocks * RANK, width)
    up = adapter_up_weight.reshape(blocks * RANK, depth)

    def back(x):
        n = lax.axis_size("pipe")
        return lax.ppermute(x, "pipe", [(i + 1, i) for i in range(n - 1)])

    share = lax.dynamic_slice_in_dim(
        frozen_value_weight[0], lax.axis_index("dp") * (width // groups), width // groups, 0
    )
    share = back(share)
    message = prepare(token_row_count[0], output_gradient[0], up)
    send = grads(block_adapter_index[0], adapter_slot_table, message, acts[0], down, groups)
    weight = lax.all_gather(share, "dp", axis=0, tiled=True)
    got = lax.all_to_all(send, "dp", split_axis=0, concat_axis=0, tiled=True)
    message, down, share = lax.optimization_barrier((message, down, share))
    message, down = back(message), back(down)
    received = product(message, weight, down)

    ranks = blocks * RANK
    slot = got[:, ranks + 8 : ranks + 8 + blocks, 0].reshape(-1)
    pick = (jnp.arange(adapters, dtype=BF16)[:, None] == slot[None, :]).astype(BF16)
    terms = got[:, :ranks, :].reshape(groups * blocks, RANK, width // groups)
    total_a = jnp.einsum("js,srd->jrd", pick, terms, preferred_element_type=F32)
    terms = got[:, ranks : ranks + 8, :].reshape(groups, 8, ranks // 8, depth // groups)
    terms = jnp.swapaxes(terms, 1, 2).reshape(groups * blocks, RANK, depth // groups)
    total_b = jnp.einsum("js,srd->jrd", pick, terms, preferred_element_type=F32)
    return received[None], total_a.astype(BF16)[None], total_b.astype(BF16)[None]


def solution(mesh):
    in_specs = (
        P("pipe", "dp", None),
        P("pipe", "dp", None),
        P("pipe", None, None),
        P("pipe", "dp", None, None),
        P("pipe", "dp", None, None),
        P("pipe", "dp"),
        P("pipe", "dp"),
        P(),
    )
    out_specs = (P("pipe", "dp", None), P("pipe", None, None, "dp"), P("pipe", None, None, "dp"))
    return jax.shard_map(body, mesh=mesh, in_specs=in_specs, out_specs=out_specs, check_vma=False)
```

time: 223 us -> 136 us (0.61)
  waiting for transfers between devices: 128 us -> 61.8 us
  matrix products: 40.2 us -> 0.65 us
  Pallas kernels: 0 us -> 24.4 us
  blocking collectives: 21.8 us -> 0 us
  between operations: 1.41 us -> 14.1 us
  local copies, waits for them, and re-layouts: 13.2 us -> 19.8 us
  starting transfers between devices: 16.2 us -> 13.7 us
    ppermute x1 -> x3, waiting for transfers between devices: 126 us -> 33.3 us  [back(): return lax.ppermute(x, 'pipe', [(i + 1, i) for i in range(n - 1)])]
    dot_general x6 -> x1, matrix products: 40 us -> 0.47 us  [body(): total_a = jnp.einsum('js,srd->jrd', pick, terms, preferred_element_type=F32)]
    pallas_call x0 -> x3, Pallas kernels: none -> 24.4 us  [the longest x1 16.5 us: product(): pl.pallas_call(product_kernel, out_shape=jax.ShapeDtypeStruct((rows, widt...]
    unnamed x1 -> x0, blocking collectives: 21.8 us -> none
    all_to_all x2 -> x1, waiting for transfers between devices: 1.94 us -> 17.2 us  [body(): got = lax.all_to_all(send, 'dp', split_axis=0, concat_axis=0, tiled=True)]
    all_gather x0 -> x1, waiting for transfers between devices: none -> 11.3 us  [body(): weight = lax.all_gather(share, 'dp', axis=0, tiled=True)]
    all_to_all x2 -> x1, starting transfers between devices: 14.9 us -> 9.77 us  [body(): got = lax.all_to_all(send, 'dp', split_axis=0, concat_axis=0, tiled=True)]
    slice x0 -> x3, local copies, waits for them, and re-layouts: none -> 3.48 us  [the longest x1 1.62 us: body(): terms = got[:, :ranks, :].reshape(groups * blocks, RANK, width // groups)]
  transfers between devices with their start and end apart: 3 -> 5, of which waited for: 2 -> 4; matrix products, arithmetic and copies ran while one was open for 8% -> 8% of each run, Pallas kernels for 0% -> 6%
where the time goes in v1:
time: 136 us; the launch traced here: 135 us
  waiting for transfers between devices  61.8 us (45%)
  Pallas kernels  24.4 us (18%)
  local copies, waits for them, and re-layouts  19.8 us (15%)
  between operations  14.1 us (10%)
  starting transfers between devices  13.7 us (10%)
    ppermute x3, waiting for transfers between devices, back(): return lax.ppermute(x, 'pipe', [(i + 1, i) for i in range(n - 1)])  33.3 us
    all_to_all x1, waiting for transfers between devices, body(): got = lax.all_to_all(send, 'dp', split_axis=0, concat_axis=0, tiled=True)  17.2 us
    pallas_call x1, Pallas kernels, product(): pl.pallas_call(product_kernel, out_shape=jax.ShapeDtypeStruct((rows, widt...  16.5 us
    all_gather x1, waiting for transfers between devices, body(): weight = lax.all_gather(share, 'dp', axis=0, tiled=True)  11.3 us
    unnamed x19, local copies, waits for them, and re-layouts  10.7 us
    all_to_all x1, starting transfers between devices, body(): got = lax.all_to_all(send, 'dp', split_axis=0, concat_axis=0, tiled=True)  9.77 us
    pallas_call x1, Pallas kernels, grads(): pl.pallas_call(functools.partial(grads_kernel, groups), out_shape=jax.Sha...  6.89 us
    ppermute x3, starting transfers between devices, back(): return lax.ppermute(x, 'pipe', [(i + 1, i) for i in range(n - 1)])  3.88 us
  transfers between devices with their start and end apart: 5, of which 4 were waited for; matrix products, arithmetic and copies ran while one was open for 8% of the time, Pallas kernels for 6%

profile of v1, /device:TPU:1, one launch (start us, length us, event | category | flops | bytes accessed | tf_op | source)
XLA Modules:
  0.0 135.2 jit_solution(8305869729058393199)
XLA Ops:
  7.2 1.1 dynamic-slice_bitcast_fusion
  8.3 1.3 collective-permute-start
  9.6 14.0 %collective-permute-done = bf16[256,1024]{1,0:T(8,128)(2,1)S(1)} collective-permute-done((bf16[256,1024]{1,0:T(8,128)(2,1)S(1)}, bf16[256,1024]{1,0:T(8,128)(2,1)S(1)}, u32[]{:S(2)}, u32[]{:S(2)}) %collective-permute-start) | collective-permute-done | bytes 524320 | tf_op jit(solution)/shard_map/ppermute | solution.py:180
  23.6 0.8 copy-done.8
  24.4 1.3 copy-done.3
  25.7 0.9 copy-done.4
  27.3 1.0 prepare.1.message_ref
  28.3 3.4 %copy-done = bf16[1,512,8192]{2,1,0:T(8,128)(2,1)S(1)} copy-done((bf16[1,512,8192]{2,1,0:T(8,128)(2,1)S(1)}, bf16[1,512,8192]{2,1,0:T(8,128)(2,1)}, u32[]{:S(2)}) %copy-start) | copy-done | bytes 8388632
  31.7 1.2 copy-done.1
  34.2 6.9 %grads.1 = bf16[32,80,256]{2,1,0:T(8,128)(2,1)} custom-call(s32[4]{0:T(128)S(1)} %bitcast.29, s32[64]{0:T(128)S(1)} %copy-done.7, bf16[528,1024]{1,0:T(8,128)(2,1)S(1)} %prepare.1.message_ref, bf16[512,8192]{1,0:T(8,128)(2,1)S(1)} %bitcast.23, bf16[64,8192]{1,0:T(8,128)(2,1)S(1)} %bitcast.24), custom_call_target="tpu_custom_call" | custom-call | tf_op jit(solution)/shard_map/grads/pallas_call | solution.py:112
  41.1 9.8 %all-to-all-start = ((bf16[32,80,256]{2,1,0:T(8,128)(2,1)}), bf16[32,80,256]{2,1,0:T(8,128)(2,1)}, u32[]{:S(2)}, u32[]{:S(2)}) async-start(bf16[32,80,256]{2,1,0:T(8,128)(2,1)} %grads.1), calls=%async_computation | async-start | bytes 2621440 | tf_op jit(solution)/shard_map/all_to_all | solution.py:189
  50.9 1.3 collective-permute-start.1
  52.2 1.3 collective-permute-start.2
  53.5 17.2 %all-to-all-done = bf16[32,80,256]{2,1,0:T(8,128)(2,1)} async-done(((bf16[32,80,256]{2,1,0:T(8,128)(2,1)}), bf16[32,80,256]{2,1,0:T(8,128)(2,1)}, u32[]{:S(2)}, u32[]{:S(2)}) %all-to-all-start) | async-done | bytes 1310752 | tf_op jit(solution)/shard_map/all_to_all | solution.py:189
  70.7 1.0 slice_reduce_fusion
  71.8 1.6 %slice.13 = bf16[32,64,256]{2,1,0:T(8,128)(2,1)S(1)} slice(bf16[32,80,256]{2,1,0:T(8,128)(2,1)} %all-to-all-done), slice={[0:32], [0:64], [0:256]} | slice | bytes 2097152 | tf_op jit(solution)/shard_map/slice | solution.py:197
  73.9 1.1 copy.16
  75.0 0.9 slice.14
  75.9 1.0 reshape.26
  76.9 1.9 %copy.14 = bf16[32,8,8,32]{3,1,2,0:T(8,128)(2,1)} copy(bf16[32,8,8,32]{3,2,1,0:T(8,128)(2,1)} %reshape.26) | data formatting | bytes 262144 | tf_op jit(solution)/shard_map/reshape | solution.py:199
  78.9 1.5 %copy.15 = bf16[128,16,32]{0,2,1:T(8,128)(2,1)S(1)} copy(bf16[128,16,32]{2,1,0:T(8,128)(2,1)} %bitcast.32) | data formatting | bytes 262144 | tf_op jit(solution)/shard_map/reshape | solution.py:200
  81.2 19.3 %collective-permute-done.2.down_ref = bf16[64,8192]{1,0:T(8,128)(2,1)} collective-permute-done((bf16[64,8192]{1,0:T(8,128)(2,1)S(1)}, bf16[64,8192]{1,0:T(8,128)(2,1)}, u32[]{:S(2)}, u32[]{:S(2)}) %collective-permute-start.2) | collective-permute-done | bytes 1048608 | tf_op jit(solution)/shard_map/ppermute | solution.py:180
  100.5 11.3 %all-gather.2.cloned.1.call-done.weight_ref = bf16[8192,1024]{1,0:T(8,128)(2,1)} async-done(((bf16[256,1024]{1,0:T(8,128)(2,1)}), bf16[8192,1024]{1,0:T(8,128)(2,1)}) %all-gather.2.cloned.1.call-update) | async-done | bytes 16777232 | tf_op jit(solution)/shard_map/all_gather | solution.py:188
  111.8 16.5 %product.1 = bf16[512,8192]{1,0:T(8,128)(2,1)} custom-call(bf16[528,1024]{1,0:T(8,128)(2,1)S(1)} %collective-permute-done.1.message_ref, bf16[8192,1024]{1,0:T(8,128)(2,1)} %all-gather.2.cloned.1.call-done.weight_ref, bf16[64,8192]{1,0:T(8,128)(2,1)} %collective-permute-done.2.down_ref), custom_call_target="tpu_custom_call" | custom-call | tf_op jit(solution)/shard_map/product/pallas_call | solution.py:145
  (20 shorter events, 3.5 us)
Async XLA Ops:
  7.2 104.7 %all-gather.2.cloned.1.call-start = ((), (), s32[]{:S(2)}) async-start(), calls=%async_computation.1 | async-start | bytes 17301504 | tf_op jit(solution)/shard_map/all_gather | solution.py:188
  8.3 15.3 %collective-permute-start = (bf16[256,1024]{1,0:T(8,128)(2,1)S(1)}, bf16[256,1024]{1,0:T(8,128)(2,1)S(1)}, u32[]{:S(2)}, u32[]{:S(2)}) collective-permute-start(bf16[256,1024]{1,0:T(8,128)(2,1)S(1)} %dynamic-slice_bitcast_fusion), channel_id=1, source_target_pairs={{32,0},{64,32},{96,64},{33,1},{65,33},{97,65},{34,2},{66,34},{98,6... | collective-permute-start | bytes 1572872 | tf_op jit(solution)/shard_map/ppermute | solution.py:180
  23.6 0.8 copy-start.8
  24.4 27.8 %copy-start.2 = (bf16[1,4,16,8192]{3,2,1,0:T(8,128)(2,1)S(1)}, bf16[1,4,16,8192]{3,2,1,0:T(8,128)(2,1)}, u32[]{:S(2)}) copy-start(bf16[1,4,16,8192]{3,2,1,0:T(8,128)(2,1)} %param.11) | copy-start | bytes 3145732
  24.4 1.3 copy-start.3
  25.7 0.9 copy-start.4
  26.6 0.7 copy-start.5
  28.3 3.4 %copy-start = (bf16[1,512,8192]{2,1,0:T(8,128)(2,1)S(1)}, bf16[1,512,8192]{2,1,0:T(8,128)(2,1)}, u32[]{:S(2)}) copy-start(bf16[1,512,8192]{2,1,0:T(8,128)(2,1)} %param.8) | copy-start | bytes 25165828
  31.7 1.2 copy-start.1
  32.9 0.7 copy-start.6
  33.5 0.7 copy-start.7
  41.1 29.6 %all-to-all-start = ((bf16[32,80,256]{2,1,0:T(8,128)(2,1)}), bf16[32,80,256]{2,1,0:T(8,128)(2,1)}, u32[]{:S(2)}, u32[]{:S(2)}) async-start(bf16[32,80,256]{2,1,0:T(8,128)(2,1)} %grads.1), calls=%async_computation | async-start | bytes 2621440 | tf_op jit(solution)/shard_map/all_to_all | solution.py:189
  50.9 49.6 %collective-permute-start.1 = (bf16[528,1024]{1,0:T(8,128)(2,1)S(1)}, bf16[528,1024]{1,0:T(8,128)(2,1)S(1)}, u32[]{:S(2)}, u32[]{:S(2)}) collective-permute-start(bf16[528,1024]{1,0:T(8,128)(2,1)S(1)} %prepare.1.message_ref), channel_id=1, source_target_pairs={{32,0},{64,32},{96,64},{33,1},{65,33},{97,65},{34,2},{66,34},{98,6... | collective-permute-start | bytes 3244040 | tf_op jit(solution)/shard_map/ppermute | solution.py:180
  52.2 48.3 %collective-permute-start.2 = (bf16[64,8192]{1,0:T(8,128)(2,1)S(1)}, bf16[64,8192]{1,0:T(8,128)(2,1)}, u32[]{:S(2)}, u32[]{:S(2)}) collective-permute-start(bf16[64,8192]{1,0:T(8,128)(2,1)S(1)} %bitcast.25), channel_id=1, source_target_pairs={{32,0},{64,32},{96,64},{33,1},{65,33},{97,65},{34,2},{66,34},{98,6... | collective-permute-start | bytes 3145736 | tf_op jit(solution)/shard_map/ppermute | solution.py:180
Sparse Core Ops, SparseCore 0:
  24.5 87.2 all-gather.1

commit v2 on v0

v2 whole, which is shorter than its diff:
```python
import functools

import jax
import jax.numpy as jnp
from jax import lax
from jax.experimental import pallas as pl
from jax.experimental.pallas import tpu as pltpu
from jax.sharding import PartitionSpec as P

BLOCK_ROWS = 128
RANK = 16
BF16 = jnp.bfloat16
F32 = jnp.float32

adapter_scale = 2.0

SIDE, CORES = 4, 2
PIECE = 128
BLOCK = SIDE * PIECE
EARLY = 384
HBM = pltpu.MemorySpace.HBM

LAST = (((1,), (1,)), ((), ()))
FIRST = (((0,), (0,)), ((), ()))


def dot(a, b, dims=(((1,), (0,)), ((), ()))):
    return lax.dot_general(a, b, dims, preferred_element_type=F32)


def vmem(mib):
    return pltpu.CompilerParams(vmem_limit_bytes=mib << 20)


def in_hbm(*arrays):
    return [pltpu.with_memory_space_constraint(a, HBM) for a in arrays]


def front_kernel(count_h, grad_ref, up_ref, acts_ref, down_ref, early_ref, late_ref, low_ref,
                 send_ref, count_ref, grad_v, up_v, acts_v, down_v, low_v, message_v,
                 send_v, in_sems, acts_sems, down_sems, out_sems, down_out_sems):
    blocks = count_ref.shape[1]
    rows, depth = grad_v.shape
    chunks, _, wide = acts_v.shape
    take = send_v.shape[2]
    ranks = blocks * RANK
    grad_in = pltpu.make_async_copy(grad_ref, grad_v, in_sems.at[0])
    up_in = pltpu.make_async_copy(up_ref, up_v, in_sems.at[1])
    count_in = pltpu.make_async_copy(count_h, count_ref, in_sems.at[2])
    count_in.start()
    grad_in.start()
    up_in.start()
    acts_in, down_in = [], []
    for i in range(chunks):
        span = pl.ds(i * wide, wide)
        acts_in.append(pltpu.make_async_copy(acts_ref.at[:, span], acts_v.at[i], acts_sems.at[i]))
        down_in.append(pltpu.make_async_copy(down_ref.at[:, span], down_v.at[i], down_sems.at[i]))
        down_in[i].start()
        acts_in[i].start()
    message_v[rows:, :] = jnp.zeros((RANK, depth), BF16)
    count_in.wait()
    grad_in.wait()
    up_in.wait()
    for b in range(blocks):
        span = slice(b * BLOCK_ROWS, (b + 1) * BLOCK_ROWS)
        at = lax.broadcasted_iota(jnp.int32, (BLOCK_ROWS, depth), 0)
        masked = jnp.where(at < count_ref[0, b], grad_v[span, :].astype(F32), 0.0).astype(BF16)
        message_v[span, :] = masked
        low = dot(up_v[b * RANK : (b + 1) * RANK, :], masked, LAST)
        message_v[rows:, span] = (adapter_scale * low).astype(BF16)
    rest = rows + RANK - EARLY
    outs = [
        pltpu.make_async_copy(message_v.at[pl.ds(0, EARLY)], early_ref, out_sems.at[0]),
        pltpu.make_async_copy(message_v.at[pl.ds(EARLY, rest)], late_ref.at[pl.ds(0, rest)], out_sems.at[1]),
    ]
    for out in outs:
        out.start()
    low_v[...] = jnp.zeros_like(low_v)
    fan = wide // take
    for i in range(chunks):
        acts_in[i].wait()
        down_in[i].wait()
        outs.append(pltpu.make_async_copy(
            down_v.at[i], late_ref.at[pl.ds(rest + i * ranks, ranks)], down_out_sems.at[i]
        ))
        outs[-1].start()
        for b in range(blocks):
            span = slice(b * BLOCK_ROWS, (b + 1) * BLOCK_ROWS)
            own = slice(b * RANK, (b + 1) * RANK)
            acts = acts_v[i, span, :]
            low_v[own, :] += dot(down_v[i, own, :], acts, LAST)
            part = dot(message_v[rows:, span], acts).astype(BF16)
            for k in range(fan):
                send_v[i * fan + k, own, :] = part[:, k * take : (k + 1) * take]
        there = (pl.ds(i * fan, fan), pl.ds(0, ranks))
        outs.append(pltpu.make_async_copy(send_v.at[there], send_ref.at[there], out_sems.at[2 + i]))
        outs[-1].start()
    low_ref[...] = low_v[...].astype(BF16)
    for out in outs:
        out.wait()


def front(count, grad, up, acts, down, groups):
    blocks = count.shape[1]
    rows, width = acts.shape
    depth = grad.shape[1]
    wide = depth
    chunks = width // wide
    ranks = blocks * RANK
    shape = jax.ShapeDtypeStruct
    hbm = pl.BlockSpec(memory_space=HBM)
    return pl.pallas_call(
        front_kernel,
        out_shape=(
            shape((EARLY, depth), BF16),
            shape((rows + RANK - EARLY + chunks * ranks, depth), BF16),
            shape((ranks, BLOCK_ROWS), BF16),
            shape((groups, ranks + 16, width // groups), BF16),
        ),
        in_specs=[hbm] * 5,
        out_specs=(hbm, hbm, pl.BlockSpec(memory_space=pltpu.VMEM), hbm),
        scratch_shapes=[
            pltpu.SMEM(count.shape, jnp.int32),
            pltpu.VMEM((rows, depth), BF16),
            pltpu.VMEM((ranks, depth), BF16),
            pltpu.VMEM((chunks, rows, wide), BF16),
            pltpu.VMEM((chunks, ranks, wide), BF16),
            pltpu.VMEM((ranks, BLOCK_ROWS), F32),
            pltpu.VMEM((rows + RANK, depth), BF16),
            pltpu.VMEM((groups, ranks, width // groups), BF16),
            pltpu.SemaphoreType.DMA((3,)),
            pltpu.SemaphoreType.DMA((chunks,)),
            pltpu.SemaphoreType.DMA((chunks,)),
            pltpu.SemaphoreType.DMA((chunks + 2,)),
            pltpu.SemaphoreType.DMA((chunks,)),
        ],
        compiler_params=vmem(16),
        cost_estimate=pl.CostEstimate(flops=10**10, transcendentals=0, bytes_accessed=3 * rows * width),
        name="front",
    )(*in_hbm(count, grad, up, acts, down))


def finish_kernel(ids_h, table_h, early_h, late_h, low_ref, send_in, send_ref, ids_ref, table_ref, message_v,
                  send_v, sems):
    blocks = ids_ref.shape[1]
    ranks = blocks * RANK
    rows, depth = message_v.shape
    groups, _, take = send_v.shape
    ins = [
        pltpu.make_async_copy(ids_h, ids_ref, sems.at[0]),
        pltpu.make_async_copy(table_h, table_ref, sems.at[1]),
        pltpu.make_async_copy(early_h, message_v.at[pl.ds(0, EARLY)], sems.at[2]),
        pltpu.make_async_copy(late_h.at[pl.ds(0, rows - EARLY)], message_v.at[pl.ds(EARLY, rows - EARLY)], sems.at[4]),
    ]
    for copy in ins:
        copy.start()
    for copy in ins:
        copy.wait()
    parts = []
    for b in range(blocks):
        span = slice(b * BLOCK_ROWS, (b + 1) * BLOCK_ROWS)
        low = low_ref[b * RANK : (b + 1) * RANK, :]
        parts.append(adapter_scale * dot(low, message_v[span, :]))
    part = jnp.concatenate(parts, axis=0)
    width = depth // groups
    lane = lax.broadcasted_iota(jnp.int32, (8, 128), 1) // width
    row = lax.broadcasted_iota(jnp.int32, (8, take), 0)
    turn = lax.broadcasted_iota(jnp.int32, (8, take), 1) // RANK % blocks
    slots = jnp.zeros((8, take), F32)
    for b in range(blocks):
        here = ((row == 0) & (turn == b)) | (row == 1 + b)
        slots = jnp.where(here, table_ref[ids_ref[0, b]].astype(F32), slots)
    fit = 128 // width
    for d in range(groups):
        column, mine = d // fit, d % fit
        halves = []
        for h in range(take // 128):
            total = jnp.zeros((8, 128), F32)
            for g in range(fit):
                k = h * fit + g
                tile = part[8 * k : 8 * k + 8, 128 * column : 128 * column + 128]
                tile = pltpu.roll(tile, ((g - mine) * width) % 128, 1)
                total = jnp.where(lane == g, tile, total)
            halves.append(total)
        packed = jnp.concatenate([jnp.concatenate(halves, axis=1), slots], axis=0)
        send_v[d] = packed.astype(BF16)
    out = pltpu.make_async_copy(send_v, send_ref.at[pl.ds(0, groups), pl.ds(ranks, 16)], sems.at[3])
    out.start()
    out.wait()


def finish(ids, table, early, late, low, send):
    hbm = pl.BlockSpec(memory_space=HBM)
    groups, _, take = send.shape
    rows, depth = ids.shape[1] * BLOCK_ROWS, early.shape[1]
    return pl.pallas_call(
        finish_kernel,
        out_shape=jax.ShapeDtypeStruct(send.shape, BF16),
        in_specs=[hbm] * 4 + [pl.BlockSpec(memory_space=pltpu.VMEM), hbm],
        out_specs=hbm,
        scratch_shapes=[
            pltpu.SMEM(ids.shape, jnp.int32),
            pltpu.SMEM(table.shape, jnp.int32),
            pltpu.VMEM((rows, depth), BF16),
            pltpu.VMEM((groups, 16, take), BF16),
            pltpu.SemaphoreType.DMA((5,)),
        ],
        input_output_aliases={5: 0},
        compiler_params=vmem(8),
        cost_estimate=pl.CostEstimate(flops=2 * 10**9, transcendentals=0, bytes_accessed=2 * rows * depth),
        name="finish",
    )(*in_hbm(ids, table, early, late), low, *in_hbm(send))


def join_kernel(counts, spots_ref, *refs):
    parts, outs = refs[: sum(counts)], refs[sum(counts) :]
    i = 0
    for n, out in zip(counts, outs):
        rows = parts[i].shape[0]
        for part in parts[i : i + n]:
            at = pl.multiple_of(spots_ref[i] * rows, rows)
            out[pl.ds(at, rows), :] = part[...]
            i += 1


def join(spots, *groups, cost):
    counts = tuple(len(g) for g in groups)
    in_vmem = pl.BlockSpec(memory_space=pltpu.VMEM)
    return pl.pallas_call(
        functools.partial(join_kernel, counts),
        out_shape=[jax.ShapeDtypeStruct((sum(v.shape[0] for v in g), g[0].shape[1]), BF16) for g in groups],
        in_specs=[pl.BlockSpec(memory_space=pltpu.SMEM)] + [in_vmem] * sum(counts),
        out_specs=[in_vmem] * len(groups),
        compiler_params=vmem(4),
        cost_estimate=pl.CostEstimate(flops=cost, transcendentals=0, bytes_accessed=1 << 21),
        name="join",
    )(spots, *[v for g in groups for v in g])


def collect_kernel(got_h, out_a, out_b, a_v, tail_v, pick_v, sems):
    sources, ranks, take = a_v.shape
    adapters = out_a.shape[0]
    blocks = ranks // RANK
    ins = [
        pltpu.make_async_copy(got_h.at[pl.ds(0, sources), pl.ds(ranks, 16)], tail_v, sems.at[0]),
        pltpu.make_async_copy(got_h.at[pl.ds(0, sources), pl.ds(0, ranks)], a_v, sems.at[1]),
    ]
    for copy in ins:
        copy.start()
    ins[0].wait()
    tail = tail_v[...].astype(F32)
    lane = lax.broadcasted_iota(jnp.int32, (RANK, 128), 1)
    same = lane % RANK == lax.broadcasted_iota(jnp.int32, (RANK, 128), 0)
    fit = 128 // ranks
    for v in range(sources // fit):
        slots = jnp.broadcast_to(tail[v * fit, 8:9, :128], (RANK, 128))
        for k in range(1, fit):
            row = jnp.broadcast_to(tail[v * fit + k, 8:9, :128], (RANK, 128))
            slots = jnp.where(lane // ranks == k, row, slots)
        slots = jnp.where(same, slots, -1.0)
        for j in range(adapters):
            pick = jnp.where(slots == float(j), 1.0, 0.0).astype(BF16)
            pick_v[j * RANK : (j + 1) * RANK, v * 128 : (v + 1) * 128] = pick
    ins[1].wait()
    total = dot(pick_v[...], a_v[...].reshape(sources * ranks, take))
    out_a[...] = total.reshape(adapters, RANK, take).astype(BF16)

    width = out_b.shape[1]
    terms = tail[:, :8, :].reshape(sources * 8, take).astype(BF16)
    lane = lax.broadcasted_iota(jnp.int32, (adapters, sources * 8), 1)
    slot = lax.broadcasted_iota(jnp.int32, (adapters, sources * 8), 0).astype(F32)
    sums = []
    for b in range(blocks):
        slots = jnp.zeros((1, sources * 8), F32)
        for source in range(sources):
            slots = jnp.where(lane[:1] // 8 == source, tail[source, 9 + b : 10 + b, : sources * 8], slots)
        hit = slots == slot
        pick = jnp.concatenate([jnp.where(hit & (lane % 8 == r), 1.0, 0.0) for r in range(8)], axis=0)
        at = b * 2 * width
        total = dot(pick.astype(BF16), terms[:, at // 128 * 128 : at // 128 * 128 + 128])
        sums.append(pltpu.roll(total, (128 - at % 128) % 128, 1))
    total = sums[0]
    for more in sums[1:]:
        total = total + more
    for r in range(8):
        turned = total[r * adapters : (r + 1) * adapters, :].T
        out_b[r] = turned[:width].astype(BF16)
        out_b[8 + r] = turned[width : 2 * width].astype(BF16)


def collect(got, adapters, blocks, depth):
    groups, _, take = got.shape
    ranks = blocks * RANK
    in_vmem = pl.BlockSpec(memory_space=pltpu.VMEM)
    return pl.pallas_call(
        collect_kernel,
        out_shape=(
            jax.ShapeDtypeStruct((adapters, RANK, take), BF16),
            jax.ShapeDtypeStruct((RANK, depth // groups, adapters), BF16),
        ),
        in_specs=[pl.BlockSpec(memory_space=HBM)],
        out_specs=(in_vmem, in_vmem),
        scratch_shapes=[
            pltpu.VMEM((groups, ranks, take), BF16),
            pltpu.VMEM((groups, 16, take), BF16),
            pltpu.VMEM((adapters * RANK, groups * ranks), BF16),
            pltpu.SemaphoreType.DMA((2,)),
        ],
        compiler_params=vmem(20),
        cost_estimate=pl.CostEstimate(flops=4 * 10**9, transcendentals=0, bytes_accessed=4 * got.size),
        name="collect",
    )(*in_hbm(got))


def unpack_kernel(early_ref, late_ref, message_ref, low_ref, down_ref):
    rows = message_ref.shape[0]
    ranks = low_ref.shape[1]
    rest = rows - EARLY
    message_ref[:EARLY, :] = early_ref[...]
    message_ref[EARLY:, :] = late_ref[:rest, :]
    down_ref[...] = late_ref[rest + RANK :, :]
    low = jnp.concatenate([late_ref[rest : rest + RANK, :rows].astype(F32)] * (ranks // RANK), axis=0)
    own = lax.broadcasted_iota(jnp.int32, low.shape, 0) // RANK
    of = lax.broadcasted_iota(jnp.int32, low.shape, 1) // BLOCK_ROWS
    low_ref[...] = jnp.where(own == of, low, 0.0).T.astype(BF16)


def unpack(early, late, rows, ranks):
    depth = early.shape[1]
    shape = jax.ShapeDtypeStruct
    in_vmem = pl.BlockSpec(memory_space=pltpu.VMEM)
    return pl.pallas_call(
        unpack_kernel,
        out_shape=(
            shape((rows, depth), BF16),
            shape((rows, ranks), BF16),
            shape((late.shape[0] + EARLY - rows - RANK, depth), BF16),
        ),
        in_specs=[in_vmem] * 2,
        out_specs=(in_vmem,) * 3,
        compiler_params=vmem(4),
        name="unpack",
    )(early, late)


def product_kernel(which, alias, starts_ref, message_ref, low_ref, down_ref, *refs):
    n = len(which)
    blocks = refs[:n]
    out_ref, out_v, out_sems = refs[n + alias :]
    ranks, wide = low_ref.shape[1], down_ref.shape[1]
    outs = []
    for i in range(n):
        start = pl.multiple_of(starts_ref[which[i]], BLOCK)
        chunk = pl.ds(pl.multiple_of(start // wide * ranks, ranks), ranks)
        down = down_ref[chunk, pl.ds(pl.multiple_of(start % wide, BLOCK), BLOCK)]
        total = dot(message_ref[...], blocks[i][...], LAST) + dot(low_ref[...], down)
        out_v[i] = total.astype(BF16)
        out = pltpu.make_async_copy(out_v.at[i], out_ref.at[:, pl.ds(start, BLOCK)], out_sems.at[i])
        out.start()
        outs.append(out)
    for out in outs:
        out.wait()


def product(blocks, starts, message, low, down, before, name):
    n = len(blocks)
    rows, depth = message.shape
    width = down.size // low.shape[1]
    operands = [starts, message, low, down, *[b[0] for b in blocks]]
    in_vmem = pl.BlockSpec(memory_space=pltpu.VMEM)
    in_specs = [pl.BlockSpec(memory_space=pltpu.SMEM)] + [in_vmem] * (len(operands) - 1)
    hbm = pl.BlockSpec(memory_space=HBM)
    if before is not None:
        operands += in_hbm(before)
        in_specs.append(hbm)
    columns = n * BLOCK
    return pl.pallas_call(
        functools.partial(product_kernel, tuple(b[1] for b in blocks), before is not None),
        out_shape=jax.ShapeDtypeStruct((rows, width), BF16),
        in_specs=in_specs,
        out_specs=hbm,
        scratch_shapes=[pltpu.VMEM((n, rows, BLOCK), BF16), pltpu.SemaphoreType.DMA((n,))],
        input_output_aliases={} if before is None else {len(operands) - 1: 0},
        compiler_params=vmem(12),
        cost_estimate=pl.CostEstimate(
            flops=3 * rows * depth * columns, transcendentals=0, bytes_accessed=2 * columns * (depth + rows)
        ),
        name=name,
    )(*operands)


def spot(at, core):
    return (at + core) % SIDE


def near(at, core):
    return ((spot(at, core) ^ 1) - core) % SIDE


def far(at, core):
    return (SIDE - 1 - spot(at, core) - core) % SIDE


def moved(array, to):
    route = []
    for d in range(SIDE * SIDE * CORES):
        x, z, core = to(d // (SIDE * CORES), d // CORES % SIDE, d % CORES)
        route.append((d, (x * SIDE + z) * CORES + core))
    return lax.ppermute(array, "dp", route)


def x_near(x, z, core):
    return near(x, core), z, core


def x_far(x, z, core):
    return far(x, core), z, core


def z_near(x, z, core):
    return x, near(z, core), core


def z_far(x, z, core):
    return x, far(z, core), core


def other_core(x, z, core):
    return x, z, 1 - core


def places(line, core):
    steps = (line, near(line, core), far(line, core), near(far(line, core), core))
    return [(s * CORES + core) * BLOCK for s in steps]


def hop(x, route):
    return lax.ppermute(x, "pipe", route)


def tie(*arrays):
    return lax.optimization_barrier(arrays)


def body(
    acts,
    output_gradient,
    frozen_value_weight,
    adapter_down_weight,
    adapter_up_weight,
    block_adapter_index,
    token_row_count,
    adapter_slot_table,
):
    blocks = token_row_count.shape[1]
    rows, width = acts.shape[1:]
    depth = output_gradient.shape[2]
    adapters = adapter_slot_table.shape[0]
    groups = lax.axis_size("dp")
    down = adapter_down_weight.reshape(blocks * RANK, width)
    up = adapter_up_weight.reshape(blocks * RANK, depth)
    half = width // 2
    me = lax.axis_index("dp")
    x, z, core = me // (SIDE * CORES), me // CORES % SIDE, me % CORES
    back = [(1, 0), (2, 1), (3, 2)]

    piece_a = lax.dynamic_slice_in_dim(
        frozen_value_weight[0], ((z * CORES + core) * SIDE + spot(x, core)) * PIECE, PIECE, 0
    )
    piece_b = lax.dynamic_slice_in_dim(
        frozen_value_weight[0], half + ((x * CORES + core) * SIDE + spot(z, core)) * PIECE, PIECE, 0
    )
    a0, b0 = hop(piece_a, back), hop(piece_b, back)
    early, late, low, send = front(token_row_count, output_gradient[0], up, acts[0], down, groups)
    spot_a, spot_b = spot(x, core), spot(z, core)
    halves = jnp.stack([spot_a % 2, 1 - spot_a % 2, spot_b % 2, 1 - spot_b % 2]).astype(jnp.int32)
    wholes = jnp.stack([spot_a // 2, 1 - spot_a // 2, spot_b // 2, 1 - spot_b // 2]).astype(jnp.int32)
    starts = []
    for c in (core, 1 - core):
        starts += places(z, c) + [half + s for s in places(x, c)]
    starts = jnp.stack(starts).astype(jnp.int32)
    a0, b0, send, early, late, low, halves, wholes, starts = tie(
        a0, b0, send, early, late, low, halves, wholes, starts
    )

    a1, b1 = moved(a0, x_near), moved(b0, z_near)
    send = finish(block_adapter_index, adapter_slot_table, early, late, low, send)
    early = hop(early, back)
    got = lax.all_to_all(send, "dp", split_axis=0, concat_axis=0, tiled=True)
    a0, b0, a1, b1, send, late = tie(a0, b0, a1, b1, send, late)

    ap, bp = join(halves, (a0, a1), (b0, b1), cost=10**6)
    aq, bq = moved(ap, x_far), moved(bp, z_far)
    aq, bq, ap, bp, early, late = tie(aq, bq, ap, bp, early, late)

    late = hop(late, back)
    a, b = join(wholes, (ap, aq), (bp, bq), cost=10**6)
    a_near, b_near = moved(a, z_near), moved(b, x_near)
    a_far, b_far = moved(a, z_far), moved(b, x_far)
    total_a, total_b = collect(got, adapters, blocks, depth)
    a, b, a_near, b_near, a_far, b_far, late, total_a, total_b = tie(
        a, b, a_near, b_near, a_far, b_far, late, total_a, total_b
    )

    def pair(a, b, step, mine=True):
        at = step if mine else step + 2 * SIDE
        return [(a, at), (b, at + SIDE)]

    def others(a, b, step):
        return pair(moved(a, other_core), moved(b, other_core), step, False)

    a_last, b_last = moved(a_near, z_far), moved(b_near, x_far)
    shared = (starts, *unpack(early, late, rows, blocks * RANK))
    mine = pair(a, b, 0) + pair(a_near, b_near, 1) + pair(a_far, b_far, 2)
    theirs = others(a, b, 0) + others(a_near, b_near, 1) + others(a_far, b_far, 2)
    received = product(mine, *shared, None, "product_mine")
    received = product(theirs, *shared, received, "product_theirs")
    received, a_last, b_last = tie(received, a_last, b_last)
    theirs = others(a_last, b_last, 3)
    received = product(pair(a_last, b_last, 3), *shared, received, "product_last")
    received = product(theirs, *shared, received, "product_end")
    return received[None], total_a[None], jnp.transpose(total_b, (2, 0, 1))[None]


def solution(mesh):
    in_specs = (
        P("pipe", "dp", None),
        P("pipe", "dp", None),
        P("pipe", None, None),
        P("pipe", "dp", None, None),
        P("pipe", "dp", None, None),
        P("pipe", "dp"),
        P("pipe", "dp"),
        P(),
    )
    out_specs = (P("pipe", "dp", None), P("pipe", None, None, "dp"), P("pipe", None, None, "dp"))
    return jax.shard_map(body, mesh=mesh, in_specs=in_specs, out_specs=out_specs, check_vma=False)
```

time: 223 us -> 114 us (0.51)
  waiting for transfers between devices: 128 us -> 33.2 us
  matrix products: 40.2 us -> 0 us
  Pallas kernels: 0 us -> 39.2 us
  blocking collectives: 21.8 us -> 0 us
  starting transfers between devices: 16.2 us -> 31.4 us
  local copies, waits for them, and re-layouts: 13.2 us -> 6.95 us
    ppermute x1 -> x22, waiting for transfers between devices: 126 us -> 30.3 us  [the longest x18 22.5 us: moved(): return lax.ppermute(array, 'dp', route)]
    dot_general x6 -> x0, matrix products: 40 us -> none  [the longest x1 19.4 us: body(): lax.dot_general(grad_rows.reshape(live_count * BLOCK_ROWS, out_width), we...]
    pallas_call x0 -> x10, Pallas kernels: none -> 39.2 us  [the longest x4 18.9 us: product(): pl.pallas_call(functools.partial(product_kernel, tuple((b[1] for b in blo...]
    unnamed x1 -> x0, blocking collectives: 21.8 us -> none
    ppermute x1 -> x22, starting transfers between devices: 1.28 us -> 22.5 us  [the longest x18 17.4 us: moved(): return lax.ppermute(array, 'dp', route)]
    all_to_all x2 -> x1, starting transfers between devices: 14.9 us -> 8.91 us  [body(): got = lax.all_to_all(send, 'dp', split_axis=0, concat_axis=0, tiled=True)]
    unnamed x17 -> x12, local copies, waits for them, and re-layouts: 11 us -> 5.79 us
  transfers between devices with their start and end apart: 3 -> 23, of which waited for: 2 -> 10; matrix products, arithmetic and copies ran while one was open for 8% -> 0% of each run, Pallas kernels for 0% -> 32%
where the time goes in v2:
time: 114 us; the launch traced here: 112 us
  Pallas kernels  39.2 us (34%)
  waiting for transfers between devices  33.2 us (29%)
  starting transfers between devices  31.4 us (28%)
  local copies, waits for them, and re-layouts  6.95 us (6%)
    ppermute x18, waiting for transfers between devices, moved(): return lax.ppermute(array, 'dp', route)  22.5 us
    pallas_call x4, Pallas kernels, product(): pl.pallas_call(functools.partial(product_kernel, tuple((b[1] for b in blo...  18.9 us
    ppermute x18, starting transfers between devices, moved(): return lax.ppermute(array, 'dp', route)  17.4 us
    pallas_call x1, Pallas kernels, front(): pl.pallas_call(front_kernel, out_shape=(shape((EARLY, depth), BF16), shap...  10.5 us
    all_to_all x1, starting transfers between devices, body(): got = lax.all_to_all(send, 'dp', split_axis=0, concat_axis=0, tiled=True)  8.91 us
    ppermute x4, waiting for transfers between devices, hop(): return lax.ppermute(x, 'pipe', route)  7.85 us
    unnamed x12, local copies, waits for them, and re-layouts  5.79 us
    ppermute x4, starting transfers between devices, hop(): return lax.ppermute(x, 'pipe', route)  5.14 us
  transfers between devices with their start and end apart: 23, of which 10 were waited for; matrix products, arithmetic and copies ran while one was open for 0% of the time, Pallas kernels for 32%

profile of v2, /device:TPU:1, one launch (start us, length us, event | category | flops | bytes accessed | tf_op | source)
XLA Modules:
  0.0 111.9 jit_solution(8615357574818352803)
XLA Ops:
  1.8 1.3 %collective-permute-start.1 = (bf16[128,1024]{1,0:T(8,128)(2,1)S(1)}, bf16[128,1024]{1,0:T(8,128)(2,1)S(1)}, u32[]{:S(2)}, u32[]{:S(2)}) collective-permute-start(bf16[128,1024]{1,0:T(8,128)(2,1)S(1)} %get-tuple-element.93), channel_id=1, source_target_pairs={{32,0},{64,32},{96,64},{33,1},{65,33},{97,65},{34,2},{66,34},{98,6... | collective-permute-start | bytes 786440 | tf_op jit(solution)/shard_map/ppermute | solution.py:438
  3.1 1.3 %collective-permute-start = (bf16[128,1024]{1,0:T(8,128)(2,1)S(1)}, bf16[128,1024]{1,0:T(8,128)(2,1)S(1)}, u32[]{:S(2)}, u32[]{:S(2)}) collective-permute-start(bf16[128,1024]{1,0:T(8,128)(2,1)S(1)} %get-tuple-element.94), channel_id=1, source_target_pairs={{32,0},{64,32},{96,64},{33,1},{65,33},{97,65},{34,2},{66,34},{98,6... | collective-permute-start | bytes 786440 | tf_op jit(solution)/shard_map/ppermute | solution.py:438
  4.4 10.5 %front.1 = (bf16[384,1024]{1,0:T(8,128)(2,1)}, bf16[656,1024]{1,0:T(8,128)(2,1)S(1)}, bf16[64,128]{1,0:T(8,128)(2,1)S(1)}, bf16[32,80,256]{2,1,0:T(8,128)(2,1)S(1)}) custom-call(s32[1,4]{1,0:T(1,128)} %count_h.1, bf16[512,1024]{1,0:T(8,128)(2,1)} %bitcast.39, bf16[64,1024]{1,0:T(8,128)(2,1)} %bitcast.41, bf16[512,8192]{1,0:T(8,128)(2,1)} %bitcast.38, ...), custom_call_target="tpu_custom_call" | custom-call | flops 10000000000 | bytes 12582912 | tf_op jit(solution)/shard_map/front/pallas_call | solution.py:112
  17.2 3.4 %collective-permute-start.2 = (bf16[128,1024]{1,0:T(8,128)(2,1)S(1)}, bf16[128,1024]{1,0:T(8,128)(2,1)S(1)}, u32[]{:S(2)}, u32[]{:S(2)}) collective-permute-start(bf16[128,1024]{1,0:T(8,128)(2,1)S(1)} %collective-permute-done.refs_0_), channel_id=1, source_target_pairs={{0,8},{1,25},{2,10},{3,27},{4,12},{5,29},{6,14},{7,31},{8,0},{9,17... | collective-permute-start | bytes 786440 | tf_op jit(solution)/shard_map/ppermute | solution.py:409
  20.6 3.8 %collective-permute-start.3 = (bf16[128,1024]{1,0:T(8,128)(2,1)S(1)}, bf16[128,1024]{1,0:T(8,128)(2,1)S(1)}, u32[]{:S(2)}, u32[]{:S(2)}) collective-permute-start(bf16[128,1024]{1,0:T(8,128)(2,1)S(1)} %collective-permute-done.1.refs_2_), channel_id=1, source_target_pairs={{0,2},{1,7},{2,0},{3,5},{4,6},{5,3},{6,4},{7,1},{8,10},{9,15},{10,... | collective-permute-start | bytes 786440 | tf_op jit(solution)/shard_map/ppermute | solution.py:409
  24.3 1.3 %collective-permute-start.6 = (bf16[384,1024]{1,0:T(8,128)(2,1)}, bf16[384,1024]{1,0:T(8,128)(2,1)S(1)}, u32[]{:S(2)}, u32[]{:S(2)}) collective-permute-start(bf16[384,1024]{1,0:T(8,128)(2,1)} %get-tuple-element.56.early_h), channel_id=1, source_target_pairs={{32,0},{64,32},{96,64},{33,1},{65,33},{97,65},{34,2},{66,34},{98,6... | collective-permute-start | bytes 2359304 | tf_op jit(solution)/shard_map/ppermute | solution.py:438
  25.6 2.4 %finish.1 = bf16[32,80,256]{2,1,0:T(8,128)(2,1)} custom-call(s32[1,4]{1,0:T(1,128)} %ids_h.1, s32[64]{0:T(128)} %table_h.1, bf16[384,1024]{1,0:T(8,128)(2,1)} %get-tuple-element.56.early_h, bf16[656,1024]{1,0:T(8,128)(2,1)} %copy-done.5, bf16[64,128]{1,0:T(8,128)(2,1)S(1)} %get-tuple-element.58.low_ref, ...), custom_call_target="tpu_custom_call", output_to_operand_aliasing={{}: (5, {})} | custom-call | flops 2000000000 | bytes 1048576 | tf_op jit(solution)/shard_map/finish/pallas_call | solution.py:196
  28.9 8.9 %all-to-all-start = ((bf16[32,80,256]{2,1,0:T(8,128)(2,1)}), bf16[32,80,256]{2,1,0:T(8,128)(2,1)}, u32[]{:S(2)}, u32[]{:S(2)}) async-start(bf16[32,80,256]{2,1,0:T(8,128)(2,1)} %finish.1), calls=%async_computation | async-start | bytes 2621440 | tf_op jit(solution)/shard_map/all_to_all | solution.py:489
  37.8 7.8 %collective-permute-done.6.early_ref = bf16[384,1024]{1,0:T(8,128)(2,1)S(1)} collective-permute-done((bf16[384,1024]{1,0:T(8,128)(2,1)}, bf16[384,1024]{1,0:T(8,128)(2,1)S(1)}, u32[]{:S(2)}, u32[]{:S(2)}) %collective-permute-start.6) | collective-permute-done | bytes 786464 | tf_op jit(solution)/shard_map/ppermute | solution.py:438
  47.3 1.3 %collective-permute-start.11 = (bf16[656,1024]{1,0:T(8,128)(2,1)}, bf16[656,1024]{1,0:T(8,128)(2,1)S(1)}, u32[]{:S(2)}, u32[]{:S(2)}) collective-permute-start(bf16[656,1024]{1,0:T(8,128)(2,1)} %copy-done.5), channel_id=1, source_target_pairs={{32,0},{64,32},{96,64},{33,1},{65,33},{97,65},{34,2},{66,34},{98,6... | collective-permute-start | bytes 4030472 | tf_op jit(solution)/shard_map/ppermute | solution.py:438
  50.6 2.0 %join.3 = (bf16[512,1024]{1,0:T(8,128)(2,1)}, bf16[512,1024]{1,0:T(8,128)(2,1)}) custom-call(s32[4]{0:T(128)S(1)} %get-tuple-element.68.spots_ref, bf16[256,1024]{1,0:T(8,128)(2,1)S(1)} %get-tuple-element.69.refs_0_, bf16[256,1024]{1,0:T(8,128)(2,1)S(1)} %copy-done.2, bf16[256,1024]{1,0:T(8,128)(2,1)S(1)} %get-tuple-element.71.refs_2_, ...), custom_call_target="tpu_custom_call" | custom-call | flops 1000000 | bytes 2097152 | tf_op jit(solution)/shard_map/join/pallas_call | solution.py:229
  52.7 1.2 %collective-permute-start.7 = (bf16[512,1024]{1,0:T(8,128)(2,1)}, bf16[512,1024]{1,0:T(8,128)(2,1)S(1)}, u32[]{:S(2)}, u32[]{:S(2)}) collective-permute-start(bf16[512,1024]{1,0:T(8,128)(2,1)} %get-tuple-element.82.refs_0_), channel_id=1, source_target_pairs={{0,2},{1,7},{2,0},{3,5},{4,6},{5,3},{6,4},{7,1},{8,10},{9,15},{10,... | collective-permute-start | bytes 3145736 | tf_op jit(solution)/shard_map/ppermute | solution.py:409
  54.9 2.9 %all-to-all-done.got_h = bf16[32,80,256]{2,1,0:T(8,128)(2,1)} async-done(((bf16[32,80,256]{2,1,0:T(8,128)(2,1)}), bf16[32,80,256]{2,1,0:T(8,128)(2,1)}, u32[]{:S(2)}, u32[]{:S(2)}) %all-to-all-start) | async-done | bytes 1310752 | tf_op jit(solution)/shard_map/all_to_all | solution.py:489
  57.8 4.6 %collect.1 = (bf16[64,16,256]{2,1,0:T(8,128)(2,1)}, bf16[16,32,64]{2,1,0:T(8,128)(2,1)}) custom-call(bf16[32,80,256]{2,1,0:T(8,128)(2,1)} %all-to-all-done.got_h), custom_call_target="tpu_custom_call" | custom-call | flops 4000000000 | bytes 2621440 | tf_op jit(solution)/shard_map/collect/pallas_call | solution.py:295
  62.4 9.6 %collective-permute-done.9.refs_4_ = bf16[512,1024]{1,0:T(8,128)(2,1)} collective-permute-done((bf16[512,1024]{1,0:T(8,128)(2,1)}, bf16[512,1024]{1,0:T(8,128)(2,1)}, u32[]{:S(2)}, u32[]{:S(2)}) %collective-permute-start.9) | collective-permute-done | bytes 1048608 | tf_op jit(solution)/shard_map/ppermute | solution.py:409
  72.0 5.9 %collective-permute-done.7.refs_2_ = bf16[512,1024]{1,0:T(8,128)(2,1)S(1)} collective-permute-done((bf16[512,1024]{1,0:T(8,128)(2,1)}, bf16[512,1024]{1,0:T(8,128)(2,1)S(1)}, u32[]{:S(2)}, u32[]{:S(2)}) %collective-permute-start.7) | collective-permute-done | bytes 1048608 | tf_op jit(solution)/shard_map/ppermute | solution.py:409
  77.9 3.6 %collective-permute-start.12 = (bf16[512,1024]{1,0:T(8,128)(2,1)}, bf16[512,1024]{1,0:T(8,128)(2,1)S(1)}, u32[]{:S(2)}, u32[]{:S(2)}) collective-permute-start(bf16[512,1024]{1,0:T(8,128)(2,1)} %get-tuple-element.82.refs_0_), channel_id=1, source_target_pairs={{0,1},{1,0},{2,3},{3,2},{4,5},{5,4},{6,7},{7,6},{8,9},{9,8},{10,11... | collective-permute-start | bytes 3145736 | tf_op jit(solution)/shard_map/ppermute | solution.py:409
  82.5 1.5 %collective-permute-done.12.refs_0_ = bf16[512,1024]{1,0:T(8,128)(2,1)S(1)} collective-permute-done((bf16[512,1024]{1,0:T(8,128)(2,1)}, bf16[512,1024]{1,0:T(8,128)(2,1)S(1)}, u32[]{:S(2)}, u32[]{:S(2)}) %collective-permute-start.12) | collective-permute-done | bytes 1048608 | tf_op jit(solution)/shard_map/ppermute | solution.py:409
  84.4 2.6 %collective-permute-done.13.refs_1_ = bf16[512,1024]{1,0:T(8,128)(2,1)S(1)} collective-permute-done((bf16[512,1024]{1,0:T(8,128)(2,1)}, bf16[512,1024]{1,0:T(8,128)(2,1)S(1)}, u32[]{:S(2)}, u32[]{:S(2)}) %collective-permute-start.13) | collective-permute-done | bytes 1048608 | tf_op jit(solution)/shard_map/ppermute | solution.py:409
  88.7 7.6 %product_mine.1.refs_6_ = bf16[512,8192]{1,0:T(8,128)(2,1)} custom-call(s32[16]{0:T(128)S(1)} %stack.107.starts_ref, bf16[512,1024]{1,0:T(8,128)(2,1)S(1)} %get-tuple-element.79.message_ref, bf16[512,64]{1,0:T(8,128)(2,1)S(1)} %get-tuple-element.80.low_ref, bf16[512,1024]{1,0:T(8,128)(2,1)S(1)} %get-tuple-element.81.down_ref, ...), custom_call_target="tpu_custom_call" | custom-call | flops 4831838208 | bytes 9437184 | tf_op jit(solution)/shard_map/product_mine/pallas_call | solution.py:377
  96.3 5.6 %product_theirs.1.refs_2_ = bf16[512,8192]{1,0:T(8,128)(2,1)} custom-call(s32[16]{0:T(128)S(1)} %stack.107.starts_ref, bf16[512,1024]{1,0:T(8,128)(2,1)S(1)} %get-tuple-element.79.message_ref, bf16[512,64]{1,0:T(8,128)(2,1)S(1)} %get-tuple-element.80.low_ref, bf16[512,1024]{1,0:T(8,128)(2,1)S(1)} %get-tuple-element.81.down_ref, ...), custom_call_target="tpu_custom_call", output_to_operand_aliasing={{}: (10, {})} | custom-call | flops 4831838208 | bytes 9437184 | tf_op jit(solution)/shard_map/product_theirs/pallas_call | solution.py:377
  102.7 2.4 %collective-permute-start.20 = (bf16[512,1024]{1,0:T(8,128)(2,1)S(1)}, bf16[512,1024]{1,0:T(8,128)(2,1)S(1)}, u32[]{:S(2)}, u32[]{:S(2)}) collective-permute-start(bf16[512,1024]{1,0:T(8,128)(2,1)S(1)} %collective-permute-done.18.refs_0_), channel_id=1, source_target_pairs={{0,1},{1,0},{2,3},{3,2},{4,5},{5,4},{6,7},{7,6},{8,9},{9,8},{10,11... | collective-permute-start | bytes 3145736 | tf_op jit(solution)/shard_map/ppermute | solution.py:409
  105.1 2.9 %product_last.1.refs_2_ = bf16[512,8192]{1,0:T(8,128)(2,1)} custom-call(s32[16]{0:T(128)S(1)} %stack.107.starts_ref, bf16[512,1024]{1,0:T(8,128)(2,1)S(1)} %get-tuple-element.79.message_ref, bf16[512,64]{1,0:T(8,128)(2,1)S(1)} %get-tuple-element.80.low_ref, bf16[512,1024]{1,0:T(8,128)(2,1)S(1)} %get-tuple-element.81.down_ref, ...), custom_call_target="tpu_custom_call", output_to_operand_aliasing={{}: (6, {})} | custom-call | flops 1610612736 | bytes 3145728 | tf_op jit(solution)/shard_map/product_last/pallas_call | solution.py:377
  108.9 2.9 %product_end.1 = bf16[512,8192]{1,0:T(8,128)(2,1)} custom-call(s32[16]{0:T(128)S(1)} %stack.107.starts_ref, bf16[512,1024]{1,0:T(8,128)(2,1)S(1)} %get-tuple-element.79.message_ref, bf16[512,64]{1,0:T(8,128)(2,1)S(1)} %get-tuple-element.80.low_ref, bf16[512,1024]{1,0:T(8,128)(2,1)S(1)} %get-tuple-element.81.down_ref, ...), custom_call_target="tpu_custom_call", output_to_operand_aliasing={{}: (6, {})} | custom-call | flops 1610612736 | bytes 3145728 | tf_op jit(solution)/shard_map/product_end/pallas_call | solution.py:377
  (47 shorter events, 13.7 us)
Async XLA Ops:
  1.8 15.4 %collective-permute-start.1 = (bf16[128,1024]{1,0:T(8,128)(2,1)S(1)}, bf16[128,1024]{1,0:T(8,128)(2,1)S(1)}, u32[]{:S(2)}, u32[]{:S(2)}) collective-permute-start(bf16[128,1024]{1,0:T(8,128)(2,1)S(1)} %get-tuple-element.93), channel_id=1, source_target_pairs={{32,0},{64,32},{96,64},{33,1},{65,33},{97,65},{34,2},{66,34},{98,6... | collective-permute-start | bytes 786440 | tf_op jit(solution)/shard_map/ppermute | solution.py:438
  3.1 14.1 %collective-permute-start = (bf16[128,1024]{1,0:T(8,128)(2,1)S(1)}, bf16[128,1024]{1,0:T(8,128)(2,1)S(1)}, u32[]{:S(2)}, u32[]{:S(2)}) collective-permute-start(bf16[128,1024]{1,0:T(8,128)(2,1)S(1)} %get-tuple-element.94), channel_id=1, source_target_pairs={{32,0},{64,32},{96,64},{33,1},{65,33},{97,65},{34,2},{66,34},{98,6... | collective-permute-start | bytes 786440 | tf_op jit(solution)/shard_map/ppermute | solution.py:438
  14.9 1.1 copy-start
  17.2 10.8 %collective-permute-start.2 = (bf16[128,1024]{1,0:T(8,128)(2,1)S(1)}, bf16[128,1024]{1,0:T(8,128)(2,1)S(1)}, u32[]{:S(2)}, u32[]{:S(2)}) collective-permute-start(bf16[128,1024]{1,0:T(8,128)(2,1)S(1)} %collective-permute-done.refs_0_), channel_id=1, source_target_pairs={{0,8},{1,25},{2,10},{3,27},{4,12},{5,29},{6,14},{7,31},{8,0},{9,17... | collective-permute-start | bytes 786440 | tf_op jit(solution)/shard_map/ppermute | solution.py:409
  20.6 7.5 %collective-permute-start.3 = (bf16[128,1024]{1,0:T(8,128)(2,1)S(1)}, bf16[128,1024]{1,0:T(8,128)(2,1)S(1)}, u32[]{:S(2)}, u32[]{:S(2)}) collective-permute-start(bf16[128,1024]{1,0:T(8,128)(2,1)S(1)} %collective-permute-done.1.refs_2_), channel_id=1, source_target_pairs={{0,2},{1,7},{2,0},{3,5},{4,6},{5,3},{6,4},{7,1},{8,10},{9,15},{10,... | collective-permute-start | bytes 786440 | tf_op jit(solution)/shard_map/ppermute | solution.py:409
  24.3 21.3 %collective-permute-start.6 = (bf16[384,1024]{1,0:T(8,128)(2,1)}, bf16[384,1024]{1,0:T(8,128)(2,1)S(1)}, u32[]{:S(2)}, u32[]{:S(2)}) collective-permute-start(bf16[384,1024]{1,0:T(8,128)(2,1)} %get-tuple-element.56.early_h), channel_id=1, source_target_pairs={{32,0},{64,32},{96,64},{33,1},{65,33},{97,65},{34,2},{66,34},{98,6... | collective-permute-start | bytes 2359304 | tf_op jit(solution)/shard_map/ppermute | solution.py:438
  28.7 16.9 %collective-permute-start.4 = (bf16[256,1024]{1,0:T(8,128)(2,1)S(1)}, bf16[256,1024]{1,0:T(8,128)(2,1)S(1)}, u32[]{:S(2)}, u32[]{:S(2)}) collective-permute-start(bf16[256,1024]{1,0:T(8,128)(2,1)S(1)} %get-tuple-element.69.refs_0_), channel_id=1, source_target_pairs={{0,24},{1,9},{2,26},{3,11},{4,28},{5,13},{6,30},{7,15},{8,16},{9,1... | collective-permute-start | bytes 1572872 | tf_op jit(solution)/shard_map/ppermute | solution.py:409
  28.8 17.7 %collective-permute-start.5 = (bf16[256,1024]{1,0:T(8,128)(2,1)S(1)}, bf16[256,1024]{1,0:T(8,128)(2,1)S(1)}, u32[]{:S(2)}, u32[]{:S(2)}) collective-permute-start(bf16[256,1024]{1,0:T(8,128)(2,1)S(1)} %get-tuple-element.71.refs_2_), channel_id=1, source_target_pairs={{0,6},{1,3},{2,4},{3,1},{4,2},{5,7},{6,0},{7,5},{8,14},{9,11},{10,... | collective-permute-start | bytes 1572872 | tf_op jit(solution)/shard_map/ppermute | solution.py:409
  28.9 28.9 %all-to-all-start = ((bf16[32,80,256]{2,1,0:T(8,128)(2,1)}), bf16[32,80,256]{2,1,0:T(8,128)(2,1)}, u32[]{:S(2)}, u32[]{:S(2)}) async-start(bf16[32,80,256]{2,1,0:T(8,128)(2,1)} %finish.1), calls=%async_computation | async-start | bytes 2621440 | tf_op jit(solution)/shard_map/all_to_all | solution.py:489
  47.3 30.6 %collective-permute-start.11 = (bf16[656,1024]{1,0:T(8,128)(2,1)}, bf16[656,1024]{1,0:T(8,128)(2,1)S(1)}, u32[]{:S(2)}, u32[]{:S(2)}) collective-permute-start(bf16[656,1024]{1,0:T(8,128)(2,1)} %copy-done.5), channel_id=1, source_target_pairs={{32,0},{64,32},{96,64},{33,1},{65,33},{97,65},{34,2},{66,34},{98,6... | collective-permute-start | bytes 4030472 | tf_op jit(solution)/shard_map/ppermute | solution.py:438
  52.7 19.3 %collective-permute-start.9 = (bf16[512,1024]{1,0:T(8,128)(2,1)}, bf16[512,1024]{1,0:T(8,128)(2,1)}, u32[]{:S(2)}, u32[]{:S(2)}) collective-permute-start(bf16[512,1024]{1,0:T(8,128)(2,1)} %get-tuple-element.82.refs_0_), channel_id=1, source_target_pairs={{0,6},{1,3},{2,4},{3,1},{4,2},{5,7},{6,0},{7,5},{8,14},{9,11},{10,... | collective-permute-start | bytes 3145736 | tf_op jit(solution)/shard_map/ppermute | solution.py:409
  52.7 25.2 %collective-permute-start.7 = (bf16[512,1024]{1,0:T(8,128)(2,1)}, bf16[512,1024]{1,0:T(8,128)(2,1)S(1)}, u32[]{:S(2)}, u32[]{:S(2)}) collective-permute-start(bf16[512,1024]{1,0:T(8,128)(2,1)} %get-tuple-element.82.refs_0_), channel_id=1, source_target_pairs={{0,2},{1,7},{2,0},{3,5},{4,6},{5,3},{6,4},{7,1},{8,10},{9,15},{10,... | collective-permute-start | bytes 3145736 | tf_op jit(solution)/shard_map/ppermute | solution.py:409
  53.9 24.0 %collective-permute-start.10 = (bf16[512,1024]{1,0:T(8,128)(2,1)}, bf16[512,1024]{1,0:T(8,128)(2,1)}, u32[]{:S(2)}, u32[]{:S(2)}) collective-permute-start(bf16[512,1024]{1,0:T(8,128)(2,1)} %get-tuple-element.83.refs_1_), channel_id=1, source_target_pairs={{0,24},{1,9},{2,26},{3,11},{4,28},{5,13},{6,30},{7,15},{8,16},{9,1... | collective-permute-start | bytes 3145736 | tf_op jit(solution)/shard_map/ppermute | solution.py:409
  53.9 24.0 %collective-permute-start.8 = (bf16[512,1024]{1,0:T(8,128)(2,1)}, bf16[512,1024]{1,0:T(8,128)(2,1)}, u32[]{:S(2)}, u32[]{:S(2)}) collective-permute-start(bf16[512,1024]{1,0:T(8,128)(2,1)} %get-tuple-element.83.refs_1_), channel_id=1, source_target_pairs={{0,8},{1,25},{2,10},{3,27},{4,12},{5,29},{6,14},{7,31},{8,0},{9,17... | collective-permute-start | bytes 3145736 | tf_op jit(solution)/shard_map/ppermute | solution.py:409
  77.9 6.1 %collective-permute-start.12 = (bf16[512,1024]{1,0:T(8,128)(2,1)}, bf16[512,1024]{1,0:T(8,128)(2,1)S(1)}, u32[]{:S(2)}, u32[]{:S(2)}) collective-permute-start(bf16[512,1024]{1,0:T(8,128)(2,1)} %get-tuple-element.82.refs_0_), channel_id=1, source_target_pairs={{0,1},{1,0},{2,3},{3,2},{4,5},{5,4},{6,7},{7,6},{8,9},{9,8},{10,11... | collective-permute-start | bytes 3145736 | tf_op jit(solution)/shard_map/ppermute | solution.py:409
  81.5 5.5 %collective-permute-start.13 = (bf16[512,1024]{1,0:T(8,128)(2,1)}, bf16[512,1024]{1,0:T(8,128)(2,1)S(1)}, u32[]{:S(2)}, u32[]{:S(2)}) collective-permute-start(bf16[512,1024]{1,0:T(8,128)(2,1)} %get-tuple-element.83.refs_1_), channel_id=1, source_target_pairs={{0,1},{1,0},{2,3},{3,2},{4,5},{5,4},{6,7},{7,6},{8,9},{9,8},{10,11... | collective-permute-start | bytes 3145736 | tf_op jit(solution)/shard_map/ppermute | solution.py:409
  81.5 7.0 %collective-permute-start.16 = (bf16[512,1024]{1,0:T(8,128)(2,1)}, bf16[512,1024]{1,0:T(8,128)(2,1)S(1)}, u32[]{:S(2)}, u32[]{:S(2)}) collective-permute-start(bf16[512,1024]{1,0:T(8,128)(2,1)} %collective-permute-done.9.refs_4_), channel_id=1, source_target_pairs={{0,1},{1,0},{2,3},{3,2},{4,5},{5,4},{6,7},{7,6},{8,9},{9,8},{10,11... | collective-permute-start | bytes 3145736 | tf_op jit(solution)/shard_map/ppermute | solution.py:409
  82.0 14.3 %collective-permute-start.17 = (bf16[512,1024]{1,0:T(8,128)(2,1)}, bf16[512,1024]{1,0:T(8,128)(2,1)S(1)}, u32[]{:S(2)}, u32[]{:S(2)}) collective-permute-start(bf16[512,1024]{1,0:T(8,128)(2,1)} %collective-permute-done.10.refs_5_), channel_id=1, source_target_pairs={{0,1},{1,0},{2,3},{3,2},{4,5},{5,4},{6,7},{7,6},{8,9},{9,8},{10,11... | collective-permute-start | bytes 3145736 | tf_op jit(solution)/shard_map/ppermute | solution.py:409
  82.0 14.3 %collective-permute-start.14 = (bf16[512,1024]{1,0:T(8,128)(2,1)S(1)}, bf16[512,1024]{1,0:T(8,128)(2,1)S(1)}, u32[]{:S(2)}, u32[]{:S(2)}) collective-permute-start(bf16[512,1024]{1,0:T(8,128)(2,1)S(1)} %collective-permute-done.7.refs_2_), channel_id=1, source_target_pairs={{0,1},{1,0},{2,3},{3,2},{4,5},{5,4},{6,7},{7,6},{8,9},{9,8},{10,11... | collective-permute-start | bytes 3145736 | tf_op jit(solution)/shard_map/ppermute | solution.py:409
  84.0 12.3 %collective-permute-start.15 = (bf16[512,1024]{1,0:T(8,128)(2,1)}, bf16[512,1024]{1,0:T(8,128)(2,1)S(1)}, u32[]{:S(2)}, u32[]{:S(2)}) collective-permute-start(bf16[512,1024]{1,0:T(8,128)(2,1)} %collective-permute-done.8.refs_3_), channel_id=1, source_target_pairs={{0,1},{1,0},{2,3},{3,2},{4,5},{5,4},{6,7},{7,6},{8,9},{9,8},{10,11... | collective-permute-start | bytes 3145736 | tf_op jit(solution)/shard_map/ppermute | solution.py:409
  87.0 14.9 %collective-permute-start.18 = (bf16[512,1024]{1,0:T(8,128)(2,1)S(1)}, bf16[512,1024]{1,0:T(8,128)(2,1)S(1)}, u32[]{:S(2)}, u32[]{:S(2)}) collective-permute-start(bf16[512,1024]{1,0:T(8,128)(2,1)S(1)} %collective-permute-done.7.refs_2_), channel_id=1, source_target_pairs={{0,6},{1,3},{2,4},{3,1},{4,2},{5,7},{6,0},{7,5},{8,14},{9,11},{10,... | collective-permute-start | bytes 3145736 | tf_op jit(solution)/shard_map/ppermute | solution.py:409
  88.5 14.2 %collective-permute-start.19 = (bf16[512,1024]{1,0:T(8,128)(2,1)}, bf16[512,1024]{1,0:T(8,128)(2,1)S(1)}, u32[]{:S(2)}, u32[]{:S(2)}) collective-permute-start(bf16[512,1024]{1,0:T(8,128)(2,1)} %collective-permute-done.8.refs_3_), channel_id=1, source_target_pairs={{0,24},{1,9},{2,26},{3,11},{4,28},{5,13},{6,30},{7,15},{8,16},{9,1... | collective-permute-start | bytes 3145736 | tf_op jit(solution)/shard_map/ppermute | solution.py:409
  102.7 5.3 %collective-permute-start.20 = (bf16[512,1024]{1,0:T(8,128)(2,1)S(1)}, bf16[512,1024]{1,0:T(8,128)(2,1)S(1)}, u32[]{:S(2)}, u32[]{:S(2)}) collective-permute-start(bf16[512,1024]{1,0:T(8,128)(2,1)S(1)} %collective-permute-done.18.refs_0_), channel_id=1, source_target_pairs={{0,1},{1,0},{2,3},{3,2},{4,5},{5,4},{6,7},{7,6},{8,9},{9,8},{10,11... | collective-permute-start | bytes 3145736 | tf_op jit(solution)/shard_map/ppermute | solution.py:409
  105.1 3.8 %collective-permute-start.21 = (bf16[512,1024]{1,0:T(8,128)(2,1)S(1)}, bf16[512,1024]{1,0:T(8,128)(2,1)S(1)}, u32[]{:S(2)}, u32[]{:S(2)}) collective-permute-start(bf16[512,1024]{1,0:T(8,128)(2,1)S(1)} %collective-permute-done.19.refs_1_), channel_id=1, source_target_pairs={{0,1},{1,0},{2,3},{3,2},{4,5},{5,4},{6,7},{7,6},{8,9},{9,8},{10,11... | collective-permute-start | bytes 3145736 | tf_op jit(solution)/shard_map/ppermute | solution.py:409
  (5 other events, 4.7 us)

commit v3 on v2

--- a/solution.py
+++ b/solution.py
@@ -17,7 +17,7 @@
 SIDE, CORES = 4, 2
 PIECE = 128
 BLOCK = SIDE * PIECE
-EARLY = 384
+EARLY = 320
 HBM = pltpu.MemorySpace.HBM
 
 LAST = (((1,), (1,)), ((), ()))
@@ -36,20 +36,23 @@
     return [pltpu.with_memory_space_constraint(a, HBM) for a in arrays]
 
 
-def front_kernel(count_h, grad_ref, up_ref, acts_ref, down_ref, early_ref, late_ref, low_ref,
-                 send_ref, count_ref, grad_v, up_v, acts_v, down_v, low_v, message_v,
-                 send_v, in_sems, acts_sems, down_sems, out_sems, down_out_sems):
+def front_kernel(count_h, ids_h, table_h, grad_ref, up_ref, acts_ref, down_ref, early_ref, late_ref,
+                 send_ref, count_ref, ids_ref, table_ref, grad_v, up_v, acts_v, down_v, low_v,
+                 message_v, send_v, in_sems, acts_sems, down_sems, out_sems, down_out_sems):
     blocks = count_ref.shape[1]
     rows, depth = grad_v.shape
     chunks, _, wide = acts_v.shape
-    take = send_v.shape[2]
+    groups, _, take = send_v.shape
     ranks = blocks * RANK
-    grad_in = pltpu.make_async_copy(grad_ref, grad_v, in_sems.at[0])
-    up_in = pltpu.make_async_copy(up_ref, up_v, in_sems.at[1])
-    count_in = pltpu.make_async_copy(count_h, count_ref, in_sems.at[2])
-    count_in.start()
-    grad_in.start()
-    up_in.start()
+    ins = [
+        pltpu.make_async_copy(count_h, count_ref, in_sems.at[0]),
+        pltpu.make_async_copy(grad_ref, grad_v, in_sems.at[1]),
+        pltpu.make_async_copy(up_ref, up_v, in_sems.at[2]),
+        pltpu.make_async_copy(ids_h, ids_ref, in_sems.at[3]),
+        pltpu.make_async_copy(table_h, table_ref, in_sems.at[4]),
+    ]
+    for copy in ins:
+        copy.start()
     acts_in, down_in = [], []
     for i in range(chunks):
         span = pl.ds(i * wide, wide)
@@ -58,9 +61,8 @@
         down_in[i].start()
         acts_in[i].start()
     message_v[rows:, :] = jnp.zeros((RANK, depth), BF16)
-    count_in.wait()
-    grad_in.wait()
-    up_in.wait()
+    for copy in ins:
+        copy.wait()
     for b in range(blocks):
         span = slice(b * BLOCK_ROWS, (b + 1) * BLOCK_ROWS)
         at = lax.broadcasted_iota(jnp.int32, (BLOCK_ROWS, depth), 0)
@@ -95,71 +97,10 @@
         there = (pl.ds(i * fan, fan), pl.ds(0, ranks))
         outs.append(pltpu.make_async_copy(send_v.at[there], send_ref.at[there], out_sems.at[2 + i]))
         outs[-1].start()
-    low_ref[...] = low_v[...].astype(BF16)
-    for out in outs:
-        out.wait()
-
-
-def front(count, grad, up, acts, down, groups):
-    blocks = count.shape[1]
-    rows, width = acts.shape
-    depth = grad.shape[1]
-    wide = depth
-    chunks = width // wide
-    ranks = blocks * RANK
-    shape = jax.ShapeDtypeStruct
-    hbm = pl.BlockSpec(memory_space=HBM)
-    return pl.pallas_call(
-        front_kernel,
-        out_shape=(
-            shape((EARLY, depth), BF16),
-            shape((rows + RANK - EARLY + chunks * ranks, depth), BF16),
-            shape((ranks, BLOCK_ROWS), BF16),
-            shape((groups, ranks + 16, width // groups), BF16),
-        ),
-        in_specs=[hbm] * 5,
-        out_specs=(hbm, hbm, pl.BlockSpec(memory_space=pltpu.VMEM), hbm),
-        scratch_shapes=[
-            pltpu.SMEM(count.shape, jnp.int32),
-            pltpu.VMEM((rows, depth), BF16),
-            pltpu.VMEM((ranks, depth), BF16),
-            pltpu.VMEM((chunks, rows, wide), BF16),
-            pltpu.VMEM((chunks, ranks, wide), BF16),
-            pltpu.VMEM((ranks, BLOCK_ROWS), F32),
-            pltpu.VMEM((rows + RANK, depth), BF16),
-            pltpu.VMEM((groups, ranks, width // groups), BF16),
-            pltpu.SemaphoreType.DMA((3,)),
-            pltpu.SemaphoreType.DMA((chunks,)),
-            pltpu.SemaphoreType.DMA((chunks,)),
-            pltpu.SemaphoreType.DMA((chunks + 2,)),
-            pltpu.SemaphoreType.DMA((chunks,)),
-        ],
-        compiler_params=vmem(16),
-        cost_estimate=pl.CostEstimate(flops=10**10, transcendentals=0, bytes_accessed=3 * rows * width),
-        name="front",
-    )(*in_hbm(count, grad, up, acts, down))
-
-
-def finish_kernel(ids_h, table_h, early_h, late_h, low_ref, send_in, send_ref, ids_ref, table_ref, message_v,
-                  send_v, sems):
-    blocks = ids_ref.shape[1]
-    ranks = blocks * RANK
-    rows, depth = message_v.shape
-    groups, _, take = send_v.shape
-    ins = [
-        pltpu.make_async_copy(ids_h, ids_ref, sems.at[0]),
-        pltpu.make_async_copy(table_h, table_ref, sems.at[1]),
-        pltpu.make_async_copy(early_h, message_v.at[pl.ds(0, EARLY)], sems.at[2]),
-        pltpu.make_async_copy(late_h.at[pl.ds(0, rows - EARLY)], message_v.at[pl.ds(EARLY, rows - EARLY)], sems.at[4]),
-    ]
-    for copy in ins:
-        copy.start()
-    for copy in ins:
-        copy.wait()
     parts = []
     for b in range(blocks):
         span = slice(b * BLOCK_ROWS, (b + 1) * BLOCK_ROWS)
-        low = low_ref[b * RANK : (b + 1) * RANK, :]
+        low = low_v[b * RANK : (b + 1) * RANK, :].astype(BF16)
         parts.append(adapter_scale * dot(low, message_v[span, :]))
     part = jnp.concatenate(parts, axis=0)
     width = depth // groups
@@ -183,33 +124,54 @@
                 total = jnp.where(lane == g, tile, total)
             halves.append(total)
         packed = jnp.concatenate([jnp.concatenate(halves, axis=1), slots], axis=0)
-        send_v[d] = packed.astype(BF16)
-    out = pltpu.make_async_copy(send_v, send_ref.at[pl.ds(0, groups), pl.ds(ranks, 16)], sems.at[3])
-    out.start()
-    out.wait()
-
-
-def finish(ids, table, early, late, low, send):
+        send_v[d, ranks:, :] = packed.astype(BF16)
+    there = (pl.ds(0, groups), pl.ds(ranks, 16))
+    outs.append(pltpu.make_async_copy(send_v.at[there], send_ref.at[there], out_sems.at[2 + chunks]))
+    outs[-1].start()
+    for out in outs:
+        out.wait()
+
+
+def front(count, ids, table, grad, up, acts, down, groups):
+    blocks = count.shape[1]
+    rows, width = acts.shape
+    depth = grad.shape[1]
+    wide = depth
+    chunks = width // wide
+    ranks = blocks * RANK
+    shape = jax.ShapeDtypeStruct
     hbm = pl.BlockSpec(memory_space=HBM)
-    groups, _, take = send.shape
-    rows, depth = ids.shape[1] * BLOCK_ROWS, early.shape[1]
+    send = shape((groups, ranks + 16, width // groups), BF16)
     return pl.pallas_call(
-        finish_kernel,
-        out_shape=jax.ShapeDtypeStruct(send.shape, BF16),
-        in_specs=[hbm] * 4 + [pl.BlockSpec(memory_space=pltpu.VMEM), hbm],
-        out_specs=hbm,
+        front_kernel,
+        out_shape=(
+            shape((EARLY, depth), BF16),
+            shape((rows + RANK - EARLY + chunks * ranks, depth), BF16),
+            send,
+        ),
+        in_specs=[hbm] * 7,
+        out_specs=(hbm,) * 3,
         scratch_shapes=[
+            pltpu.SMEM(count.shape, jnp.int32),
             pltpu.SMEM(ids.shape, jnp.int32),
             pltpu.SMEM(table.shape, jnp.int32),
             pltpu.VMEM((rows, depth), BF16),
-            pltpu.VMEM((groups, 16, take), BF16),
+            pltpu.VMEM((ranks, depth), BF16),
+            pltpu.VMEM((chunks, rows, wide), BF16),
+            pltpu.VMEM((chunks, ranks, wide), BF16),
+            pltpu.VMEM((ranks, BLOCK_ROWS), F32),
+            pltpu.VMEM((rows + RANK, depth), BF16),
+            pltpu.VMEM(send.shape, BF16),
             pltpu.SemaphoreType.DMA((5,)),
+            pltpu.SemaphoreType.DMA((chunks,)),
+            pltpu.SemaphoreType.DMA((chunks,)),
+            pltpu.SemaphoreType.DMA((chunks + 3,)),
+            pltpu.SemaphoreType.DMA((chunks,)),
         ],
-        input_output_aliases={5: 0},
-        compiler_params=vmem(8),
-        cost_estimate=pl.CostEstimate(flops=2 * 10**9, transcendentals=0, bytes_accessed=2 * rows * depth),
-        name="finish",
-    )(*in_hbm(ids, table, early, late), low, *in_hbm(send))
+        compiler_params=vmem(18),
+        cost_estimate=pl.CostEstimate(flops=10**10, transcendentals=0, bytes_accessed=3 * rows * width),
+        name="front",
+    )(*in_hbm(count, ids, table, grad, up, acts, down))
 
 
 def join_kernel(counts, spots_ref, *refs):
@@ -223,7 +185,7 @@
             i += 1
 
 
-def join(spots, *groups, cost):
+def join(spots, *groups):
     counts = tuple(len(g) for g in groups)
     in_vmem = pl.BlockSpec(memory_space=pltpu.VMEM)
     return pl.pallas_call(
@@ -232,7 +194,7 @@
         in_specs=[pl.BlockSpec(memory_space=pltpu.SMEM)] + [in_vmem] * sum(counts),
         out_specs=[in_vmem] * len(groups),
         compiler_params=vmem(4),
-        cost_estimate=pl.CostEstimate(flops=cost, transcendentals=0, bytes_accessed=1 << 21),
+        cost_estimate=pl.CostEstimate(flops=10**6, transcendentals=0, bytes_accessed=1 << 21),
         name="join",
     )(spots, *[v for g in groups for v in g])
 
@@ -383,7 +345,7 @@
         input_output_aliases={} if before is None else {len(operands) - 1: 0},
         compiler_params=vmem(12),
         cost_estimate=pl.CostEstimate(
-            flops=3 * rows * depth * columns, transcendentals=0, bytes_accessed=2 * columns * (depth + rows)
+            flops=10**6, transcendentals=0, bytes_accessed=10**6
         ),
         name=name,
     )(*operands)
@@ -471,7 +433,10 @@
         frozen_value_weight[0], half + ((x * CORES + core) * SIDE + spot(z, core)) * PIECE, PIECE, 0
     )
     a0, b0 = hop(piece_a, back), hop(piece_b, back)
-    early, late, low, send = front(token_row_count, output_gradient[0], up, acts[0], down, groups)
+    early, late, send = front(
+        token_row_count, block_adapter_index, adapter_slot_table,
+        output_gradient[0], up, acts[0], down, groups,
+    )
     spot_a, spot_b = spot(x, core), spot(z, core)
     halves = jnp.stack([spot_a % 2, 1 - spot_a % 2, spot_b % 2, 1 - spot_b % 2]).astype(jnp.int32)
     wholes = jnp.stack([spot_a // 2, 1 - spot_a // 2, spot_b // 2, 1 - spot_b // 2]).astype(jnp.int32)
@@ -479,27 +444,26 @@
     for c in (core, 1 - core):
         starts += places(z, c) + [half + s for s in places(x, c)]
     starts = jnp.stack(starts).astype(jnp.int32)
-    a0, b0, send, early, late, low, halves, wholes, starts = tie(
-        a0, b0, send, early, late, low, halves, wholes, starts
+    a0, b0, send, early, late, halves, wholes, starts = tie(
+        a0, b0, send, early, late, halves, wholes, starts
     )
 
     a1, b1 = moved(a0, x_near), moved(b0, z_near)
-    send = finish(block_adapter_index, adapter_slot_table, early, late, low, send)
     early = hop(early, back)
+    a0, b0, a1, b1, send, late = tie(a0, b0, a1, b1, send, late)
+
     got = lax.all_to_all(send, "dp", split_axis=0, concat_axis=0, tiled=True)
-    a0, b0, a1, b1, send, late = tie(a0, b0, a1, b1, send, late)
-
-    ap, bp = join(halves, (a0, a1), (b0, b1), cost=10**6)
+    ap, bp = join(halves, (a0, a1), (b0, b1))
     aq, bq = moved(ap, x_far), moved(bp, z_far)
-    aq, bq, ap, bp, early, late = tie(aq, bq, ap, bp, early, late)
+    aq, bq, early, late = tie(aq, bq, early, late)
 
     late = hop(late, back)
-    a, b = join(wholes, (ap, aq), (bp, bq), cost=10**6)
+    a, b = join(wholes, (ap, aq), (bp, bq))
     a_near, b_near = moved(a, z_near), moved(b, x_near)
     a_far, b_far = moved(a, z_far), moved(b, x_far)
     total_a, total_b = collect(got, adapters, blocks, depth)
-    a, b, a_near, b_near, a_far, b_far, late, total_a, total_b = tie(
-        a, b, a_near, b_near, a_far, b_far, late, total_a, total_b
+    a, b, a_near, b_near, a_far, b_far, total_a, total_b = tie(
+        a, b, a_near, b_near, a_far, b_far, total_a, total_b
     )
 
     def pair(a, b, step, mine=True):
@@ -510,14 +474,21 @@
         return pair(moved(a, other_core), moved(b, other_core), step, False)
 
     a_last, b_last = moved(a_near, z_far), moved(b_near, x_far)
-    shared = (starts, *unpack(early, late, rows, blocks * RANK))
+    message, low, down = unpack(early, late, rows, blocks * RANK)
+    message, a, b, a_near = tie(message, a, b, a_near)
+    shared = (starts, message, low, down)
     mine = pair(a, b, 0) + pair(a_near, b_near, 1) + pair(a_far, b_far, 2)
-    theirs = others(a, b, 0) + others(a_near, b_near, 1) + others(a_far, b_far, 2)
     received = product(mine, *shared, None, "product_mine")
-    received = product(theirs, *shared, received, "product_theirs")
+    a_other, b_other, a_near_other = [moved(v, other_core) for v in (a, b, a_near)]
+    received, a_other, b_other, a_near_other, b_near, a_far, b_far = tie(
+        received, a_other, b_other, a_near_other, b_near, a_far, b_far
+    )
+    first = pair(a_other, b_other, 0, False) + [(a_near_other, 1 + 2 * SIDE)]
+    second = [(moved(b_near, other_core), 1 + 3 * SIDE)] + others(a_far, b_far, 2)
+    received = product(first, *shared, received, "product_first")
     received, a_last, b_last = tie(received, a_last, b_last)
     theirs = others(a_last, b_last, 3)
-    received = product(pair(a_last, b_last, 3), *shared, received, "product_last")
+    received = product(second + pair(a_last, b_last, 3), *shared, received, "product_second")
     received = product(theirs, *shared, received, "product_end")
     return received[None], total_a[None], jnp.transpose(total_b, (2, 0, 1))[None]
 

time: 114 us -> 108 us (0.947)
  waiting for transfers between devices: 33.2 us -> 27 us
  starting transfers between devices: 31.4 us -> 35.9 us
  Pallas kernels: 39.2 us -> 36.8 us
    ppermute x18, waiting for transfers between devices: 22.5 us -> 15.4 us  [moved(): return lax.ppermute(array, 'dp', route)]
    all_to_all x1, waiting for transfers between devices: 2.87 us -> 6.75 us  [body(): got = lax.all_to_all(send, 'dp', split_axis=0, concat_axis=0, tiled=True)]
    ppermute x18, starting transfers between devices: 17.4 us -> 21 us  [moved(): return lax.ppermute(array, 'dp', route)]
    ppermute x4, waiting for transfers between devices: 7.85 us -> 4.87 us  [hop(): return lax.ppermute(x, 'pipe', route)]
    pallas_call x1 -> x0, Pallas kernels: 2.35 us -> none  [finish(): pl.pallas_call(finish_kernel, out_shape=jax.ShapeDtypeStruct(send.shape,...]
    unnamed x12 -> x10, local copies, waits for them, and re-layouts: 5.79 us -> 4.76 us
  transfers between devices with their start and end apart: 23 -> 23, of which waited for: 10 -> 7; matrix products, arithmetic and copies ran while one was open for 0% -> 0% of each run, Pallas kernels for 32% -> 32%
where the time goes in v3:
time: 108 us; the launch traced here: 107 us
  Pallas kernels  36.8 us (34%)
  starting transfers between devices  35.9 us (33%)
  waiting for transfers between devices  27 us (25%)
  local copies, waits for them, and re-layouts  5.92 us (5%)
  between operations  1.09 us (1%)
    ppermute x18, starting transfers between devices, moved(): return lax.ppermute(array, 'dp', route)  21 us
    pallas_call x4, Pallas kernels, product(): pl.pallas_call(functools.partial(product_kernel, tuple((b[1] for b in blo...  18.9 us
    ppermute x18, waiting for transfers between devices, moved(): return lax.ppermute(array, 'dp', route)  15.4 us
    pallas_call x1, Pallas kernels, front(): pl.pallas_call(front_kernel, out_shape=(shape((EARLY, depth), BF16), shap...  10.5 us
    all_to_all x1, starting transfers between devices, body(): got = lax.all_to_all(send, 'dp', split_axis=0, concat_axis=0, tiled=True)  9.71 us
    all_to_all x1, waiting for transfers between devices, body(): got = lax.all_to_all(send, 'dp', split_axis=0, concat_axis=0, tiled=True)  6.75 us
    ppermute x4, starting transfers between devices, hop(): return lax.ppermute(x, 'pipe', route)  5.14 us
    ppermute x4, waiting for transfers between devices, hop(): return lax.ppermute(x, 'pipe', route)  4.87 us
  transfers between devices with their start and end apart: 23, of which 7 were waited for; matrix products, arithmetic and copies ran while one was open for 0% of the time, Pallas kernels for 32%

profile of v3, /device:TPU:1, one launch (start us, length us, event | category | flops | bytes accessed | tf_op | source)
XLA Modules:
  0.0 106.9 jit_solution(10627171758932406308)
XLA Ops:
  0.7 1.1 %dynamic-slice_bitcast_fusion = (bf16[128,1024]{1,0:T(8,128)(2,1)S(1)}, bf16[128,1024]{1,0:T(8,128)(2,1)S(1)}) fusion(bf16[1,8192,1024]{2,1,0:T(8,128)(2,1)} %param.10, s32[]{:T(128)S(6)} %select_n.163, s32[]{:T(128)S(6)} %select_n.161), kind=kLoop, calls=%fused_computation | loop fusion | bytes 1048584 | tf_op jit(solution)/shard_map/dynamic_slice | solution.py:432
  1.8 1.3 %collective-permute-start = (bf16[128,1024]{1,0:T(8,128)(2,1)S(1)}, bf16[128,1024]{1,0:T(8,128)(2,1)S(1)}, u32[]{:S(2)}, u32[]{:S(2)}) collective-permute-start(bf16[128,1024]{1,0:T(8,128)(2,1)S(1)} %get-tuple-element.108), channel_id=1, source_target_pairs={{32,0},{64,32},{96,64},{33,1},{65,33},{97,65},{34,2},{66,34},{98,6... | collective-permute-start | bytes 786440 | tf_op jit(solution)/shard_map/ppermute | solution.py:400
  3.1 1.3 %collective-permute-start.1 = (bf16[128,1024]{1,0:T(8,128)(2,1)S(1)}, bf16[128,1024]{1,0:T(8,128)(2,1)S(1)}, u32[]{:S(2)}, u32[]{:S(2)}) collective-permute-start(bf16[128,1024]{1,0:T(8,128)(2,1)S(1)} %get-tuple-element.107), channel_id=1, source_target_pairs={{32,0},{64,32},{96,64},{33,1},{65,33},{97,65},{34,2},{66,34},{98,6... | collective-permute-start | bytes 786440 | tf_op jit(solution)/shard_map/ppermute | solution.py:400
  4.4 10.5 %front.1 = (bf16[320,1024]{1,0:T(8,128)(2,1)}, bf16[720,1024]{1,0:T(8,128)(2,1)S(1)}, bf16[32,80,256]{2,1,0:T(8,128)(2,1)}) custom-call(s32[1,4]{1,0:T(1,128)} %count_h.1, s32[1,4]{1,0:T(1,128)} %ids_h.1, s32[64]{0:T(128)} %table_h.1, bf16[512,1024]{1,0:T(8,128)(2,1)} %bitcast.39, bf16[64,1024]{1,0:T(8,128)(2,1)} %bitcast.41, bf16[512,8192]{1,0:T(8,128)(2,1)} %bitcast.38, ...), custom_call_target="tpu_custom_call" | custom-call | flops 10000000000 | bytes 12582912 | tf_op jit(solution)/shard_map/front/pallas_call | solution.py:145
  14.9 1.1 %copy-done.4 = bf16[720,1024]{1,0:T(8,128)(2,1)} copy-done((bf16[720,1024]{1,0:T(8,128)(2,1)}, bf16[720,1024]{1,0:T(8,128)(2,1)S(1)}, u32[]{:S(2)}) %copy-start.4) | copy-done | bytes 1474584
  17.0 2.8 %collective-permute-start.2 = (bf16[128,1024]{1,0:T(8,128)(2,1)S(1)}, bf16[128,1024]{1,0:T(8,128)(2,1)S(1)}, u32[]{:S(2)}, u32[]{:S(2)}) collective-permute-start(bf16[128,1024]{1,0:T(8,128)(2,1)S(1)} %collective-permute-done.refs_0_), channel_id=1, source_target_pairs={{0,8},{1,25},{2,10},{3,27},{4,12},{5,29},{6,14},{7,31},{8,0},{9,17... | collective-permute-start | bytes 786440 | tf_op jit(solution)/shard_map/ppermute | solution.py:371
  19.8 3.8 %collective-permute-start.3 = (bf16[128,1024]{1,0:T(8,128)(2,1)S(1)}, bf16[128,1024]{1,0:T(8,128)(2,1)S(1)}, u32[]{:S(2)}, u32[]{:S(2)}) collective-permute-start(bf16[128,1024]{1,0:T(8,128)(2,1)S(1)} %collective-permute-done.1.refs_2_), channel_id=1, source_target_pairs={{0,2},{1,7},{2,0},{3,5},{4,6},{5,3},{6,4},{7,1},{8,10},{9,15},{10,... | collective-permute-start | bytes 786440 | tf_op jit(solution)/shard_map/ppermute | solution.py:371
  23.5 1.3 %collective-permute-start.6 = (bf16[320,1024]{1,0:T(8,128)(2,1)}, bf16[320,1024]{1,0:T(8,128)(2,1)S(1)}, u32[]{:S(2)}, u32[]{:S(2)}) collective-permute-start(bf16[320,1024]{1,0:T(8,128)(2,1)} %get-tuple-element.70), channel_id=1, source_target_pairs={{32,0},{64,32},{96,64},{33,1},{65,33},{97,65},{34,2},{66,34},{98,6... | collective-permute-start | bytes 1966088 | tf_op jit(solution)/shard_map/ppermute | solution.py:400
  24.8 2.5 %collective-permute-done.3.refs_3_ = bf16[128,1024]{1,0:T(8,128)(2,1)S(1)} collective-permute-done((bf16[128,1024]{1,0:T(8,128)(2,1)S(1)}, bf16[128,1024]{1,0:T(8,128)(2,1)S(1)}, u32[]{:S(2)}, u32[]{:S(2)}) %collective-permute-start.3) | collective-permute-done | bytes 262176 | tf_op jit(solution)/shard_map/ppermute | solution.py:371
  28.1 9.7 %all-to-all-start = ((bf16[32,80,256]{2,1,0:T(8,128)(2,1)}), bf16[32,80,256]{2,1,0:T(8,128)(2,1)}, u32[]{:S(2)}, u32[]{:S(2)}) async-start(bf16[32,80,256]{2,1,0:T(8,128)(2,1)} %get-tuple-element.80), calls=%async_computation | async-start | bytes 2621440 | tf_op jit(solution)/shard_map/all_to_all | solution.py:455
  37.8 4.0 %collective-permute-done.6.early_ref = bf16[320,1024]{1,0:T(8,128)(2,1)S(1)} collective-permute-done((bf16[320,1024]{1,0:T(8,128)(2,1)}, bf16[320,1024]{1,0:T(8,128)(2,1)S(1)}, u32[]{:S(2)}, u32[]{:S(2)}) %collective-permute-start.6) | collective-permute-done | bytes 655392 | tf_op jit(solution)/shard_map/ppermute | solution.py:400
  43.4 1.3 %collective-permute-start.7 = (bf16[720,1024]{1,0:T(8,128)(2,1)}, bf16[720,1024]{1,0:T(8,128)(2,1)S(1)}, u32[]{:S(2)}, u32[]{:S(2)}) collective-permute-start(bf16[720,1024]{1,0:T(8,128)(2,1)} %copy-done.4), channel_id=1, source_target_pairs={{32,0},{64,32},{96,64},{33,1},{65,33},{97,65},{34,2},{66,34},{98,6... | collective-permute-start | bytes 4423688 | tf_op jit(solution)/shard_map/ppermute | solution.py:400
  46.8 2.0 %join.3 = (bf16[512,1024]{1,0:T(8,128)(2,1)}, bf16[512,1024]{1,0:T(8,128)(2,1)}) custom-call(s32[4]{0:T(128)S(1)} %get-tuple-element.75.spots_ref, bf16[256,1024]{1,0:T(8,128)(2,1)S(1)} %get-tuple-element.68.refs_0_, bf16[256,1024]{1,0:T(8,128)(2,1)S(1)} %copy-done.1, bf16[256,1024]{1,0:T(8,128)(2,1)S(1)} %get-tuple-element.69.refs_2_, ...), custom_call_target="tpu_custom_call" | custom-call | flops 1000000 | bytes 2097152 | tf_op jit(solution)/shard_map/join/pallas_call | solution.py:191
  51.1 6.8 %all-to-all-done.got_h = bf16[32,80,256]{2,1,0:T(8,128)(2,1)} async-done(((bf16[32,80,256]{2,1,0:T(8,128)(2,1)}), bf16[32,80,256]{2,1,0:T(8,128)(2,1)}, u32[]{:S(2)}, u32[]{:S(2)}) %all-to-all-start) | async-done | bytes 1310752 | tf_op jit(solution)/shard_map/all_to_all | solution.py:455
  57.8 4.6 %collect.1 = (bf16[64,16,256]{2,1,0:T(8,128)(2,1)}, bf16[16,32,64]{2,1,0:T(8,128)(2,1)}) custom-call(bf16[32,80,256]{2,1,0:T(8,128)(2,1)} %all-to-all-done.got_h), custom_call_target="tpu_custom_call" | custom-call | flops 4000000000 | bytes 2621440 | tf_op jit(solution)/shard_map/collect/pallas_call | solution.py:257
  62.4 6.9 %collective-permute-done.10.refs_4_ = bf16[512,1024]{1,0:T(8,128)(2,1)S(1)} collective-permute-done((bf16[512,1024]{1,0:T(8,128)(2,1)}, bf16[512,1024]{1,0:T(8,128)(2,1)S(1)}, u32[]{:S(2)}, u32[]{:S(2)}) %collective-permute-start.10) | collective-permute-done | bytes 1048608 | tf_op jit(solution)/shard_map/ppermute | solution.py:371
  69.3 6.0 %collective-permute-done.8.refs_2_ = bf16[512,1024]{1,0:T(8,128)(2,1)} collective-permute-done((bf16[512,1024]{1,0:T(8,128)(2,1)}, bf16[512,1024]{1,0:T(8,128)(2,1)}, u32[]{:S(2)}, u32[]{:S(2)}) %collective-permute-start.8) | collective-permute-done | bytes 1048608 | tf_op jit(solution)/shard_map/ppermute | solution.py:371
  75.5 5.0 %collective-permute-start.12 = (bf16[512,1024]{1,0:T(8,128)(2,1)}, bf16[512,1024]{1,0:T(8,128)(2,1)S(1)}, u32[]{:S(2)}, u32[]{:S(2)}) collective-permute-start(bf16[512,1024]{1,0:T(8,128)(2,1)} %get-tuple-element.89.refs_0_), channel_id=1, source_target_pairs={{0,1},{1,0},{2,3},{3,2},{4,5},{5,4},{6,7},{7,6},{8,9},{9,8},{10,11... | collective-permute-start | bytes 3145736 | tf_op jit(solution)/shard_map/ppermute | solution.py:371
  81.1 7.6 %product_mine.1.refs_3_ = bf16[512,8192]{1,0:T(8,128)(2,1)} custom-call(s32[16]{0:T(128)S(1)} %stack.107.starts_ref, bf16[512,1024]{1,0:T(8,128)(2,1)S(1)} %get-tuple-element.86.message_ref, bf16[512,64]{1,0:T(8,128)(2,1)S(1)} %get-tuple-element.87.low_ref, bf16[512,1024]{1,0:T(8,128)(2,1)S(1)} %get-tuple-element.88.down_ref, ...), custom_call_target="tpu_custom_call" | custom-call | flops 1000000 | bytes 1000000 | tf_op jit(solution)/shard_map/product_mine/pallas_call | solution.py:339
  88.7 2.4 %collective-permute-start.19 = (bf16[512,1024]{1,0:T(8,128)(2,1)}, bf16[512,1024]{1,0:T(8,128)(2,1)S(1)}, u32[]{:S(2)}, u32[]{:S(2)}) collective-permute-start(bf16[512,1024]{1,0:T(8,128)(2,1)} %collective-permute-done.9.refs_3_), channel_id=1, source_target_pairs={{0,1},{1,0},{2,3},{3,2},{4,5},{5,4},{6,7},{7,6},{8,9},{9,8},{10,11... | collective-permute-start | bytes 3145736 | tf_op jit(solution)/shard_map/ppermute | solution.py:371
  91.6 3.5 %product_first.1.refs_5_ = bf16[512,8192]{1,0:T(8,128)(2,1)} custom-call(s32[16]{0:T(128)S(1)} %stack.107.starts_ref, bf16[512,1024]{1,0:T(8,128)(2,1)S(1)} %get-tuple-element.86.message_ref, bf16[512,64]{1,0:T(8,128)(2,1)S(1)} %get-tuple-element.87.low_ref, bf16[512,1024]{1,0:T(8,128)(2,1)S(1)} %get-tuple-element.88.down_ref, ...), custom_call_target="tpu_custom_call", output_to_operand_aliasing={{}: (7, {})} | custom-call | flops 1000000 | bytes 1000000 | tf_op jit(solution)/shard_map/product_first/pallas_call | solution.py:339
  95.2 3.6 %collective-permute-start.17 = (bf16[512,1024]{1,0:T(8,128)(2,1)S(1)}, bf16[512,1024]{1,0:T(8,128)(2,1)S(1)}, u32[]{:S(2)}, u32[]{:S(2)}) collective-permute-start(bf16[512,1024]{1,0:T(8,128)(2,1)S(1)} %collective-permute-done.15.refs_3_), channel_id=1, source_target_pairs={{0,1},{1,0},{2,3},{3,2},{4,5},{5,4},{6,7},{7,6},{8,9},{9,8},{10,11... | collective-permute-start | bytes 3145736 | tf_op jit(solution)/shard_map/ppermute | solution.py:371
  98.9 4.9 %product_second.1.refs_2_ = bf16[512,8192]{1,0:T(8,128)(2,1)} custom-call(s32[16]{0:T(128)S(1)} %stack.107.starts_ref, bf16[512,1024]{1,0:T(8,128)(2,1)S(1)} %get-tuple-element.86.message_ref, bf16[512,64]{1,0:T(8,128)(2,1)S(1)} %get-tuple-element.87.low_ref, bf16[512,1024]{1,0:T(8,128)(2,1)S(1)} %get-tuple-element.88.down_ref, ...), custom_call_target="tpu_custom_call", output_to_operand_aliasing={{}: (9, {})} | custom-call | flops 1000000 | bytes 1000000 | tf_op jit(solution)/shard_map/product_second/pallas_call | solution.py:339
  103.8 2.9 %product_end.1 = bf16[512,8192]{1,0:T(8,128)(2,1)} custom-call(s32[16]{0:T(128)S(1)} %stack.107.starts_ref, bf16[512,1024]{1,0:T(8,128)(2,1)S(1)} %get-tuple-element.86.message_ref, bf16[512,64]{1,0:T(8,128)(2,1)S(1)} %get-tuple-element.87.low_ref, bf16[512,1024]{1,0:T(8,128)(2,1)S(1)} %get-tuple-element.88.down_ref, ...), custom_call_target="tpu_custom_call", output_to_operand_aliasing={{}: (6, {})} | custom-call | flops 1000000 | bytes 1000000 | tf_op jit(solution)/shard_map/product_end/pallas_call | solution.py:339
  (44 shorter events, 9.1 us)
Async XLA Ops:
  1.8 14.4 %collective-permute-start = (bf16[128,1024]{1,0:T(8,128)(2,1)S(1)}, bf16[128,1024]{1,0:T(8,128)(2,1)S(1)}, u32[]{:S(2)}, u32[]{:S(2)}) collective-permute-start(bf16[128,1024]{1,0:T(8,128)(2,1)S(1)} %get-tuple-element.108), channel_id=1, source_target_pairs={{32,0},{64,32},{96,64},{33,1},{65,33},{97,65},{34,2},{66,34},{98,6... | collective-permute-start | bytes 786440 | tf_op jit(solution)/shard_map/ppermute | solution.py:400
  3.1 13.9 %collective-permute-start.1 = (bf16[128,1024]{1,0:T(8,128)(2,1)S(1)}, bf16[128,1024]{1,0:T(8,128)(2,1)S(1)}, u32[]{:S(2)}, u32[]{:S(2)}) collective-permute-start(bf16[128,1024]{1,0:T(8,128)(2,1)S(1)} %get-tuple-element.107), channel_id=1, source_target_pairs={{32,0},{64,32},{96,64},{33,1},{65,33},{97,65},{34,2},{66,34},{98,6... | collective-permute-start | bytes 786440 | tf_op jit(solution)/shard_map/ppermute | solution.py:400
  14.9 1.1 %copy-start.4 = (bf16[720,1024]{1,0:T(8,128)(2,1)}, bf16[720,1024]{1,0:T(8,128)(2,1)S(1)}, u32[]{:S(2)}) copy-start(bf16[720,1024]{1,0:T(8,128)(2,1)S(1)} %get-tuple-element.73) | copy-start | bytes 4423684
  17.0 7.8 %collective-permute-start.2 = (bf16[128,1024]{1,0:T(8,128)(2,1)S(1)}, bf16[128,1024]{1,0:T(8,128)(2,1)S(1)}, u32[]{:S(2)}, u32[]{:S(2)}) collective-permute-start(bf16[128,1024]{1,0:T(8,128)(2,1)S(1)} %collective-permute-done.refs_0_), channel_id=1, source_target_pairs={{0,8},{1,25},{2,10},{3,27},{4,12},{5,29},{6,14},{7,31},{8,0},{9,17... | collective-permute-start | bytes 786440 | tf_op jit(solution)/shard_map/ppermute | solution.py:371
  19.8 7.5 %collective-permute-start.3 = (bf16[128,1024]{1,0:T(8,128)(2,1)S(1)}, bf16[128,1024]{1,0:T(8,128)(2,1)S(1)}, u32[]{:S(2)}, u32[]{:S(2)}) collective-permute-start(bf16[128,1024]{1,0:T(8,128)(2,1)S(1)} %collective-permute-done.1.refs_2_), channel_id=1, source_target_pairs={{0,2},{1,7},{2,0},{3,5},{4,6},{5,3},{6,4},{7,1},{8,10},{9,15},{10,... | collective-permute-start | bytes 786440 | tf_op jit(solution)/shard_map/ppermute | solution.py:371
  23.5 18.3 %collective-permute-start.6 = (bf16[320,1024]{1,0:T(8,128)(2,1)}, bf16[320,1024]{1,0:T(8,128)(2,1)S(1)}, u32[]{:S(2)}, u32[]{:S(2)}) collective-permute-start(bf16[320,1024]{1,0:T(8,128)(2,1)} %get-tuple-element.70), channel_id=1, source_target_pairs={{32,0},{64,32},{96,64},{33,1},{65,33},{97,65},{34,2},{66,34},{98,6... | collective-permute-start | bytes 1966088 | tf_op jit(solution)/shard_map/ppermute | solution.py:400
  27.9 13.9 %collective-permute-start.4 = (bf16[256,1024]{1,0:T(8,128)(2,1)S(1)}, bf16[256,1024]{1,0:T(8,128)(2,1)S(1)}, u32[]{:S(2)}, u32[]{:S(2)}) collective-permute-start(bf16[256,1024]{1,0:T(8,128)(2,1)S(1)} %get-tuple-element.68.refs_0_), channel_id=1, source_target_pairs={{0,24},{1,9},{2,26},{3,11},{4,28},{5,13},{6,30},{7,15},{8,16},{9,1... | collective-permute-start | bytes 1572872 | tf_op jit(solution)/shard_map/ppermute | solution.py:371
  28.0 14.6 %collective-permute-start.5 = (bf16[256,1024]{1,0:T(8,128)(2,1)S(1)}, bf16[256,1024]{1,0:T(8,128)(2,1)S(1)}, u32[]{:S(2)}, u32[]{:S(2)}) collective-permute-start(bf16[256,1024]{1,0:T(8,128)(2,1)S(1)} %get-tuple-element.69.refs_2_), channel_id=1, source_target_pairs={{0,6},{1,3},{2,4},{3,1},{4,2},{5,7},{6,0},{7,5},{8,14},{9,11},{10,... | collective-permute-start | bytes 1572872 | tf_op jit(solution)/shard_map/ppermute | solution.py:371
  28.1 29.7 %all-to-all-start = ((bf16[32,80,256]{2,1,0:T(8,128)(2,1)}), bf16[32,80,256]{2,1,0:T(8,128)(2,1)}, u32[]{:S(2)}, u32[]{:S(2)}) async-start(bf16[32,80,256]{2,1,0:T(8,128)(2,1)} %get-tuple-element.80), calls=%async_computation | async-start | bytes 2621440 | tf_op jit(solution)/shard_map/all_to_all | solution.py:455
  43.4 31.9 %collective-permute-start.7 = (bf16[720,1024]{1,0:T(8,128)(2,1)}, bf16[720,1024]{1,0:T(8,128)(2,1)S(1)}, u32[]{:S(2)}, u32[]{:S(2)}) collective-permute-start(bf16[720,1024]{1,0:T(8,128)(2,1)} %copy-done.4), channel_id=1, source_target_pairs={{32,0},{64,32},{96,64},{33,1},{65,33},{97,65},{34,2},{66,34},{98,6... | collective-permute-start | bytes 4423688 | tf_op jit(solution)/shard_map/ppermute | solution.py:400
  48.8 20.5 %collective-permute-start.10 = (bf16[512,1024]{1,0:T(8,128)(2,1)}, bf16[512,1024]{1,0:T(8,128)(2,1)S(1)}, u32[]{:S(2)}, u32[]{:S(2)}) collective-permute-start(bf16[512,1024]{1,0:T(8,128)(2,1)} %get-tuple-element.89.refs_0_), channel_id=1, source_target_pairs={{0,6},{1,3},{2,4},{3,1},{4,2},{5,7},{6,0},{7,5},{8,14},{9,11},{10,... | collective-permute-start | bytes 3145736 | tf_op jit(solution)/shard_map/ppermute | solution.py:371
  48.8 20.5 %collective-permute-start.11 = (bf16[512,1024]{1,0:T(8,128)(2,1)}, bf16[512,1024]{1,0:T(8,128)(2,1)}, u32[]{:S(2)}, u32[]{:S(2)}) collective-permute-start(bf16[512,1024]{1,0:T(8,128)(2,1)} %get-tuple-element.90.refs_1_), channel_id=1, source_target_pairs={{0,24},{1,9},{2,26},{3,11},{4,28},{5,13},{6,30},{7,15},{8,16},{9,1... | collective-permute-start | bytes 3145736 | tf_op jit(solution)/shard_map/ppermute | solution.py:371
  49.1 26.2 %collective-permute-start.8 = (bf16[512,1024]{1,0:T(8,128)(2,1)}, bf16[512,1024]{1,0:T(8,128)(2,1)}, u32[]{:S(2)}, u32[]{:S(2)}) collective-permute-start(bf16[512,1024]{1,0:T(8,128)(2,1)} %get-tuple-element.89.refs_0_), channel_id=1, source_target_pairs={{0,2},{1,7},{2,0},{3,5},{4,6},{5,3},{6,4},{7,1},{8,10},{9,15},{10,... | collective-permute-start | bytes 3145736 | tf_op jit(solution)/shard_map/ppermute | solution.py:371
  50.0 25.3 %collective-permute-start.9 = (bf16[512,1024]{1,0:T(8,128)(2,1)}, bf16[512,1024]{1,0:T(8,128)(2,1)}, u32[]{:S(2)}, u32[]{:S(2)}) collective-permute-start(bf16[512,1024]{1,0:T(8,128)(2,1)} %get-tuple-element.90.refs_1_), channel_id=1, source_target_pairs={{0,8},{1,25},{2,10},{3,27},{4,12},{5,29},{6,14},{7,31},{8,0},{9,17... | collective-permute-start | bytes 3145736 | tf_op jit(solution)/shard_map/ppermute | solution.py:371
  75.5 13.1 %collective-permute-start.12 = (bf16[512,1024]{1,0:T(8,128)(2,1)}, bf16[512,1024]{1,0:T(8,128)(2,1)S(1)}, u32[]{:S(2)}, u32[]{:S(2)}) collective-permute-start(bf16[512,1024]{1,0:T(8,128)(2,1)} %get-tuple-element.89.refs_0_), channel_id=1, source_target_pairs={{0,1},{1,0},{2,3},{3,2},{4,5},{5,4},{6,7},{7,6},{8,9},{9,8},{10,11... | collective-permute-start | bytes 3145736 | tf_op jit(solution)/shard_map/ppermute | solution.py:371
  80.5 8.1 %collective-permute-start.13 = (bf16[512,1024]{1,0:T(8,128)(2,1)}, bf16[512,1024]{1,0:T(8,128)(2,1)S(1)}, u32[]{:S(2)}, u32[]{:S(2)}) collective-permute-start(bf16[512,1024]{1,0:T(8,128)(2,1)} %get-tuple-element.90.refs_1_), channel_id=1, source_target_pairs={{0,1},{1,0},{2,3},{3,2},{4,5},{5,4},{6,7},{7,6},{8,9},{9,8},{10,11... | collective-permute-start | bytes 3145736 | tf_op jit(solution)/shard_map/ppermute | solution.py:371
  80.6 8.1 %collective-permute-start.14 = (bf16[512,1024]{1,0:T(8,128)(2,1)}, bf16[512,1024]{1,0:T(8,128)(2,1)S(1)}, u32[]{:S(2)}, u32[]{:S(2)}) collective-permute-start(bf16[512,1024]{1,0:T(8,128)(2,1)} %collective-permute-done.8.refs_2_), channel_id=1, source_target_pairs={{0,1},{1,0},{2,3},{3,2},{4,5},{5,4},{6,7},{7,6},{8,9},{9,8},{10,11... | collective-permute-start | bytes 3145736 | tf_op jit(solution)/shard_map/ppermute | solution.py:371
  81.0 14.2 %collective-permute-start.15 = (bf16[512,1024]{1,0:T(8,128)(2,1)}, bf16[512,1024]{1,0:T(8,128)(2,1)S(1)}, u32[]{:S(2)}, u32[]{:S(2)}) collective-permute-start(bf16[512,1024]{1,0:T(8,128)(2,1)} %collective-permute-done.8.refs_2_), channel_id=1, source_target_pairs={{0,6},{1,3},{2,4},{3,1},{4,2},{5,7},{6,0},{7,5},{8,14},{9,11},{10,... | collective-permute-start | bytes 3145736 | tf_op jit(solution)/shard_map/ppermute | solution.py:371
  81.1 14.2 %collective-permute-start.16 = (bf16[512,1024]{1,0:T(8,128)(2,1)}, bf16[512,1024]{1,0:T(8,128)(2,1)S(1)}, u32[]{:S(2)}, u32[]{:S(2)}) collective-permute-start(bf16[512,1024]{1,0:T(8,128)(2,1)} %collective-permute-done.9.refs_3_), channel_id=1, source_target_pairs={{0,24},{1,9},{2,26},{3,11},{4,28},{5,13},{6,30},{7,15},{8,16},{9,1... | collective-permute-start | bytes 3145736 | tf_op jit(solution)/shard_map/ppermute | solution.py:371
  88.7 10.2 %collective-permute-start.19 = (bf16[512,1024]{1,0:T(8,128)(2,1)}, bf16[512,1024]{1,0:T(8,128)(2,1)S(1)}, u32[]{:S(2)}, u32[]{:S(2)}) collective-permute-start(bf16[512,1024]{1,0:T(8,128)(2,1)} %collective-permute-done.9.refs_3_), channel_id=1, source_target_pairs={{0,1},{1,0},{2,3},{3,2},{4,5},{5,4},{6,7},{7,6},{8,9},{9,8},{10,11... | collective-permute-start | bytes 3145736 | tf_op jit(solution)/shard_map/ppermute | solution.py:371
  91.1 7.8 %collective-permute-start.20 = (bf16[512,1024]{1,0:T(8,128)(2,1)S(1)}, bf16[512,1024]{1,0:T(8,128)(2,1)S(1)}, u32[]{:S(2)}, u32[]{:S(2)}) collective-permute-start(bf16[512,1024]{1,0:T(8,128)(2,1)S(1)} %collective-permute-done.10.refs_4_), channel_id=1, source_target_pairs={{0,1},{1,0},{2,3},{3,2},{4,5},{5,4},{6,7},{7,6},{8,9},{9,8},{10,11... | collective-permute-start | bytes 3145736 | tf_op jit(solution)/shard_map/ppermute | solution.py:371
  91.2 7.7 %collective-permute-start.21 = (bf16[512,1024]{1,0:T(8,128)(2,1)}, bf16[512,1024]{1,0:T(8,128)(2,1)S(1)}, u32[]{:S(2)}, u32[]{:S(2)}) collective-permute-start(bf16[512,1024]{1,0:T(8,128)(2,1)} %collective-permute-done.11.refs_5_), channel_id=1, source_target_pairs={{0,1},{1,0},{2,3},{3,2},{4,5},{5,4},{6,7},{7,6},{8,9},{9,8},{10,11... | collective-permute-start | bytes 3145736 | tf_op jit(solution)/shard_map/ppermute | solution.py:371
  95.2 8.6 %collective-permute-start.17 = (bf16[512,1024]{1,0:T(8,128)(2,1)S(1)}, bf16[512,1024]{1,0:T(8,128)(2,1)S(1)}, u32[]{:S(2)}, u32[]{:S(2)}) collective-permute-start(bf16[512,1024]{1,0:T(8,128)(2,1)S(1)} %collective-permute-done.15.refs_3_), channel_id=1, source_target_pairs={{0,1},{1,0},{2,3},{3,2},{4,5},{5,4},{6,7},{7,6},{8,9},{9,8},{10,11... | collective-permute-start | bytes 3145736 | tf_op jit(solution)/shard_map/ppermute | solution.py:371
  98.9 5.0 %collective-permute-start.18 = (bf16[512,1024]{1,0:T(8,128)(2,1)S(1)}, bf16[512,1024]{1,0:T(8,128)(2,1)S(1)}, u32[]{:S(2)}, u32[]{:S(2)}) collective-permute-start(bf16[512,1024]{1,0:T(8,128)(2,1)S(1)} %collective-permute-done.16.refs_4_), channel_id=1, source_target_pairs={{0,1},{1,0},{2,3},{3,2},{4,5},{5,4},{6,7},{7,6},{8,9},{9,8},{10,11... | collective-permute-start | bytes 3145736 | tf_op jit(solution)/shard_map/ppermute | solution.py:371
  (4 other events, 3.7 us)

commit v4 on v3

--- a/solution.py
+++ b/solution.py
@@ -145,9 +145,9 @@
     return pl.pallas_call(
         front_kernel,
         out_shape=(
-            shape((EARLY, depth), BF16),
-            shape((rows + RANK - EARLY + chunks * ranks, depth), BF16),
-            send,
+            HBM((EARLY, depth), BF16),
+            HBM((rows + RANK - EARLY + chunks * ranks, depth), BF16),
+            HBM(send.shape, BF16),
         ),
         in_specs=[hbm] * 7,
         out_specs=(hbm,) * 3,
@@ -438,22 +438,24 @@
         output_gradient[0], up, acts[0], down, groups,
     )
     spot_a, spot_b = spot(x, core), spot(z, core)
-    halves = jnp.stack([spot_a % 2, 1 - spot_a % 2, spot_b % 2, 1 - spot_b % 2]).astype(jnp.int32)
+    halves_a = jnp.stack([spot_a % 2, 1 - spot_a % 2]).astype(jnp.int32)
+    halves_b = jnp.stack([spot_b % 2, 1 - spot_b % 2]).astype(jnp.int32)
     wholes = jnp.stack([spot_a // 2, 1 - spot_a // 2, spot_b // 2, 1 - spot_b // 2]).astype(jnp.int32)
     starts = []
     for c in (core, 1 - core):
         starts += places(z, c) + [half + s for s in places(x, c)]
     starts = jnp.stack(starts).astype(jnp.int32)
-    a0, b0, send, early, late, halves, wholes, starts = tie(
-        a0, b0, send, early, late, halves, wholes, starts
+    a0, b0, send, early, late, halves_a, halves_b, wholes, starts = tie(
+        a0, b0, send, early, late, halves_a, halves_b, wholes, starts
     )
 
     a1, b1 = moved(a0, x_near), moved(b0, z_near)
     early = hop(early, back)
-    a0, b0, a1, b1, send, late = tie(a0, b0, a1, b1, send, late)
+    b0, b1, send, late = tie(b0, b1, send, late)
 
     got = lax.all_to_all(send, "dp", split_axis=0, concat_axis=0, tiled=True)
-    ap, bp = join(halves, (a0, a1), (b0, b1))
+    ap, = join(halves_a, (a0, a1))
+    bp, = join(halves_b, (b0, b1))
     aq, bq = moved(ap, x_far), moved(bp, z_far)
     aq, bq, early, late = tie(aq, bq, early, late)
 
@@ -462,9 +464,7 @@
     a_near, b_near = moved(a, z_near), moved(b, x_near)
     a_far, b_far = moved(a, z_far), moved(b, x_far)
     total_a, total_b = collect(got, adapters, blocks, depth)
-    a, b, a_near, b_near, a_far, b_far, total_a, total_b = tie(
-        a, b, a_near, b_near, a_far, b_far, total_a, total_b
-    )
+    a, b, a_near, b_near, total_a, total_b = tie(a, b, a_near, b_near, total_a, total_b)
 
     def pair(a, b, step, mine=True):
         at = step if mine else step + 2 * SIDE
@@ -474,6 +474,7 @@
         return pair(moved(a, other_core), moved(b, other_core), step, False)
 
     a_last, b_last = moved(a_near, z_far), moved(b_near, x_far)
+    late, a_far, b_far = tie(late, a_far, b_far)
     message, low, down = unpack(early, late, rows, blocks * RANK)
     message, a, b, a_near = tie(message, a, b, a_near)
     shared = (starts, message, low, down)

time: 108 us -> 107 us (level)
  waiting for transfers between devices: 27 us -> 34 us
  starting transfers between devices: 35.9 us -> 29.8 us
  local copies, waits for them, and re-layouts: 5.92 us -> 4.82 us
    ppermute x18, starting transfers between devices: 21 us -> 15.5 us  [moved(): return lax.ppermute(array, 'dp', route)]
    ppermute x18, waiting for transfers between devices: 15.4 us -> 18.7 us  [moved(): return lax.ppermute(array, 'dp', route)]
    ppermute x4, waiting for transfers between devices: 4.87 us -> 7.51 us  [hop(): return lax.ppermute(x, 'pipe', route)]
    pallas_call x1, Pallas kernels: 10.5 us -> 9.05 us  [front(): pl.pallas_call(front_kernel, out_shape=(HBM((EARLY, depth), BF16), HBM((r...]
    unnamed x10 -> x8, local copies, waits for them, and re-layouts: 4.76 us -> 3.66 us
    pallas_call x2 -> x3, Pallas kernels: 2.6 us -> 3.2 us  [join(): pl.pallas_call(functools.partial(join_kernel, counts), out_shape=[jax.Sha...]
  transfers between devices with their start and end apart: 23 -> 23, of which waited for: 7 -> 6; matrix products, arithmetic and copies ran while one was open for 0% -> 0% of each run, Pallas kernels for 32% -> 31%
where the time goes in v4:
time: 107 us; the launch traced here: 106 us
  Pallas kernels  36 us (34%)
  waiting for transfers between devices  34 us (32%)
  starting transfers between devices  29.8 us (28%)
  local copies, waits for them, and re-layouts  4.82 us (5%)
  between operations  1.54 us (1%)
    pallas_call x4, Pallas kernels, product(): pl.pallas_call(functools.partial(product_kernel, tuple((b[1] for b in blo...  18.9 us
    ppermute x18, waiting for transfers between devices, moved(): return lax.ppermute(array, 'dp', route)  18.7 us
    ppermute x18, starting transfers between devices, moved(): return lax.ppermute(array, 'dp', route)  15.5 us
    all_to_all x1, starting transfers between devices, body(): got = lax.all_to_all(send, 'dp', split_axis=0, concat_axis=0, tiled=True)  9.16 us
    pallas_call x1, Pallas kernels, front(): pl.pallas_call(front_kernel, out_shape=(HBM((EARLY, depth), BF16), HBM((r...  9.05 us
    all_to_all x1, waiting for transfers between devices, body(): got = lax.all_to_all(send, 'dp', split_axis=0, concat_axis=0, tiled=True)  7.78 us
    ppermute x4, waiting for transfers between devices, hop(): return lax.ppermute(x, 'pipe', route)  7.51 us
    ppermute x4, starting transfers between devices, hop(): return lax.ppermute(x, 'pipe', route)  5.14 us
  transfers between devices with their start and end apart: 23, of which 6 were waited for; matrix products, arithmetic and copies ran while one was open for 0% of the time, Pallas kernels for 31%

profile of v4, /device:TPU:1, one launch (start us, length us, event | category | flops | bytes accessed | tf_op | source)
XLA Modules:
  0.0 106.3 jit_solution(445929682254387405)
XLA Ops:
  0.7 1.1 %dynamic-slice_bitcast_fusion = (bf16[128,1024]{1,0:T(8,128)(2,1)S(1)}, bf16[128,1024]{1,0:T(8,128)(2,1)S(1)}) fusion(bf16[1,8192,1024]{2,1,0:T(8,128)(2,1)} %param.10, s32[]{:T(128)S(6)} %select_n.163, s32[]{:T(128)S(6)} %select_n.161), kind=kLoop, calls=%fused_computation | loop fusion | bytes 1048584 | tf_op jit(solution)/shard_map/dynamic_slice | solution.py:432
  1.8 1.3 %collective-permute-start = (bf16[128,1024]{1,0:T(8,128)(2,1)S(1)}, bf16[128,1024]{1,0:T(8,128)(2,1)S(1)}, u32[]{:S(2)}, u32[]{:S(2)}) collective-permute-start(bf16[128,1024]{1,0:T(8,128)(2,1)S(1)} %get-tuple-element.104), channel_id=1, source_target_pairs={{32,0},{64,32},{96,64},{33,1},{65,33},{97,65},{34,2},{66,34},{98,6... | collective-permute-start | bytes 786440 | tf_op jit(solution)/shard_map/ppermute | solution.py:400
  3.1 1.3 %collective-permute-start.1 = (bf16[128,1024]{1,0:T(8,128)(2,1)S(1)}, bf16[128,1024]{1,0:T(8,128)(2,1)S(1)}, u32[]{:S(2)}, u32[]{:S(2)}) collective-permute-start(bf16[128,1024]{1,0:T(8,128)(2,1)S(1)} %get-tuple-element.103), channel_id=1, source_target_pairs={{32,0},{64,32},{96,64},{33,1},{65,33},{97,65},{34,2},{66,34},{98,6... | collective-permute-start | bytes 786440 | tf_op jit(solution)/shard_map/ppermute | solution.py:400
  4.4 9.1 %front.1 = (bf16[320,1024]{1,0:T(8,128)(2,1)}, bf16[720,1024]{1,0:T(8,128)(2,1)}, bf16[32,80,256]{2,1,0:T(8,128)(2,1)}) custom-call(s32[1,4]{1,0:T(1,128)} %count_h.1, s32[1,4]{1,0:T(1,128)} %ids_h.1, s32[64]{0:T(128)} %table_h.1, bf16[512,1024]{1,0:T(8,128)(2,1)} %bitcast.39, bf16[64,1024]{1,0:T(8,128)(2,1)} %bitcast.41, bf16[512,8192]{1,0:T(8,128)(2,1)} %bitcast.38, ...), custom_call_target="tpu_custom_call" | custom-call | flops 10000000000 | bytes 12582912 | tf_op jit(solution)/shard_map/front/pallas_call | solution.py:145
  14.2 2.9 %collective-permute-done.1.refs_0_ = bf16[128,1024]{1,0:T(8,128)(2,1)S(1)} collective-permute-done((bf16[128,1024]{1,0:T(8,128)(2,1)S(1)}, bf16[128,1024]{1,0:T(8,128)(2,1)S(1)}, u32[]{:S(2)}, u32[]{:S(2)}) %collective-permute-start.1) | collective-permute-done | bytes 262176 | tf_op jit(solution)/shard_map/ppermute | solution.py:400
  17.0 4.0 %collective-permute-start.4 = (bf16[128,1024]{1,0:T(8,128)(2,1)S(1)}, bf16[128,1024]{1,0:T(8,128)(2,1)S(1)}, u32[]{:S(2)}, u32[]{:S(2)}) collective-permute-start(bf16[128,1024]{1,0:T(8,128)(2,1)S(1)} %collective-permute-done.1.refs_0_), channel_id=1, source_target_pairs={{0,2},{1,7},{2,0},{3,5},{4,6},{5,3},{6,4},{7,1},{8,10},{9,15},{10,... | collective-permute-start | bytes 786440 | tf_op jit(solution)/shard_map/ppermute | solution.py:371
  21.1 2.5 %collective-permute-start.2 = (bf16[128,1024]{1,0:T(8,128)(2,1)S(1)}, bf16[128,1024]{1,0:T(8,128)(2,1)S(1)}, u32[]{:S(2)}, u32[]{:S(2)}) collective-permute-start(bf16[128,1024]{1,0:T(8,128)(2,1)S(1)} %collective-permute-done.refs_0_), channel_id=1, source_target_pairs={{0,8},{1,25},{2,10},{3,27},{4,12},{5,29},{6,14},{7,31},{8,0},{9,17... | collective-permute-start | bytes 786440 | tf_op jit(solution)/shard_map/ppermute | solution.py:371
  23.5 1.3 %collective-permute-start.6 = (bf16[320,1024]{1,0:T(8,128)(2,1)}, bf16[320,1024]{1,0:T(8,128)(2,1)S(1)}, u32[]{:S(2)}, u32[]{:S(2)}) collective-permute-start(bf16[320,1024]{1,0:T(8,128)(2,1)} %get-tuple-element.65), channel_id=1, source_target_pairs={{32,0},{64,32},{96,64},{33,1},{65,33},{97,65},{34,2},{66,34},{98,6... | collective-permute-start | bytes 1966088 | tf_op jit(solution)/shard_map/ppermute | solution.py:400
  25.5 2.0 %collective-permute-done.2.refs_1_ = bf16[128,1024]{1,0:T(8,128)(2,1)S(1)} collective-permute-done((bf16[128,1024]{1,0:T(8,128)(2,1)S(1)}, bf16[128,1024]{1,0:T(8,128)(2,1)S(1)}, u32[]{:S(2)}, u32[]{:S(2)}) %collective-permute-start.2) | collective-permute-done | bytes 262176 | tf_op jit(solution)/shard_map/ppermute | solution.py:371
  28.5 9.2 %all-to-all-start = ((bf16[32,80,256]{2,1,0:T(8,128)(2,1)}), bf16[32,80,256]{2,1,0:T(8,128)(2,1)}, u32[]{:S(2)}, u32[]{:S(2)}) async-start(bf16[32,80,256]{2,1,0:T(8,128)(2,1)} %get-tuple-element.76), calls=%async_computation | async-start | bytes 2621440 | tf_op jit(solution)/shard_map/all_to_all | solution.py:456
  37.6 4.0 %collective-permute-done.6.early_ref = bf16[320,1024]{1,0:T(8,128)(2,1)S(1)} collective-permute-done((bf16[320,1024]{1,0:T(8,128)(2,1)}, bf16[320,1024]{1,0:T(8,128)(2,1)S(1)}, u32[]{:S(2)}, u32[]{:S(2)}) %collective-permute-start.6) | collective-permute-done | bytes 655392 | tf_op jit(solution)/shard_map/ppermute | solution.py:400
  43.3 1.3 %collective-permute-start.7 = (bf16[720,1024]{1,0:T(8,128)(2,1)}, bf16[720,1024]{1,0:T(8,128)(2,1)S(1)}, u32[]{:S(2)}, u32[]{:S(2)}) collective-permute-start(bf16[720,1024]{1,0:T(8,128)(2,1)} %get-tuple-element.68), channel_id=1, source_target_pairs={{32,0},{64,32},{96,64},{33,1},{65,33},{97,65},{34,2},{66,34},{98,6... | collective-permute-start | bytes 4423688 | tf_op jit(solution)/shard_map/ppermute | solution.py:400
  45.6 1.0 copy-done.3
  46.6 2.0 %join.5 = (bf16[512,1024]{1,0:T(8,128)(2,1)}, bf16[512,1024]{1,0:T(8,128)(2,1)}) custom-call(s32[4]{0:T(128)S(1)} %pad_add_fusion.2.spots_ref, bf16[256,1024]{1,0:T(8,128)(2,1)S(1)} %join.3.refs_0_, bf16[256,1024]{1,0:T(8,128)(2,1)S(1)} %copy-done.3, bf16[256,1024]{1,0:T(8,128)(2,1)S(1)} %join.4.refs_2_, bf16[256,1024]{1,0:T(8,128)(2,1)S(1)} %copy-done.1), custom_call_target="tpu_custom_call" | custom-call | flops 1000000 | bytes 2097152 | tf_op jit(solution)/shard_map/join/pallas_call | solution.py:191
  48.7 1.2 %collective-permute-start.11 = (bf16[512,1024]{1,0:T(8,128)(2,1)}, bf16[512,1024]{1,0:T(8,128)(2,1)S(1)}, u32[]{:S(2)}, u32[]{:S(2)}) collective-permute-start(bf16[512,1024]{1,0:T(8,128)(2,1)} %get-tuple-element.86.refs_1_), channel_id=1, source_target_pairs={{0,8},{1,25},{2,10},{3,27},{4,12},{5,29},{6,14},{7,31},{8,0},{9,17... | collective-permute-start | bytes 3145736 | tf_op jit(solution)/shard_map/ppermute | solution.py:371
  49.9 7.8 %all-to-all-done.got_h = bf16[32,80,256]{2,1,0:T(8,128)(2,1)} async-done(((bf16[32,80,256]{2,1,0:T(8,128)(2,1)}), bf16[32,80,256]{2,1,0:T(8,128)(2,1)}, u32[]{:S(2)}, u32[]{:S(2)}) %all-to-all-start) | async-done | bytes 1310752 | tf_op jit(solution)/shard_map/all_to_all | solution.py:456
  57.6 4.6 %collect.1 = (bf16[64,16,256]{2,1,0:T(8,128)(2,1)}, bf16[16,32,64]{2,1,0:T(8,128)(2,1)}) custom-call(bf16[32,80,256]{2,1,0:T(8,128)(2,1)} %all-to-all-done.got_h), custom_call_target="tpu_custom_call" | custom-call | flops 4000000000 | bytes 2621440 | tf_op jit(solution)/shard_map/collect/pallas_call | solution.py:257
  62.2 16.7 %collective-permute-done.10.refs_2_ = bf16[512,1024]{1,0:T(8,128)(2,1)} collective-permute-done((bf16[512,1024]{1,0:T(8,128)(2,1)}, bf16[512,1024]{1,0:T(8,128)(2,1)}, u32[]{:S(2)}, u32[]{:S(2)}) %collective-permute-start.10) | collective-permute-done | bytes 1048608 | tf_op jit(solution)/shard_map/ppermute | solution.py:371
  81.1 7.6 %product_mine.1.refs_3_ = bf16[512,8192]{1,0:T(8,128)(2,1)} custom-call(s32[16]{0:T(128)S(1)} %stack.111.starts_ref, bf16[512,1024]{1,0:T(8,128)(2,1)S(1)} %get-tuple-element.82.message_ref, bf16[512,64]{1,0:T(8,128)(2,1)S(1)} %get-tuple-element.83.low_ref, bf16[512,1024]{1,0:T(8,128)(2,1)S(1)} %get-tuple-element.84.down_ref, ...), custom_call_target="tpu_custom_call" | custom-call | flops 1000000 | bytes 1000000 | tf_op jit(solution)/shard_map/product_mine/pallas_call | solution.py:339
  88.8 2.1 %collective-permute-start.19 = (bf16[512,1024]{1,0:T(8,128)(2,1)S(1)}, bf16[512,1024]{1,0:T(8,128)(2,1)S(1)}, u32[]{:S(2)}, u32[]{:S(2)}) collective-permute-start(bf16[512,1024]{1,0:T(8,128)(2,1)S(1)} %collective-permute-done.11.refs_3_), channel_id=1, source_target_pairs={{0,1},{1,0},{2,3},{3,2},{4,5},{5,4},{6,7},{7,6},{8,9},{9,8},{10,11... | collective-permute-start | bytes 3145736 | tf_op jit(solution)/shard_map/ppermute | solution.py:371
  91.4 3.5 %product_first.1.refs_5_ = bf16[512,8192]{1,0:T(8,128)(2,1)} custom-call(s32[16]{0:T(128)S(1)} %stack.111.starts_ref, bf16[512,1024]{1,0:T(8,128)(2,1)S(1)} %get-tuple-element.82.message_ref, bf16[512,64]{1,0:T(8,128)(2,1)S(1)} %get-tuple-element.83.low_ref, bf16[512,1024]{1,0:T(8,128)(2,1)S(1)} %get-tuple-element.84.down_ref, ...), custom_call_target="tpu_custom_call", output_to_operand_aliasing={{}: (7, {})} | custom-call | flops 1000000 | bytes 1000000 | tf_op jit(solution)/shard_map/product_first/pallas_call | solution.py:339
  95.0 3.3 %collective-permute-start.17 = (bf16[512,1024]{1,0:T(8,128)(2,1)S(1)}, bf16[512,1024]{1,0:T(8,128)(2,1)S(1)}, u32[]{:S(2)}, u32[]{:S(2)}) collective-permute-start(bf16[512,1024]{1,0:T(8,128)(2,1)S(1)} %collective-permute-done.15.refs_3_), channel_id=1, source_target_pairs={{0,1},{1,0},{2,3},{3,2},{4,5},{5,4},{6,7},{7,6},{8,9},{9,8},{10,11... | collective-permute-start | bytes 3145736 | tf_op jit(solution)/shard_map/ppermute | solution.py:371
  98.4 4.9 %product_second.1.refs_2_ = bf16[512,8192]{1,0:T(8,128)(2,1)} custom-call(s32[16]{0:T(128)S(1)} %stack.111.starts_ref, bf16[512,1024]{1,0:T(8,128)(2,1)S(1)} %get-tuple-element.82.message_ref, bf16[512,64]{1,0:T(8,128)(2,1)S(1)} %get-tuple-element.83.low_ref, bf16[512,1024]{1,0:T(8,128)(2,1)S(1)} %get-tuple-element.84.down_ref, ...), custom_call_target="tpu_custom_call", output_to_operand_aliasing={{}: (9, {})} | custom-call | flops 1000000 | bytes 1000000 | tf_op jit(solution)/shard_map/product_second/pallas_call | solution.py:339
  103.3 2.9 %product_end.1 = bf16[512,8192]{1,0:T(8,128)(2,1)} custom-call(s32[16]{0:T(128)S(1)} %stack.111.starts_ref, bf16[512,1024]{1,0:T(8,128)(2,1)S(1)} %get-tuple-element.82.message_ref, bf16[512,64]{1,0:T(8,128)(2,1)S(1)} %get-tuple-element.83.low_ref, bf16[512,1024]{1,0:T(8,128)(2,1)S(1)} %get-tuple-element.84.down_ref, ...), custom_call_target="tpu_custom_call", output_to_operand_aliasing={{}: (6, {})} | custom-call | flops 1000000 | bytes 1000000 | tf_op jit(solution)/shard_map/product_end/pallas_call | solution.py:339
  (44 shorter events, 7.2 us)
Async XLA Ops:
  1.8 12.4 %collective-permute-start = (bf16[128,1024]{1,0:T(8,128)(2,1)S(1)}, bf16[128,1024]{1,0:T(8,128)(2,1)S(1)}, u32[]{:S(2)}, u32[]{:S(2)}) collective-permute-start(bf16[128,1024]{1,0:T(8,128)(2,1)S(1)} %get-tuple-element.104), channel_id=1, source_target_pairs={{32,0},{64,32},{96,64},{33,1},{65,33},{97,65},{34,2},{66,34},{98,6... | collective-permute-start | bytes 786440 | tf_op jit(solution)/shard_map/ppermute | solution.py:400
  3.1 13.9 %collective-permute-start.1 = (bf16[128,1024]{1,0:T(8,128)(2,1)S(1)}, bf16[128,1024]{1,0:T(8,128)(2,1)S(1)}, u32[]{:S(2)}, u32[]{:S(2)}) collective-permute-start(bf16[128,1024]{1,0:T(8,128)(2,1)S(1)} %get-tuple-element.103), channel_id=1, source_target_pairs={{32,0},{64,32},{96,64},{33,1},{65,33},{97,65},{34,2},{66,34},{98,6... | collective-permute-start | bytes 786440 | tf_op jit(solution)/shard_map/ppermute | solution.py:400
  17.0 7.8 %collective-permute-start.4 = (bf16[128,1024]{1,0:T(8,128)(2,1)S(1)}, bf16[128,1024]{1,0:T(8,128)(2,1)S(1)}, u32[]{:S(2)}, u32[]{:S(2)}) collective-permute-start(bf16[128,1024]{1,0:T(8,128)(2,1)S(1)} %collective-permute-done.1.refs_0_), channel_id=1, source_target_pairs={{0,2},{1,7},{2,0},{3,5},{4,6},{5,3},{6,4},{7,1},{8,10},{9,15},{10,... | collective-permute-start | bytes 786440 | tf_op jit(solution)/shard_map/ppermute | solution.py:371
  21.1 6.4 %collective-permute-start.2 = (bf16[128,1024]{1,0:T(8,128)(2,1)S(1)}, bf16[128,1024]{1,0:T(8,128)(2,1)S(1)}, u32[]{:S(2)}, u32[]{:S(2)}) collective-permute-start(bf16[128,1024]{1,0:T(8,128)(2,1)S(1)} %collective-permute-done.refs_0_), channel_id=1, source_target_pairs={{0,8},{1,25},{2,10},{3,27},{4,12},{5,29},{6,14},{7,31},{8,0},{9,17... | collective-permute-start | bytes 786440 | tf_op jit(solution)/shard_map/ppermute | solution.py:371
  23.5 18.1 %collective-permute-start.6 = (bf16[320,1024]{1,0:T(8,128)(2,1)}, bf16[320,1024]{1,0:T(8,128)(2,1)S(1)}, u32[]{:S(2)}, u32[]{:S(2)}) collective-permute-start(bf16[320,1024]{1,0:T(8,128)(2,1)} %get-tuple-element.65), channel_id=1, source_target_pairs={{32,0},{64,32},{96,64},{33,1},{65,33},{97,65},{34,2},{66,34},{98,6... | collective-permute-start | bytes 1966088 | tf_op jit(solution)/shard_map/ppermute | solution.py:400
  25.4 16.2 %collective-permute-start.5 = (bf16[256,1024]{1,0:T(8,128)(2,1)S(1)}, bf16[256,1024]{1,0:T(8,128)(2,1)S(1)}, u32[]{:S(2)}, u32[]{:S(2)}) collective-permute-start(bf16[256,1024]{1,0:T(8,128)(2,1)S(1)} %join.4.refs_2_), channel_id=1, source_target_pairs={{0,6},{1,3},{2,4},{3,1},{4,2},{5,7},{6,0},{7,5},{8,14},{9,11},{10,... | collective-permute-start | bytes 1572872 | tf_op jit(solution)/shard_map/ppermute | solution.py:371
  28.1 14.4 %collective-permute-start.3 = (bf16[256,1024]{1,0:T(8,128)(2,1)S(1)}, bf16[256,1024]{1,0:T(8,128)(2,1)S(1)}, u32[]{:S(2)}, u32[]{:S(2)}) collective-permute-start(bf16[256,1024]{1,0:T(8,128)(2,1)S(1)} %join.3.refs_0_), channel_id=1, source_target_pairs={{0,24},{1,9},{2,26},{3,11},{4,28},{5,13},{6,30},{7,15},{8,16},{9,1... | collective-permute-start | bytes 1572872 | tf_op jit(solution)/shard_map/ppermute | solution.py:371
  28.5 29.2 %all-to-all-start = ((bf16[32,80,256]{2,1,0:T(8,128)(2,1)}), bf16[32,80,256]{2,1,0:T(8,128)(2,1)}, u32[]{:S(2)}, u32[]{:S(2)}) async-start(bf16[32,80,256]{2,1,0:T(8,128)(2,1)} %get-tuple-element.76), calls=%async_computation | async-start | bytes 2621440 | tf_op jit(solution)/shard_map/all_to_all | solution.py:456
  43.3 36.3 %collective-permute-start.7 = (bf16[720,1024]{1,0:T(8,128)(2,1)}, bf16[720,1024]{1,0:T(8,128)(2,1)S(1)}, u32[]{:S(2)}, u32[]{:S(2)}) collective-permute-start(bf16[720,1024]{1,0:T(8,128)(2,1)} %get-tuple-element.68), channel_id=1, source_target_pairs={{32,0},{64,32},{96,64},{33,1},{65,33},{97,65},{34,2},{66,34},{98,6... | collective-permute-start | bytes 4423688 | tf_op jit(solution)/shard_map/ppermute | solution.py:400
  44.6 1.0 copy-start.1
  48.7 30.3 %collective-permute-start.10 = (bf16[512,1024]{1,0:T(8,128)(2,1)}, bf16[512,1024]{1,0:T(8,128)(2,1)}, u32[]{:S(2)}, u32[]{:S(2)}) collective-permute-start(bf16[512,1024]{1,0:T(8,128)(2,1)} %get-tuple-element.85.refs_0_), channel_id=1, source_target_pairs={{0,2},{1,7},{2,0},{3,5},{4,6},{5,3},{6,4},{7,1},{8,10},{9,15},{10,... | collective-permute-start | bytes 3145736 | tf_op jit(solution)/shard_map/ppermute | solution.py:371
  48.7 30.3 %collective-permute-start.11 = (bf16[512,1024]{1,0:T(8,128)(2,1)}, bf16[512,1024]{1,0:T(8,128)(2,1)S(1)}, u32[]{:S(2)}, u32[]{:S(2)}) collective-permute-start(bf16[512,1024]{1,0:T(8,128)(2,1)} %get-tuple-element.86.refs_1_), channel_id=1, source_target_pairs={{0,8},{1,25},{2,10},{3,27},{4,12},{5,29},{6,14},{7,31},{8,0},{9,17... | collective-permute-start | bytes 3145736 | tf_op jit(solution)/shard_map/ppermute | solution.py:371
  49.8 29.1 %collective-permute-start.8 = (bf16[512,1024]{1,0:T(8,128)(2,1)}, bf16[512,1024]{1,0:T(8,128)(2,1)}, u32[]{:S(2)}, u32[]{:S(2)}) collective-permute-start(bf16[512,1024]{1,0:T(8,128)(2,1)} %get-tuple-element.85.refs_0_), channel_id=1, source_target_pairs={{0,6},{1,3},{2,4},{3,1},{4,2},{5,7},{6,0},{7,5},{8,14},{9,11},{10,... | collective-permute-start | bytes 3145736 | tf_op jit(solution)/shard_map/ppermute | solution.py:371
  49.8 29.1 %collective-permute-start.9 = (bf16[512,1024]{1,0:T(8,128)(2,1)}, bf16[512,1024]{1,0:T(8,128)(2,1)}, u32[]{:S(2)}, u32[]{:S(2)}) collective-permute-start(bf16[512,1024]{1,0:T(8,128)(2,1)} %get-tuple-element.86.refs_1_), channel_id=1, source_target_pairs={{0,24},{1,9},{2,26},{3,11},{4,28},{5,13},{6,30},{7,15},{8,16},{9,1... | collective-permute-start | bytes 3145736 | tf_op jit(solution)/shard_map/ppermute | solution.py:371
  79.8 9.0 %collective-permute-start.12 = (bf16[512,1024]{1,0:T(8,128)(2,1)}, bf16[512,1024]{1,0:T(8,128)(2,1)S(1)}, u32[]{:S(2)}, u32[]{:S(2)}) collective-permute-start(bf16[512,1024]{1,0:T(8,128)(2,1)} %get-tuple-element.85.refs_0_), channel_id=1, source_target_pairs={{0,1},{1,0},{2,3},{3,2},{4,5},{5,4},{6,7},{7,6},{8,9},{9,8},{10,11... | collective-permute-start | bytes 3145736 | tf_op jit(solution)/shard_map/ppermute | solution.py:371
  80.3 8.5 %collective-permute-start.13 = (bf16[512,1024]{1,0:T(8,128)(2,1)}, bf16[512,1024]{1,0:T(8,128)(2,1)S(1)}, u32[]{:S(2)}, u32[]{:S(2)}) collective-permute-start(bf16[512,1024]{1,0:T(8,128)(2,1)} %get-tuple-element.86.refs_1_), channel_id=1, source_target_pairs={{0,1},{1,0},{2,3},{3,2},{4,5},{5,4},{6,7},{7,6},{8,9},{9,8},{10,11... | collective-permute-start | bytes 3145736 | tf_op jit(solution)/shard_map/ppermute | solution.py:371
  80.4 8.4 %collective-permute-start.14 = (bf16[512,1024]{1,0:T(8,128)(2,1)}, bf16[512,1024]{1,0:T(8,128)(2,1)S(1)}, u32[]{:S(2)}, u32[]{:S(2)}) collective-permute-start(bf16[512,1024]{1,0:T(8,128)(2,1)} %collective-permute-done.10.refs_2_), channel_id=1, source_target_pairs={{0,1},{1,0},{2,3},{3,2},{4,5},{5,4},{6,7},{7,6},{8,9},{9,8},{10,11... | collective-permute-start | bytes 3145736 | tf_op jit(solution)/shard_map/ppermute | solution.py:371
  80.8 14.2 %collective-permute-start.15 = (bf16[512,1024]{1,0:T(8,128)(2,1)}, bf16[512,1024]{1,0:T(8,128)(2,1)S(1)}, u32[]{:S(2)}, u32[]{:S(2)}) collective-permute-start(bf16[512,1024]{1,0:T(8,128)(2,1)} %collective-permute-done.10.refs_2_), channel_id=1, source_target_pairs={{0,6},{1,3},{2,4},{3,1},{4,2},{5,7},{6,0},{7,5},{8,14},{9,11},{10,... | collective-permute-start | bytes 3145736 | tf_op jit(solution)/shard_map/ppermute | solution.py:371
  80.8 14.2 %collective-permute-start.16 = (bf16[512,1024]{1,0:T(8,128)(2,1)S(1)}, bf16[512,1024]{1,0:T(8,128)(2,1)S(1)}, u32[]{:S(2)}, u32[]{:S(2)}) collective-permute-start(bf16[512,1024]{1,0:T(8,128)(2,1)S(1)} %collective-permute-done.11.refs_3_), channel_id=1, source_target_pairs={{0,24},{1,9},{2,26},{3,11},{4,28},{5,13},{6,30},{7,15},{8,16},{9,1... | collective-permute-start | bytes 3145736 | tf_op jit(solution)/shard_map/ppermute | solution.py:371
  88.8 9.6 %collective-permute-start.19 = (bf16[512,1024]{1,0:T(8,128)(2,1)S(1)}, bf16[512,1024]{1,0:T(8,128)(2,1)S(1)}, u32[]{:S(2)}, u32[]{:S(2)}) collective-permute-start(bf16[512,1024]{1,0:T(8,128)(2,1)S(1)} %collective-permute-done.11.refs_3_), channel_id=1, source_target_pairs={{0,1},{1,0},{2,3},{3,2},{4,5},{5,4},{6,7},{7,6},{8,9},{9,8},{10,11... | collective-permute-start | bytes 3145736 | tf_op jit(solution)/shard_map/ppermute | solution.py:371
  90.9 7.4 %collective-permute-start.20 = (bf16[512,1024]{1,0:T(8,128)(2,1)}, bf16[512,1024]{1,0:T(8,128)(2,1)S(1)}, u32[]{:S(2)}, u32[]{:S(2)}) collective-permute-start(bf16[512,1024]{1,0:T(8,128)(2,1)} %collective-permute-done.8.refs_4_), channel_id=1, source_target_pairs={{0,1},{1,0},{2,3},{3,2},{4,5},{5,4},{6,7},{7,6},{8,9},{9,8},{10,11... | collective-permute-start | bytes 3145736 | tf_op jit(solution)/shard_map/ppermute | solution.py:371
  91.0 7.3 %collective-permute-start.21 = (bf16[512,1024]{1,0:T(8,128)(2,1)}, bf16[512,1024]{1,0:T(8,128)(2,1)S(1)}, u32[]{:S(2)}, u32[]{:S(2)}) collective-permute-start(bf16[512,1024]{1,0:T(8,128)(2,1)} %collective-permute-done.9.refs_5_), channel_id=1, source_target_pairs={{0,1},{1,0},{2,3},{3,2},{4,5},{5,4},{6,7},{7,6},{8,9},{9,8},{10,11... | collective-permute-start | bytes 3145736 | tf_op jit(solution)/shard_map/ppermute | solution.py:371
  95.0 8.3 %collective-permute-start.17 = (bf16[512,1024]{1,0:T(8,128)(2,1)S(1)}, bf16[512,1024]{1,0:T(8,128)(2,1)S(1)}, u32[]{:S(2)}, u32[]{:S(2)}) collective-permute-start(bf16[512,1024]{1,0:T(8,128)(2,1)S(1)} %collective-permute-done.15.refs_3_), channel_id=1, source_target_pairs={{0,1},{1,0},{2,3},{3,2},{4,5},{5,4},{6,7},{7,6},{8,9},{9,8},{10,11... | collective-permute-start | bytes 3145736 | tf_op jit(solution)/shard_map/ppermute | solution.py:371
  98.3 5.0 %collective-permute-start.18 = (bf16[512,1024]{1,0:T(8,128)(2,1)S(1)}, bf16[512,1024]{1,0:T(8,128)(2,1)S(1)}, u32[]{:S(2)}, u32[]{:S(2)}) collective-permute-start(bf16[512,1024]{1,0:T(8,128)(2,1)S(1)} %collective-permute-done.16.refs_4_), channel_id=1, source_target_pairs={{0,1},{1,0},{2,3},{3,2},{4,5},{5,4},{6,7},{7,6},{8,9},{9,8},{10,11... | collective-permute-start | bytes 3145736 | tf_op jit(solution)/shard_map/ppermute | solution.py:371
  (3 other events, 2.6 us)

commit v5 on v4

--- a/solution.py
+++ b/solution.py
@@ -17,7 +17,7 @@
 SIDE, CORES = 4, 2
 PIECE = 128
 BLOCK = SIDE * PIECE
-EARLY = 320
+EARLY = 352
 HBM = pltpu.MemorySpace.HBM
 
 LAST = (((1,), (1,)), ((), ()))
@@ -175,28 +175,35 @@
 
 
 def join_kernel(counts, spots_ref, *refs):
-    parts, outs = refs[: sum(counts)], refs[sum(counts) :]
-    i = 0
+    parts, outs, sems = refs[: sum(counts)], refs[sum(counts) : -1], refs[-1]
+    copies = []
     for n, out in zip(counts, outs):
-        rows = parts[i].shape[0]
-        for part in parts[i : i + n]:
+        for _ in range(n):
+            i = len(copies)
+            rows = parts[i].shape[0]
             at = pl.multiple_of(spots_ref[i] * rows, rows)
-            out[pl.ds(at, rows), :] = part[...]
-            i += 1
-
-
-def join(spots, *groups):
+            copies.append(pltpu.make_async_copy(parts[i], out.at[pl.ds(at, rows)], sems.at[i]))
+            copies[i].start()
+    for copy in copies:
+        copy.wait()
+
+
+def join(spots, *groups, constrain):
     counts = tuple(len(g) for g in groups)
     in_vmem = pl.BlockSpec(memory_space=pltpu.VMEM)
+    parts = [v for g in groups for v in g]
+    if constrain:
+        parts = in_hbm(*parts)
     return pl.pallas_call(
         functools.partial(join_kernel, counts),
         out_shape=[jax.ShapeDtypeStruct((sum(v.shape[0] for v in g), g[0].shape[1]), BF16) for g in groups],
-        in_specs=[pl.BlockSpec(memory_space=pltpu.SMEM)] + [in_vmem] * sum(counts),
+        in_specs=[pl.BlockSpec(memory_space=pltpu.SMEM)] + [pl.BlockSpec(memory_space=HBM if constrain else pl.ANY)] * sum(counts),
         out_specs=[in_vmem] * len(groups),
-        compiler_params=vmem(4),
+        scratch_shapes=[pltpu.SemaphoreType.DMA((sum(counts),))],
+        compiler_params=vmem(6),
         cost_estimate=pl.CostEstimate(flops=10**6, transcendentals=0, bytes_accessed=1 << 21),
         name="join",
-    )(spots, *[v for g in groups for v in g])
+    )(spots, *parts)
 
 
 def collect_kernel(got_h, out_a, out_b, a_v, tail_v, pick_v, sems):
@@ -454,13 +461,13 @@
     b0, b1, send, late = tie(b0, b1, send, late)
 
     got = lax.all_to_all(send, "dp", split_axis=0, concat_axis=0, tiled=True)
-    ap, = join(halves_a, (a0, a1))
-    bp, = join(halves_b, (b0, b1))
+    ap, = join(halves_a, (a0, a1), constrain=False)
+    bp, = join(halves_b, (b0, b1), constrain=False)
     aq, bq = moved(ap, x_far), moved(bp, z_far)
     aq, bq, early, late = tie(aq, bq, early, late)
 
     late = hop(late, back)
-    a, b = join(wholes, (ap, aq), (bp, bq))
+    a, b = join(wholes, (ap, aq), (bp, bq), constrain=True)
     a_near, b_near = moved(a, z_near), moved(b, x_near)
     a_far, b_far = moved(a, z_far), moved(b, x_far)
     total_a, total_b = collect(got, adapters, blocks, depth)

time: 107 us -> 107 us (level)
  local copies, waits for them, and re-layouts: 4.82 us -> 2.04 us
  Pallas kernels: 36 us -> 37.3 us
  waiting for transfers between devices: 34 us -> 35.1 us
    unnamed x8 -> x10, local copies, waits for them, and re-layouts: 3.66 us -> 0.88 us
    pallas_call x3, Pallas kernels: 3.2 us -> 4.67 us  [join(): pl.pallas_call(functools.partial(join_kernel, counts), out_shape=[jax.Sha...]
  transfers between devices with their start and end apart: 23 -> 23, of which waited for: 6 -> 5; matrix products, arithmetic and copies ran while one was open for 0% -> 0% of each run, Pallas kernels for 31% -> 32%
where the time goes in v5:
time: 107 us; the launch traced here: 106 us
  Pallas kernels  37.3 us (35%)
  waiting for transfers between devices  35.1 us (33%)
  starting transfers between devices  30.2 us (28%)
  local copies, waits for them, and re-layouts  2.04 us (2%)
  between operations  1.6 us (1%)
    pallas_call x4, Pallas kernels, product(): pl.pallas_call(functools.partial(product_kernel, tuple((b[1] for b in blo...  18.6 us
    ppermute x18, waiting for transfers between devices, moved(): return lax.ppermute(array, 'dp', route)  18.5 us
    ppermute x18, starting transfers between devices, moved(): return lax.ppermute(array, 'dp', route)  15.9 us
    all_to_all x1, starting transfers between devices, body(): got = lax.all_to_all(send, 'dp', split_axis=0, concat_axis=0, tiled=True)  9.2 us
    pallas_call x1, Pallas kernels, front(): pl.pallas_call(front_kernel, out_shape=(HBM((EARLY, depth), BF16), HBM((r...  9.12 us
    all_to_all x1, waiting for transfers between devices, body(): got = lax.all_to_all(send, 'dp', split_axis=0, concat_axis=0, tiled=True)  8.35 us
    ppermute x4, waiting for transfers between devices, hop(): return lax.ppermute(x, 'pipe', route)  8.19 us
    ppermute x4, starting transfers between devices, hop(): return lax.ppermute(x, 'pipe', route)  5.16 us
  transfers between devices with their start and end apart: 23, of which 5 were waited for; matrix products, arithmetic and copies ran while one was open for 0% of the time, Pallas kernels for 32%

profile of v5, /device:TPU:1, one launch (start us, length us, event | category | flops | bytes accessed | tf_op | source)
XLA Modules:
  0.0 106.4 jit_solution(13615120622786499301)
XLA Ops:
  0.7 1.1 %dynamic-slice_bitcast_fusion = (bf16[128,1024]{1,0:T(8,128)(2,1)S(1)}, bf16[128,1024]{1,0:T(8,128)(2,1)S(1)}) fusion(bf16[1,8192,1024]{2,1,0:T(8,128)(2,1)} %param.10, s32[]{:T(128)S(6)} %select_n.163, s32[]{:T(128)S(6)} %select_n.161), kind=kLoop, calls=%fused_computation | loop fusion | bytes 1048584 | tf_op jit(solution)/shard_map/dynamic_slice | solution.py:439
  1.8 1.3 %collective-permute-start = (bf16[128,1024]{1,0:T(8,128)(2,1)S(1)}, bf16[128,1024]{1,0:T(8,128)(2,1)S(1)}, u32[]{:S(2)}, u32[]{:S(2)}) collective-permute-start(bf16[128,1024]{1,0:T(8,128)(2,1)S(1)} %get-tuple-element.104), channel_id=1, source_target_pairs={{32,0},{64,32},{96,64},{33,1},{65,33},{97,65},{34,2},{66,34},{98,6... | collective-permute-start | bytes 786440 | tf_op jit(solution)/shard_map/ppermute | solution.py:407
  3.1 1.3 %collective-permute-start.1 = (bf16[128,1024]{1,0:T(8,128)(2,1)S(1)}, bf16[128,1024]{1,0:T(8,128)(2,1)S(1)}, u32[]{:S(2)}, u32[]{:S(2)}) collective-permute-start(bf16[128,1024]{1,0:T(8,128)(2,1)S(1)} %get-tuple-element.103), channel_id=1, source_target_pairs={{32,0},{64,32},{96,64},{33,1},{65,33},{97,65},{34,2},{66,34},{98,6... | collective-permute-start | bytes 786440 | tf_op jit(solution)/shard_map/ppermute | solution.py:407
  4.4 9.1 %front.1 = (bf16[352,1024]{1,0:T(8,128)(2,1)}, bf16[688,1024]{1,0:T(8,128)(2,1)}, bf16[32,80,256]{2,1,0:T(8,128)(2,1)}) custom-call(s32[1,4]{1,0:T(1,128)} %count_h.1, s32[1,4]{1,0:T(1,128)} %ids_h.1, s32[64]{0:T(128)} %table_h.1, bf16[512,1024]{1,0:T(8,128)(2,1)} %bitcast.39, bf16[64,1024]{1,0:T(8,128)(2,1)} %bitcast.41, bf16[512,8192]{1,0:T(8,128)(2,1)} %bitcast.38, ...), custom_call_target="tpu_custom_call" | custom-call | flops 10000000000 | bytes 12582912 | tf_op jit(solution)/shard_map/front/pallas_call | solution.py:145
  14.2 2.8 %collective-permute-done.1.refs_0_ = bf16[128,1024]{1,0:T(8,128)(2,1)S(1)} collective-permute-done((bf16[128,1024]{1,0:T(8,128)(2,1)S(1)}, bf16[128,1024]{1,0:T(8,128)(2,1)S(1)}, u32[]{:S(2)}, u32[]{:S(2)}) %collective-permute-start.1) | collective-permute-done | bytes 262176 | tf_op jit(solution)/shard_map/ppermute | solution.py:407
  17.0 4.0 %collective-permute-start.4 = (bf16[128,1024]{1,0:T(8,128)(2,1)S(1)}, bf16[128,1024]{1,0:T(8,128)(2,1)S(1)}, u32[]{:S(2)}, u32[]{:S(2)}) collective-permute-start(bf16[128,1024]{1,0:T(8,128)(2,1)S(1)} %collective-permute-done.1.refs_0_), channel_id=1, source_target_pairs={{0,2},{1,7},{2,0},{3,5},{4,6},{5,3},{6,4},{7,1},{8,10},{9,15},{10,... | collective-permute-start | bytes 786440 | tf_op jit(solution)/shard_map/ppermute | solution.py:378
  21.1 2.5 %collective-permute-start.2 = (bf16[128,1024]{1,0:T(8,128)(2,1)S(1)}, bf16[128,1024]{1,0:T(8,128)(2,1)S(1)}, u32[]{:S(2)}, u32[]{:S(2)}) collective-permute-start(bf16[128,1024]{1,0:T(8,128)(2,1)S(1)} %collective-permute-done.refs_0_), channel_id=1, source_target_pairs={{0,8},{1,25},{2,10},{3,27},{4,12},{5,29},{6,14},{7,31},{8,0},{9,17... | collective-permute-start | bytes 786440 | tf_op jit(solution)/shard_map/ppermute | solution.py:378
  23.5 1.3 %collective-permute-start.6 = (bf16[352,1024]{1,0:T(8,128)(2,1)}, bf16[352,1024]{1,0:T(8,128)(2,1)S(1)}, u32[]{:S(2)}, u32[]{:S(2)}) collective-permute-start(bf16[352,1024]{1,0:T(8,128)(2,1)} %get-tuple-element.65), channel_id=1, source_target_pairs={{32,0},{64,32},{96,64},{33,1},{65,33},{97,65},{34,2},{66,34},{98,6... | collective-permute-start | bytes 2162696 | tf_op jit(solution)/shard_map/ppermute | solution.py:407
  24.8 0.6 join.4.refs_2_
  25.6 1.9 %collective-permute-done.2.refs_1_ = bf16[128,1024]{1,0:T(8,128)(2,1)S(1)} collective-permute-done((bf16[128,1024]{1,0:T(8,128)(2,1)S(1)}, bf16[128,1024]{1,0:T(8,128)(2,1)S(1)}, u32[]{:S(2)}, u32[]{:S(2)}) %collective-permute-start.2) | collective-permute-done | bytes 262176 | tf_op jit(solution)/shard_map/ppermute | solution.py:378
  28.5 9.2 %all-to-all-start = ((bf16[32,80,256]{2,1,0:T(8,128)(2,1)}), bf16[32,80,256]{2,1,0:T(8,128)(2,1)}, u32[]{:S(2)}, u32[]{:S(2)}) async-start(bf16[32,80,256]{2,1,0:T(8,128)(2,1)} %get-tuple-element.76), calls=%async_computation | async-start | bytes 2621440 | tf_op jit(solution)/shard_map/all_to_all | solution.py:463
  37.7 5.4 %collective-permute-done.6.early_ref = bf16[352,1024]{1,0:T(8,128)(2,1)S(1)} collective-permute-done((bf16[352,1024]{1,0:T(8,128)(2,1)}, bf16[352,1024]{1,0:T(8,128)(2,1)S(1)}, u32[]{:S(2)}, u32[]{:S(2)}) %collective-permute-start.6) | collective-permute-done | bytes 720928 | tf_op jit(solution)/shard_map/ppermute | solution.py:407
  43.1 0.9 copy-done.2
  44.0 1.3 %collective-permute-start.7 = (bf16[688,1024]{1,0:T(8,128)(2,1)}, bf16[688,1024]{1,0:T(8,128)(2,1)S(1)}, u32[]{:S(2)}, u32[]{:S(2)}) collective-permute-start(bf16[688,1024]{1,0:T(8,128)(2,1)} %get-tuple-element.68), channel_id=1, source_target_pairs={{32,0},{64,32},{96,64},{33,1},{65,33},{97,65},{34,2},{66,34},{98,6... | collective-permute-start | bytes 4227080 | tf_op jit(solution)/shard_map/ppermute | solution.py:407
  45.3 3.5 %join.5 = (bf16[512,1024]{1,0:T(8,128)(2,1)}, bf16[512,1024]{1,0:T(8,128)(2,1)}) custom-call(s32[4]{0:T(128)S(1)} %pad_add_fusion.2.spots_ref, bf16[256,1024]{1,0:T(8,128)(2,1)} %copy-done.1, bf16[256,1024]{1,0:T(8,128)(2,1)} %collective-permute-done.3.refs_1_, bf16[256,1024]{1,0:T(8,128)(2,1)} %copy-done, bf16[256,1024]{1,0:T(8,128)(2,1)} %copy-done.4), custom_call_target="tpu_custom_call" | custom-call | flops 1000000 | bytes 2097152 | tf_op jit(solution)/shard_map/join/pallas_call | solution.py:197
  49.4 8.4 %all-to-all-done.got_h = bf16[32,80,256]{2,1,0:T(8,128)(2,1)} async-done(((bf16[32,80,256]{2,1,0:T(8,128)(2,1)}), bf16[32,80,256]{2,1,0:T(8,128)(2,1)}, u32[]{:S(2)}, u32[]{:S(2)}) %all-to-all-start) | async-done | bytes 1310752 | tf_op jit(solution)/shard_map/all_to_all | solution.py:463
  57.7 4.7 %collect.1 = (bf16[64,16,256]{2,1,0:T(8,128)(2,1)}, bf16[16,32,64]{2,1,0:T(8,128)(2,1)}) custom-call(bf16[32,80,256]{2,1,0:T(8,128)(2,1)} %all-to-all-done.got_h), custom_call_target="tpu_custom_call" | custom-call | flops 4000000000 | bytes 2621440 | tf_op jit(solution)/shard_map/collect/pallas_call | solution.py:264
  62.4 16.5 %collective-permute-done.10.refs_2_ = bf16[512,1024]{1,0:T(8,128)(2,1)} collective-permute-done((bf16[512,1024]{1,0:T(8,128)(2,1)}, bf16[512,1024]{1,0:T(8,128)(2,1)}, u32[]{:S(2)}, u32[]{:S(2)}) %collective-permute-start.10) | collective-permute-done | bytes 1048608 | tf_op jit(solution)/shard_map/ppermute | solution.py:378
  80.9 7.3 %product_mine.1.refs_3_ = bf16[512,8192]{1,0:T(8,128)(2,1)} custom-call(s32[16]{0:T(128)S(1)} %stack.111.starts_ref, bf16[512,1024]{1,0:T(8,128)(2,1)S(1)} %get-tuple-element.82.message_ref, bf16[512,64]{1,0:T(8,128)(2,1)S(1)} %get-tuple-element.83.low_ref, bf16[512,1024]{1,0:T(8,128)(2,1)S(1)} %get-tuple-element.84.down_ref, ...), custom_call_target="tpu_custom_call" | custom-call | flops 1000000 | bytes 1000000 | tf_op jit(solution)/shard_map/product_mine/pallas_call | solution.py:346
  88.2 2.5 %collective-permute-start.19 = (bf16[512,1024]{1,0:T(8,128)(2,1)S(1)}, bf16[512,1024]{1,0:T(8,128)(2,1)S(1)}, u32[]{:S(2)}, u32[]{:S(2)}) collective-permute-start(bf16[512,1024]{1,0:T(8,128)(2,1)S(1)} %collective-permute-done.11.refs_3_), channel_id=1, source_target_pairs={{0,1},{1,0},{2,3},{3,2},{4,5},{5,4},{6,7},{7,6},{8,9},{9,8},{10,11... | collective-permute-start | bytes 3145736 | tf_op jit(solution)/shard_map/ppermute | solution.py:378
  91.2 3.5 %product_first.1.refs_5_ = bf16[512,8192]{1,0:T(8,128)(2,1)} custom-call(s32[16]{0:T(128)S(1)} %stack.111.starts_ref, bf16[512,1024]{1,0:T(8,128)(2,1)S(1)} %get-tuple-element.82.message_ref, bf16[512,64]{1,0:T(8,128)(2,1)S(1)} %get-tuple-element.83.low_ref, bf16[512,1024]{1,0:T(8,128)(2,1)S(1)} %get-tuple-element.84.down_ref, ...), custom_call_target="tpu_custom_call", output_to_operand_aliasing={{}: (7, {})} | custom-call | flops 1000000 | bytes 1000000 | tf_op jit(solution)/shard_map/product_first/pallas_call | solution.py:346
  94.8 3.6 %collective-permute-start.17 = (bf16[512,1024]{1,0:T(8,128)(2,1)S(1)}, bf16[512,1024]{1,0:T(8,128)(2,1)S(1)}, u32[]{:S(2)}, u32[]{:S(2)}) collective-permute-start(bf16[512,1024]{1,0:T(8,128)(2,1)S(1)} %collective-permute-done.15.refs_3_), channel_id=1, source_target_pairs={{0,1},{1,0},{2,3},{3,2},{4,5},{5,4},{6,7},{7,6},{8,9},{9,8},{10,11... | collective-permute-start | bytes 3145736 | tf_op jit(solution)/shard_map/ppermute | solution.py:378
  98.4 4.9 %product_second.1.refs_2_ = bf16[512,8192]{1,0:T(8,128)(2,1)} custom-call(s32[16]{0:T(128)S(1)} %stack.111.starts_ref, bf16[512,1024]{1,0:T(8,128)(2,1)S(1)} %get-tuple-element.82.message_ref, bf16[512,64]{1,0:T(8,128)(2,1)S(1)} %get-tuple-element.83.low_ref, bf16[512,1024]{1,0:T(8,128)(2,1)S(1)} %get-tuple-element.84.down_ref, ...), custom_call_target="tpu_custom_call", output_to_operand_aliasing={{}: (9, {})} | custom-call | flops 1000000 | bytes 1000000 | tf_op jit(solution)/shard_map/product_second/pallas_call | solution.py:346
  103.4 2.9 %product_end.1 = bf16[512,8192]{1,0:T(8,128)(2,1)} custom-call(s32[16]{0:T(128)S(1)} %stack.111.starts_ref, bf16[512,1024]{1,0:T(8,128)(2,1)S(1)} %get-tuple-element.82.message_ref, bf16[512,64]{1,0:T(8,128)(2,1)S(1)} %get-tuple-element.83.low_ref, bf16[512,1024]{1,0:T(8,128)(2,1)S(1)} %get-tuple-element.84.down_ref, ...), custom_call_target="tpu_custom_call", output_to_operand_aliasing={{}: (6, {})} | custom-call | flops 1000000 | bytes 1000000 | tf_op jit(solution)/shard_map/product_end/pallas_call | solution.py:346
  (46 shorter events, 4.4 us)
Async XLA Ops:
  1.8 12.4 %collective-permute-start = (bf16[128,1024]{1,0:T(8,128)(2,1)S(1)}, bf16[128,1024]{1,0:T(8,128)(2,1)S(1)}, u32[]{:S(2)}, u32[]{:S(2)}) collective-permute-start(bf16[128,1024]{1,0:T(8,128)(2,1)S(1)} %get-tuple-element.104), channel_id=1, source_target_pairs={{32,0},{64,32},{96,64},{33,1},{65,33},{97,65},{34,2},{66,34},{98,6... | collective-permute-start | bytes 786440 | tf_op jit(solution)/shard_map/ppermute | solution.py:407
  3.1 13.9 %collective-permute-start.1 = (bf16[128,1024]{1,0:T(8,128)(2,1)S(1)}, bf16[128,1024]{1,0:T(8,128)(2,1)S(1)}, u32[]{:S(2)}, u32[]{:S(2)}) collective-permute-start(bf16[128,1024]{1,0:T(8,128)(2,1)S(1)} %get-tuple-element.103), channel_id=1, source_target_pairs={{32,0},{64,32},{96,64},{33,1},{65,33},{97,65},{34,2},{66,34},{98,6... | collective-permute-start | bytes 786440 | tf_op jit(solution)/shard_map/ppermute | solution.py:407
  17.0 7.8 %collective-permute-start.4 = (bf16[128,1024]{1,0:T(8,128)(2,1)S(1)}, bf16[128,1024]{1,0:T(8,128)(2,1)S(1)}, u32[]{:S(2)}, u32[]{:S(2)}) collective-permute-start(bf16[128,1024]{1,0:T(8,128)(2,1)S(1)} %collective-permute-done.1.refs_0_), channel_id=1, source_target_pairs={{0,2},{1,7},{2,0},{3,5},{4,6},{5,3},{6,4},{7,1},{8,10},{9,15},{10,... | collective-permute-start | bytes 786440 | tf_op jit(solution)/shard_map/ppermute | solution.py:378
  21.1 6.4 %collective-permute-start.2 = (bf16[128,1024]{1,0:T(8,128)(2,1)S(1)}, bf16[128,1024]{1,0:T(8,128)(2,1)S(1)}, u32[]{:S(2)}, u32[]{:S(2)}) collective-permute-start(bf16[128,1024]{1,0:T(8,128)(2,1)S(1)} %collective-permute-done.refs_0_), channel_id=1, source_target_pairs={{0,8},{1,25},{2,10},{3,27},{4,12},{5,29},{6,14},{7,31},{8,0},{9,17... | collective-permute-start | bytes 786440 | tf_op jit(solution)/shard_map/ppermute | solution.py:378
  23.5 19.5 %collective-permute-start.6 = (bf16[352,1024]{1,0:T(8,128)(2,1)}, bf16[352,1024]{1,0:T(8,128)(2,1)S(1)}, u32[]{:S(2)}, u32[]{:S(2)}) collective-permute-start(bf16[352,1024]{1,0:T(8,128)(2,1)} %get-tuple-element.65), channel_id=1, source_target_pairs={{32,0},{64,32},{96,64},{33,1},{65,33},{97,65},{34,2},{66,34},{98,6... | collective-permute-start | bytes 2162696 | tf_op jit(solution)/shard_map/ppermute | solution.py:407
  25.5 18.5 %collective-permute-start.5 = (bf16[256,1024]{1,0:T(8,128)(2,1)S(1)}, bf16[256,1024]{1,0:T(8,128)(2,1)S(1)}, u32[]{:S(2)}, u32[]{:S(2)}) collective-permute-start(bf16[256,1024]{1,0:T(8,128)(2,1)S(1)} %join.4.refs_2_), channel_id=1, source_target_pairs={{0,6},{1,3},{2,4},{3,1},{4,2},{5,7},{6,0},{7,5},{8,14},{9,11},{10,... | collective-permute-start | bytes 1572872 | tf_op jit(solution)/shard_map/ppermute | solution.py:378
  28.1 15.8 %collective-permute-start.3 = (bf16[256,1024]{1,0:T(8,128)(2,1)S(1)}, bf16[256,1024]{1,0:T(8,128)(2,1)}, u32[]{:S(2)}, u32[]{:S(2)}) collective-permute-start(bf16[256,1024]{1,0:T(8,128)(2,1)S(1)} %join.3.refs_0_), channel_id=1, source_target_pairs={{0,24},{1,9},{2,26},{3,11},{4,28},{5,13},{6,30},{7,15},{8,16},{9,1... | collective-permute-start | bytes 1572872 | tf_op jit(solution)/shard_map/ppermute | solution.py:378
  28.5 29.2 %all-to-all-start = ((bf16[32,80,256]{2,1,0:T(8,128)(2,1)}), bf16[32,80,256]{2,1,0:T(8,128)(2,1)}, u32[]{:S(2)}, u32[]{:S(2)}) async-start(bf16[32,80,256]{2,1,0:T(8,128)(2,1)} %get-tuple-element.76), calls=%async_computation | async-start | bytes 2621440 | tf_op jit(solution)/shard_map/all_to_all | solution.py:463
  44.0 35.0 %collective-permute-start.7 = (bf16[688,1024]{1,0:T(8,128)(2,1)}, bf16[688,1024]{1,0:T(8,128)(2,1)S(1)}, u32[]{:S(2)}, u32[]{:S(2)}) collective-permute-start(bf16[688,1024]{1,0:T(8,128)(2,1)} %get-tuple-element.68), channel_id=1, source_target_pairs={{32,0},{64,32},{96,64},{33,1},{65,33},{97,65},{34,2},{66,34},{98,6... | collective-permute-start | bytes 4227080 | tf_op jit(solution)/shard_map/ppermute | solution.py:407
  48.7 30.2 %collective-permute-start.10 = (bf16[512,1024]{1,0:T(8,128)(2,1)}, bf16[512,1024]{1,0:T(8,128)(2,1)}, u32[]{:S(2)}, u32[]{:S(2)}) collective-permute-start(bf16[512,1024]{1,0:T(8,128)(2,1)} %get-tuple-element.85.refs_0_), channel_id=1, source_target_pairs={{0,2},{1,7},{2,0},{3,5},{4,6},{5,3},{6,4},{7,1},{8,10},{9,15},{10,... | collective-permute-start | bytes 3145736 | tf_op jit(solution)/shard_map/ppermute | solution.py:378
  48.8 30.1 %collective-permute-start.11 = (bf16[512,1024]{1,0:T(8,128)(2,1)}, bf16[512,1024]{1,0:T(8,128)(2,1)S(1)}, u32[]{:S(2)}, u32[]{:S(2)}) collective-permute-start(bf16[512,1024]{1,0:T(8,128)(2,1)} %get-tuple-element.86.refs_1_), channel_id=1, source_target_pairs={{0,8},{1,25},{2,10},{3,27},{4,12},{5,29},{6,14},{7,31},{8,0},{9,17... | collective-permute-start | bytes 3145736 | tf_op jit(solution)/shard_map/ppermute | solution.py:378
  49.2 29.8 %collective-permute-start.8 = (bf16[512,1024]{1,0:T(8,128)(2,1)}, bf16[512,1024]{1,0:T(8,128)(2,1)S(1)}, u32[]{:S(2)}, u32[]{:S(2)}) collective-permute-start(bf16[512,1024]{1,0:T(8,128)(2,1)} %get-tuple-element.85.refs_0_), channel_id=1, source_target_pairs={{0,6},{1,3},{2,4},{3,1},{4,2},{5,7},{6,0},{7,5},{8,14},{9,11},{10,... | collective-permute-start | bytes 3145736 | tf_op jit(solution)/shard_map/ppermute | solution.py:378
  49.2 29.8 %collective-permute-start.9 = (bf16[512,1024]{1,0:T(8,128)(2,1)}, bf16[512,1024]{1,0:T(8,128)(2,1)}, u32[]{:S(2)}, u32[]{:S(2)}) collective-permute-start(bf16[512,1024]{1,0:T(8,128)(2,1)} %get-tuple-element.86.refs_1_), channel_id=1, source_target_pairs={{0,24},{1,9},{2,26},{3,11},{4,28},{5,13},{6,30},{7,15},{8,16},{9,1... | collective-permute-start | bytes 3145736 | tf_op jit(solution)/shard_map/ppermute | solution.py:378
  57.7 21.3 %copy-start.3 = (bf16[352,1024]{1,0:T(8,128)(2,1)S(1)}, bf16[352,1024]{1,0:T(8,128)(2,1)}, u32[]{:S(2)}) copy-start(bf16[352,1024]{1,0:T(8,128)(2,1)} %copy-done.2) | copy-start | bytes 2162692
  79.2 8.9 %collective-permute-start.12 = (bf16[512,1024]{1,0:T(8,128)(2,1)}, bf16[512,1024]{1,0:T(8,128)(2,1)S(1)}, u32[]{:S(2)}, u32[]{:S(2)}) collective-permute-start(bf16[512,1024]{1,0:T(8,128)(2,1)} %get-tuple-element.85.refs_0_), channel_id=1, source_target_pairs={{0,1},{1,0},{2,3},{3,2},{4,5},{5,4},{6,7},{7,6},{8,9},{9,8},{10,11... | collective-permute-start | bytes 3145736 | tf_op jit(solution)/shard_map/ppermute | solution.py:378
  79.7 8.4 %collective-permute-start.13 = (bf16[512,1024]{1,0:T(8,128)(2,1)}, bf16[512,1024]{1,0:T(8,128)(2,1)S(1)}, u32[]{:S(2)}, u32[]{:S(2)}) collective-permute-start(bf16[512,1024]{1,0:T(8,128)(2,1)} %get-tuple-element.86.refs_1_), channel_id=1, source_target_pairs={{0,1},{1,0},{2,3},{3,2},{4,5},{5,4},{6,7},{7,6},{8,9},{9,8},{10,11... | collective-permute-start | bytes 3145736 | tf_op jit(solution)/shard_map/ppermute | solution.py:378
  79.8 8.3 %collective-permute-start.14 = (bf16[512,1024]{1,0:T(8,128)(2,1)}, bf16[512,1024]{1,0:T(8,128)(2,1)S(1)}, u32[]{:S(2)}, u32[]{:S(2)}) collective-permute-start(bf16[512,1024]{1,0:T(8,128)(2,1)} %collective-permute-done.10.refs_2_), channel_id=1, source_target_pairs={{0,1},{1,0},{2,3},{3,2},{4,5},{5,4},{6,7},{7,6},{8,9},{9,8},{10,11... | collective-permute-start | bytes 3145736 | tf_op jit(solution)/shard_map/ppermute | solution.py:378
  80.2 14.5 %collective-permute-start.15 = (bf16[512,1024]{1,0:T(8,128)(2,1)}, bf16[512,1024]{1,0:T(8,128)(2,1)S(1)}, u32[]{:S(2)}, u32[]{:S(2)}) collective-permute-start(bf16[512,1024]{1,0:T(8,128)(2,1)} %collective-permute-done.10.refs_2_), channel_id=1, source_target_pairs={{0,6},{1,3},{2,4},{3,1},{4,2},{5,7},{6,0},{7,5},{8,14},{9,11},{10,... | collective-permute-start | bytes 3145736 | tf_op jit(solution)/shard_map/ppermute | solution.py:378
  80.8 14.0 %collective-permute-start.16 = (bf16[512,1024]{1,0:T(8,128)(2,1)S(1)}, bf16[512,1024]{1,0:T(8,128)(2,1)S(1)}, u32[]{:S(2)}, u32[]{:S(2)}) collective-permute-start(bf16[512,1024]{1,0:T(8,128)(2,1)S(1)} %collective-permute-done.11.refs_3_), channel_id=1, source_target_pairs={{0,24},{1,9},{2,26},{3,11},{4,28},{5,13},{6,30},{7,15},{8,16},{9,1... | collective-permute-start | bytes 3145736 | tf_op jit(solution)/shard_map/ppermute | solution.py:378
  88.2 10.2 %collective-permute-start.19 = (bf16[512,1024]{1,0:T(8,128)(2,1)S(1)}, bf16[512,1024]{1,0:T(8,128)(2,1)S(1)}, u32[]{:S(2)}, u32[]{:S(2)}) collective-permute-start(bf16[512,1024]{1,0:T(8,128)(2,1)S(1)} %collective-permute-done.11.refs_3_), channel_id=1, source_target_pairs={{0,1},{1,0},{2,3},{3,2},{4,5},{5,4},{6,7},{7,6},{8,9},{9,8},{10,11... | collective-permute-start | bytes 3145736 | tf_op jit(solution)/shard_map/ppermute | solution.py:378
  90.7 7.7 %collective-permute-start.20 = (bf16[512,1024]{1,0:T(8,128)(2,1)S(1)}, bf16[512,1024]{1,0:T(8,128)(2,1)S(1)}, u32[]{:S(2)}, u32[]{:S(2)}) collective-permute-start(bf16[512,1024]{1,0:T(8,128)(2,1)S(1)} %collective-permute-done.8.refs_4_), channel_id=1, source_target_pairs={{0,1},{1,0},{2,3},{3,2},{4,5},{5,4},{6,7},{7,6},{8,9},{9,8},{10,11... | collective-permute-start | bytes 3145736 | tf_op jit(solution)/shard_map/ppermute | solution.py:378
  90.8 7.7 %collective-permute-start.21 = (bf16[512,1024]{1,0:T(8,128)(2,1)}, bf16[512,1024]{1,0:T(8,128)(2,1)S(1)}, u32[]{:S(2)}, u32[]{:S(2)}) collective-permute-start(bf16[512,1024]{1,0:T(8,128)(2,1)} %collective-permute-done.9.refs_5_), channel_id=1, source_target_pairs={{0,1},{1,0},{2,3},{3,2},{4,5},{5,4},{6,7},{7,6},{8,9},{9,8},{10,11... | collective-permute-start | bytes 3145736 | tf_op jit(solution)/shard_map/ppermute | solution.py:378
  94.8 8.6 %collective-permute-start.17 = (bf16[512,1024]{1,0:T(8,128)(2,1)S(1)}, bf16[512,1024]{1,0:T(8,128)(2,1)S(1)}, u32[]{:S(2)}, u32[]{:S(2)}) collective-permute-start(bf16[512,1024]{1,0:T(8,128)(2,1)S(1)} %collective-permute-done.15.refs_3_), channel_id=1, source_target_pairs={{0,1},{1,0},{2,3},{3,2},{4,5},{5,4},{6,7},{7,6},{8,9},{9,8},{10,11... | collective-permute-start | bytes 3145736 | tf_op jit(solution)/shard_map/ppermute | solution.py:378
  98.4 5.0 %collective-permute-start.18 = (bf16[512,1024]{1,0:T(8,128)(2,1)S(1)}, bf16[512,1024]{1,0:T(8,128)(2,1)S(1)}, u32[]{:S(2)}, u32[]{:S(2)}) collective-permute-start(bf16[512,1024]{1,0:T(8,128)(2,1)S(1)} %collective-permute-done.16.refs_4_), channel_id=1, source_target_pairs={{0,1},{1,0},{2,3},{3,2},{4,5},{5,4},{6,7},{7,6},{8,9},{9,8},{10,11... | collective-permute-start | bytes 3145736 | tf_op jit(solution)/shard_map/ppermute | solution.py:378
  (4 other events, 39.1 us)
